TPU v7x, 512 devices: a whole 4x8x8 slice. The times are simulated.
512 devices in a mesh: slab: 64 (over y, x, core), panel: 8 (over z).
Axes of the slice: x: 4, y: 8, z: 8, core: 2. Of those that a mesh axis runs over, the one named last changes fastest.
Arguments:
- vectors: float32 [65536, 1024], P('slab', 'panel'), may hold values from -6 to 6
- hop_table: bfloat16 [8, 256, 256], replicated, may hold values from -0.375 to 0.375
- block_kind: int32 [256, 2], P('slab'), may hold values from 0 to 8
- block_phase: int32 [256], P('slab'), may hold values from 0 to 15
- phase_angles: float32 [16, 256], replicated, may hold values from -3.140625 to 3.140625
- centre: float32 [1], replicated, may hold values from -1 to 1
- half_width: float32 [1], replicated, may hold values from 1.5 to 3
Outputs:
- filtered: float32 [65536, 1024], P('slab', 'panel')
Inputs may be any that keep to these rules, and one draw needn't show every extreme that they name: `block_kind`: the value 8 marks a missing block.
All inputs are finite; a program needn't handle non-finite values.
Results may differ from a plain program's by a relative error of at most 0.0059.
Values may be sent and summed in bfloat16 or wider, within the bound.
No kernel may reach another device: no remote copies, remote signals or barrier semaphores. Data moves between devices by JAX's collectives and lax.ppermute only.
A program may use at most 64 MiB of HBM per device.

v0:
```python
import jax
import jax.numpy as jnp
from jax import lax
from jax.sharding import PartitionSpec as P

GS_STEPS = 2


HIGHEST = lax.Precision.HIGHEST


def passed_along(value, axis, steps):
    count = lax.axis_size(axis)
    initial, last = (max(0, -steps), min(count, count - steps))
    return lax.ppermute(value, axis, [(source, source + steps) for source in range(initial, last)])


def with_halo(cells, sides, width):
    for axis, dim in sides:
        count = lax.axis_size(axis)
        ends = count - 1
        head = lax.slice_in_dim(cells, 0, width, axis=dim)
        tail = lax.slice_in_dim(cells, cells.shape[dim] - width, cells.shape[dim], axis=dim)
        cells = jnp.concatenate(
            [
                lax.ppermute(tail, axis, [(i, (i + 1) % count) for i in range(ends)]),
                cells,
                lax.ppermute(head, axis, [((i + 1) % count, i) for i in range(ends)]),
            ],
            axis=dim,
        )
    return cells


def spread(value, axis, source):
    kept = jnp.where(lax.axis_index(axis) == source, value, 0).astype(value.dtype)
    return lax.psum(kept, axis)


def complex_inner(left_side, right_side):
    product = jnp.einsum("sa,sb->ab", left_side, right_side, precision=HIGHEST)
    split_at = left_side.shape[1] // 2
    real_part = product[:split_at, :split_at] + product[split_at:, split_at:]
    imag_part = product[:split_at, split_at:] - product[split_at:, :split_at]
    return (real_part, imag_part)


def times_embedded(field_data, real_part, imag_part):
    upper_half = jnp.concatenate([real_part, imag_part], axis=1)
    lower_half = jnp.concatenate([-imag_part, real_part], axis=1)
    return jnp.dot(field_data, jnp.concatenate([upper_half, lower_half], axis=0), precision=HIGHEST)


def cholesky_inverse(gram_real, gram_imag):
    order_size = gram_real.shape[0]
    embedded = jnp.stack(
        [jnp.stack([gram_real, -gram_imag], -1), jnp.stack([gram_imag, gram_real], -1)], 1
    )
    embedded = embedded.reshape(2 * order_size, 2 * order_size)
    factor = jnp.linalg.cholesky(embedded)
    identity = jnp.eye(2 * order_size, dtype=jnp.float32)
    inverse = jax.scipy.linalg.solve_triangular(factor, identity, lower=True)
    pieces = inverse.reshape(order_size, 2, order_size, 2)
    return (pieces[:, 0, :, 0], pieces[:, 1, :, 0])


def body(vectors, hop_table, block_kind, block_phase, phase_angles, centre, half_width):
    site_rows = vectors.shape[0]
    width_all = vectors.shape[1]
    panel_width = width_all // 2
    block_rows = hop_table.shape[1]
    block_count = block_kind.shape[0]
    pattern_count = phase_angles.shape[0]
    table_wide = hop_table.astype(jnp.float32)
    sym_table = ((table_wide + jnp.transpose(table_wide, (0, 2, 1))) * 0.5).astype(jnp.bfloat16)
    empty_block = jnp.zeros((1, block_rows, block_rows), jnp.bfloat16)
    sym_lookup = jnp.concatenate([sym_table, empty_block], axis=0)
    hop_lookup = jnp.concatenate([hop_table, empty_block], axis=0)
    own_blocks = sym_lookup[block_kind[:, 0]]
    next_blocks = hop_lookup[block_kind[:, 1]].astype(jnp.float32)
    pattern_ids = jnp.arange(pattern_count)
    selector = (block_phase[:, None] == pattern_ids[None, :]).astype(jnp.float32)
    angles = jnp.dot(selector, phase_angles, precision=HIGHEST)
    fwd_real = (jnp.cos(angles)[:, :, None] * next_blocks).astype(jnp.bfloat16)
    fwd_imag = (jnp.sin(angles)[:, :, None] * next_blocks).astype(jnp.bfloat16)
    edge_real, edge_imag = passed_along((fwd_real[-1], fwd_imag[-1]), "slab", 1)
    back_real = jnp.concatenate([edge_real[None], fwd_real[:-1]], axis=0)
    back_imag = jnp.concatenate([edge_imag[None], fwd_imag[:-1]], axis=0)

    def hop_apply(source_field):
        rounded = source_field.astype(jnp.bfloat16)
        extended = with_halo(rounded, (("slab", 0),), block_rows)
        extended = extended.reshape(block_count + 2, block_rows, width_all)
        ahead = extended[2:]
        behind = extended[:block_count]
        own_part = jnp.einsum(
            "rij,rjc->ric",
            own_blocks,
            extended[1 : block_count + 1],
            preferred_element_type=jnp.float32,
        )
        ahead_a = jnp.einsum("rij,rjc->ric", fwd_real, ahead, preferred_element_type=jnp.float32)
        ahead_b = jnp.einsum("rij,rjc->ric", fwd_imag, ahead, preferred_element_type=jnp.float32)
        behind_a = jnp.einsum("rji,rjc->ric", back_real, behind, preferred_element_type=jnp.float32)
        behind_b = jnp.einsum("rji,rjc->ric", back_imag, behind, preferred_element_type=jnp.float32)
        real_out = (
            ahead_a[:, :, :panel_width]
            - ahead_b[:, :, panel_width:]
            + behind_a[:, :, :panel_width]
            + behind_b[:, :, panel_width:]
        )
        imag_out = (
            ahead_a[:, :, panel_width:]
            + ahead_b[:, :, :panel_width]
            + behind_a[:, :, panel_width:]
            - behind_b[:, :, :panel_width]
        )
        summed = own_part + jnp.concatenate([real_out, imag_out], axis=2)
        return summed.reshape(site_rows, width_all)

    previous = vectors
    current = (hop_apply(vectors) - centre[0] * vectors) / half_width[0]
    following = 2.0 * (hop_apply(current) - centre[0] * current) / half_width[0] - previous
    previous, current = (current, following)
    panel_data = current
    position = lax.axis_index("panel")
    for section_index in range(GS_STEPS):
        is_root = position == section_index
        is_done = position < section_index
        gram_real, gram_imag = complex_inner(panel_data, panel_data)
        gram_real, gram_imag = lax.psum((gram_real, gram_imag), "slab")
        inv_real, inv_imag = cholesky_inverse(gram_real, gram_imag)
        basis_own = times_embedded(panel_data, inv_real.T, -inv_imag.T)
        basis = spread(basis_own, "panel", section_index)
        coef_real, coef_imag = complex_inner(basis, panel_data)
        coef_real, coef_imag = lax.psum((coef_real, coef_imag), "slab")
        projected = panel_data - times_embedded(basis, coef_real, coef_imag)
        panel_data = jnp.where(is_root, basis, jnp.where(is_done, panel_data, projected))
    return panel_data


def solution(mesh):
    in_specs = (P("slab", "panel"), P(), P("slab", None), P("slab"), P(), P(), P())
    out_specs = P("slab", "panel")
    return jax.shard_map(body, mesh=mesh, in_specs=in_specs, out_specs=out_specs, check_vma=False)
```

profile of v0, /device:TPU:1, one launch (start us, length us, event | category | flops | bytes accessed | tf_op | source)
XLA Modules:
  0.0 1297.2 jit_solution(3326080898684005005)
XLA Ops:
  6.5 1.1 convert_element_type.33
  7.6 0.7 fusion.70
  8.4 8.8 collective-permute-start
  17.1 1.9 collective-permute-start.2
  19.1 0.8 fusion.60
  20.4 1.3 concatenate.69
  21.8 1.4 gather_fusion.1
  23.4 1.4 fusion.6
  25.4 1.9 collective-permute-start.3
  28.0 1.9 collective-permute-start.1
  29.9 1.6 copy.60
  31.6 1.9 fusion.1
  33.5 1.1 concatenate.68
  35.9 2.0 gather_fusion
  37.9 0.9 pad_maximum_fusion.9
  39.8 1.2 fusion.15
  42.8 0.7 copy-done.5
  44.2 3.0 collective-permute-start.4
  47.2 2.5 collective-permute-start.5
  50.1 1.3 collective-permute-done.5
  51.4 1.1 pad_maximum_fusion.7
  52.8 1.3 fusion.14
  56.1 1.0 fusion.76
  57.2 241.6 %all-reduce.5 = (f32[64,64,1]{1,0,2:T(8,128)S(1)}, f32[64,64]{1,0:T(8,128)S(1)}) all-reduce(f32[64,64,1]{1,0,2:T(8,128)S(1)} %get-tuple-element.40, f32[64,64]{1,0:T(8,128)S(1)} %get-tuple-element.39), channel_id=1, replica_groups=mesh['slab'=64,'panel'=8] {'slab'}, use_global_device_ids=true, to_apply=%region_0.0 | all-reduce | flops 8192 | bytes 65536 | tf_op jit(solution)/shard_map/psum | solution.py:131
  298.8 2.7 copy.85
  301.5 4.0 reshape.39
  305.7 11.7 cholesky.44
  318.7 9.8 custom-call.6
  328.8 5.5 reshape.40
  334.3 3.4 slice_reduce_fusion.2
  337.7 1.5 convolution_select_fusion.1
  339.5 87.1 %all-reduce.9.cloned.1.call-done = f32[1024,128]{1,0:T(8,128)} async-done(((f32[1024,128]{1,0:T(8,128)}), f32[1024,128]{1,0:T(8,128)}) %all-reduce.9.cloned.1.call-update) | async-done | bytes 524304 | tf_op jit(solution)/shard_map/psum | solution.py:37
  426.6 2.0 fusion.77
  428.8 245.6 %all-reduce.4 = (f32[64,64]{1,0:T(8,128)S(1)}, f32[64,64]{1,0:T(8,128)S(1)}) all-reduce(f32[64,64]{1,0:T(8,128)S(1)} %get-tuple-element.38, f32[64,64]{1,0:T(8,128)S(1)} %get-tuple-element.37), channel_id=1, replica_groups=mesh['slab'=64,'panel'=8] {'slab'}, use_global_device_ids=true, to_apply=%region_5.8 | all-reduce | flops 8192 | bytes 65536 | tf_op jit(solution)/shard_map/psum | solution.py:136
  674.4 1.8 fusion.5
  676.2 1.0 fusion.78
  677.3 246.1 %all-reduce.3 = (f32[64,64,1]{1,0,2:T(8,128)S(1)}, f32[64,64]{1,0:T(8,128)S(1)}) all-reduce(f32[64,64,1]{1,0,2:T(8,128)S(1)} %get-tuple-element.36, f32[64,64]{1,0:T(8,128)S(1)} %get-tuple-element.35), channel_id=1, replica_groups=mesh['slab'=64,'panel'=8] {'slab'}, use_global_device_ids=true, to_apply=%region_7.10 | all-reduce | flops 8192 | bytes 65536 | tf_op jit(solution)/shard_map/psum | solution.py:131
  923.5 2.7 copy.87
  926.2 4.0 reshape.41
  930.4 11.7 cholesky.55
  943.4 9.8 custom-call.7
  953.5 5.5 reshape.42
  959.0 3.4 slice_reduce_fusion
  962.4 1.5 convolution_select_fusion
  963.9 76.0 %all-reduce.11.cloned.1.call-done = f32[1024,128]{1,0:T(8,128)} async-done(((f32[1024,128]{1,0:T(8,128)}), f32[1024,128]{1,0:T(8,128)}) %all-reduce.11.cloned.1.call-update) | async-done | bytes 524304 | tf_op jit(solution)/shard_map/psum | solution.py:37
  1040.0 2.0 fusion.79
  1042.1 245.6 %all-reduce.2 = (f32[64,64]{1,0:T(8,128)S(1)}, f32[64,64]{1,0:T(8,128)S(1)}) all-reduce(f32[64,64]{1,0:T(8,128)S(1)} %get-tuple-element.34, f32[64,64]{1,0:T(8,128)S(1)} %get-tuple-element.33), channel_id=1, replica_groups=mesh['slab'=64,'panel'=8] {'slab'}, use_global_device_ids=true, to_apply=%region_10.13 | all-reduce | flops 8192 | bytes 65536 | tf_op jit(solution)/shard_map/psum | solution.py:136
  1287.7 2.6 fusion.3
  (69 shorter events, 12.3 us)
Async XLA Ops:
  6.5 16.6 %copy-start = (f32[16,256]{1,0:T(8,128)S(1)}, f32[16,256]{1,0:T(8,128)}, u32[]{:S(2)}) copy-start(f32[16,256]{1,0:T(8,128)} %param.14) | copy-start | bytes 49156
  6.5 16.6 %copy-start.7 = (s32[4]{0:T(128)S(1)}, s32[4]{0:T(128)}, u32[]{:S(2)}) copy-start(s32[4]{0:T(128)} %param.13) | copy-start | bytes 52
  6.5 420.1 %all-reduce.9.cloned.1.call-start = ((), (), s32[]{:S(2)}) async-start(), calls=%async_computation | async-start | bytes 1048576 | tf_op jit(solution)/shard_map/psum | solution.py:37
  7.6 30.3 %copy-start.3 = (bf16[1024,128]{1,0:T(8,128)(2,1)}, bf16[1024,128]{1,0:T(8,128)(2,1)S(1)}, u32[]{:S(2)}) copy-start(bf16[1024,128]{1,0:T(8,128)(2,1)S(1)} %convert_element_type.33) | copy-start | bytes 786436
  8.4 29.5 %collective-permute-start = (bf16[256,128]{1,0:T(8,128)(2,1)}, bf16[256,128]{1,0:T(8,128)(2,1)}, u32[]{:S(2)}, u32[]{:S(2)}) collective-permute-start(bf16[256,128]{1,0:T(8,128)(2,1)} %get-tuple-element.31), channel_id=1, source_target_pairs={{8,0},{16,8},{24,16},{32,24},{40,32},{48,40},{56,48},{64,56},{72,6... | collective-permute-start | bytes 196616 | tf_op jit(solution)/shard_map/ppermute | solution.py:28
  17.1 20.8 %collective-permute-start.2 = (bf16[256,128]{1,0:T(8,128)(2,1)}, bf16[256,128]{1,0:T(8,128)(2,1)}, u32[]{:S(2)}, u32[]{:S(2)}) collective-permute-start(bf16[256,128]{1,0:T(8,128)(2,1)} %get-tuple-element.32), channel_id=1, source_target_pairs={{0,8},{8,16},{16,24},{24,32},{32,40},{40,48},{48,56},{56,64},{64,7... | collective-permute-start | bytes 196616 | tf_op jit(solution)/shard_map/ppermute | solution.py:26
  21.7 8.2 copy-start.1
  25.4 14.0 %collective-permute-start.3 = (bf16[256,256]{1,0:T(8,128)(2,1)}, bf16[256,256]{1,0:T(8,128)(2,1)S(1)}, u32[]{:S(2)}, u32[]{:S(2)}) collective-permute-start(bf16[256,256]{1,0:T(8,128)(2,1)} %slice_bitcast_fusion), channel_id=1, source_target_pairs={{0,8},{8,16},{16,24},{24,32},{32,40},{40,48},{48,56},{56,64},{64,7... | collective-permute-start | bytes 393224 | tf_op jit(solution)/shard_map/ppermute | solution.py:15
  28.0 11.8 collective-permute-start.1
  41.1 1.0 copy-start.4
  41.7 1.1 copy-start.2
  42.8 0.7 copy-start.5
  44.2 5.9 collective-permute-start.4
  47.2 4.2 collective-permute-start.5
  54.7 1.0 copy-start.6
  339.2 700.7 %all-reduce.11.cloned.1.call-start = ((), (), s32[]{:S(2)}) async-start(), calls=%async_computation.1 | async-start | bytes 1048576 | tf_op jit(solution)/shard_map/psum | solution.py:37
Sparse Core Ops, SparseCore 0:
  339.3 87.2 all-reduce.8
  964.0 75.8 all-reduce.10
where the time goes:
time: 1300 us
  blocking collectives  979 us (75%)
  waiting for transfers between devices  165 us (13%)
  other arithmetic  55.3 us (4%)
  local copies, waits for them, and re-layouts  43.4 us (3%)
  starting transfers between devices  20.3 us (2%)
  matrix products  19.2 us (1%)
  between operations  15.2 us (1%)
    psum x2, blocking collectives, body(): coef_real, coef_imag = lax.psum((coef_real, coef_imag), 'slab')  491 us
    psum x2, blocking collectives, body(): gram_real, gram_imag = lax.psum((gram_real, gram_imag), 'slab')  488 us
    psum x2, waiting for transfers between devices, spread(): return lax.psum(kept, axis)  163 us
  transfers between devices with their start and end apart: 8, of which 4 were waited for; matrix products, arithmetic and copies ran while one was open for 1% of the time, Pallas kernels for 0%

commit v1 on v0

v1 whole, which is shorter than its diff:
```python
import jax
import jax.numpy as jnp
import numpy as np
from jax import lax
from jax.experimental import pallas as pl
from jax.experimental.pallas import tpu as pltpu
from jax.sharding import Mesh, PartitionSpec as P

HIGHEST = lax.Precision.HIGHEST
F32 = jnp.float32
BF16 = jnp.bfloat16
BLK = 256
WIDE = 128
HALF = 64
META = 16
VM = pltpu.VMEM
SM = pltpu.SMEM


def lane_sign(first):
    lane = lax.broadcasted_iota(jnp.int32, (1, WIDE), 1)
    return jnp.where(lane < HALF, first, -first).astype(F32)


def times_i(packed):
    return lane_sign(-1.0) * pltpu.roll(packed, HALF, 1)


def dot(a, b, **kw):
    return lax.dot_general(a, b, (((1,), (0,)), ((), ())), preferred_element_type=F32, **kw)


def dot_t(a, b, **kw):
    return lax.dot_general(a, b, (((0,), (0,)), ((), ())), preferred_element_type=F32, **kw)


def split(x):
    hi = x.astype(BF16)
    return hi, (x - hi.astype(F32)).astype(BF16)


def filter_kernel(meta, nums, v, left, right, hop, hop_t, sym, cos_t, sin_t, w, w_hi, cosb, sinb, z, y1, y1b):
    centre, inv_h, has_left, has_right = nums[0], nums[1], nums[2], nums[3]
    pick = lax.broadcasted_iota(jnp.int32, (cos_t.shape[1], WIDE), 0) % 16

    def own_kind(r):
        return meta[3 * (r + 2)]

    def next_kind(r):
        return meta[3 * (r + 2) + 1]

    def flag(kind):
        return jnp.where(kind < 8, 1.0, 0.0).astype(F32)

    for r in range(-2, 5):
        hot = jnp.where(pick == meta[3 * (r + 2) + 2], 1.0, 0.0).astype(BF16)
        cosb[r + 2] = dot(cos_t[...], hot)
        sinb[r + 2] = dot(sin_t[...], hot)

    def v_row(r):
        if r < 0:
            return left[(r + 2) * BLK : (r + 3) * BLK, :]
        if r > 3:
            return right[(r - 4) * BLK : (r - 3) * BLK, :]
        return v[r * BLK : (r + 1) * BLK, :].astype(BF16)

    def y_row(r):
        return y1b[r + 1]

    def back_phase(x, r):
        x = x.astype(F32)
        return (cosb[r + 2] * x - sinb[r + 2] * times_i(x)).astype(BF16)

    def hop_row(r, row):
        ko, kn, kb = own_kind(r), next_kind(r), next_kind(r - 1)
        total = flag(ko) * dot(sym[jnp.minimum(ko, 7)], row(r))
        ahead = flag(kn) * dot(hop[jnp.minimum(kn, 7)], row(r + 1))
        total += cosb[r + 2] * ahead + sinb[r + 2] * times_i(ahead)
        return total + flag(kb) * dot(hop_t[jnp.minimum(kb, 7)], z[r + 1])

    for r in range(-2, 4):
        z[r + 2] = back_phase(v_row(r), r)
    for r in range(-1, 5):
        vr = v[r * BLK : (r + 1) * BLK, :] if 0 <= r < 4 else v_row(r).astype(F32)
        y = (hop_row(r, v_row) - centre * vr) * inv_h
        if r == -1:
            y = y * has_left
        if r == 4:
            y = y * has_right
        if 0 <= r < 4:
            y1[r] = y
        y1b[r + 1] = y.astype(BF16)
    for r in range(-1, 4):
        z[r + 2] = back_phase(y_row(r), r)
    for r in range(4):
        y = (2.0 * inv_h) * (hop_row(r, y_row) - centre * y1[r]) - v[r * BLK : (r + 1) * BLK, :]
        w[r * BLK : (r + 1) * BLK, :] = y
        w_hi[r * BLK : (r + 1) * BLK, :] = y.astype(BF16)


def chebyshev(meta, nums, v, left, right, hop, hop_t, sym, cos_t, sin_t):
    spec = pl.BlockSpec(memory_space=VM)
    smem = pl.BlockSpec(memory_space=SM)
    return pl.pallas_call(
        filter_kernel,
        out_shape=(jax.ShapeDtypeStruct(v.shape, F32), jax.ShapeDtypeStruct(v.shape, BF16)),
        in_specs=[smem, smem] + [spec] * 8,
        out_specs=(spec, spec),
        scratch_shapes=[
            VM((7, BLK, WIDE), F32),
            VM((7, BLK, WIDE), F32),
            VM((6, BLK, WIDE), BF16),
            VM((4, BLK, WIDE), F32),
            VM((6, BLK, WIDE), BF16),
        ],
        compiler_params=pltpu.CompilerParams(vmem_limit_bytes=40 << 20),
        name="chebyshev",
    )(meta, nums, v, left, right, hop, hop_t, sym, cos_t, sin_t)


def gram_kernel(w, pq, out):
    rows = w.shape[0]
    p0 = pq[:, 0].reshape(rows, WIDE)
    p1 = pq[:, 1].reshape(rows, WIDE)
    w_hi, w_lo = split(w[...])
    prod = dot_t(jnp.concatenate([p0, p1], 1), jnp.concatenate([p0, p1, w_hi, w_lo], 1))

    def inner(a, b):
        d = prod[a * WIDE : (a + 1) * WIDE, b * WIDE : (b + 1) * WIDE]
        return d[:HALF] + lane_sign(1.0) * pltpu.roll(d[HALF:], HALF, 1)

    out[0:HALF, :] = inner(0, 0)
    out[HALF : 2 * HALF, :] = inner(0, 1)
    out[2 * HALF : 3 * HALF, :] = inner(1, 1)
    out[3 * HALF : 4 * HALF, :] = inner(0, 2) + inner(0, 3)
    out[4 * HALF : 5 * HALF, :] = inner(1, 2) + inner(1, 3)


def gram(w, pq):
    spec = pl.BlockSpec(memory_space=VM)
    return pl.pallas_call(
        gram_kernel,
        out_shape=jax.ShapeDtypeStruct((5 * HALF, WIDE), F32),
        in_specs=[spec, spec],
        out_specs=spec,
        compiler_params=pltpu.CompilerParams(vmem_limit_bytes=32 << 20),
        name="gram",
    )(w, pq)


def inverse_factor(tr, ti):
    tiles = WIDE // 8
    re = [tr[8 * t : 8 * t + 8] for t in range(tiles)]
    im = [ti[8 * t : 8 * t + 8] for t in range(tiles)]
    lane = lax.broadcasted_iota(jnp.int32, (8, WIDE), 1)
    sub = lax.broadcasted_iota(jnp.int32, (8, WIDE), 0)
    for k in range(WIDE):
        g, j = divmod(k, 8)
        at_k = lane == k
        row_r = re[g][j : j + 1]
        row_i = im[g][j : j + 1]
        inv = 1.0 / jnp.broadcast_to(row_r[:, k : k + 1], (1, WIDE))
        row_r = jnp.where(at_k[:1], 1.0, row_r) * inv
        row_i = jnp.where(at_k[:1], 0.0, row_i) * inv
        row_r = jnp.broadcast_to(row_r, (8, WIDE))
        row_i = jnp.broadcast_to(row_i, (8, WIDE))
        for t in range(g, tiles):
            if t == g and j == 7:
                continue
            cr = jnp.broadcast_to(re[t][:, k : k + 1], (8, WIDE))
            ci = jnp.broadcast_to(im[t][:, k : k + 1], (8, WIDE))
            keep_r = jnp.where(at_k, 0.0, re[t])
            keep_i = jnp.where(at_k, 0.0, im[t])
            new_r = keep_r - (cr * row_r - ci * row_i)
            new_i = keep_i - (cr * row_i + ci * row_r)
            if t == g:
                new_r = jnp.where(sub > j, new_r, re[t])
                new_i = jnp.where(sub > j, new_i, im[t])
            re[t], im[t] = new_r, new_i
    out_r, out_i = [], []
    for t in range(tiles):
        diag = lane == sub + 8 * t
        below = lane < sub + 8 * t
        pivot = jnp.sum(jnp.where(diag, re[t], 0.0), axis=1, keepdims=True)
        scale = lax.rsqrt(pivot)
        out_r.append(jnp.where(diag, 1.0, jnp.where(below, re[t], 0.0)) * scale)
        out_i.append(jnp.where(below, im[t], 0.0) * scale)
    return jnp.concatenate(out_r, 0), jnp.concatenate(out_i, 0)


def embed(block):
    return jnp.concatenate([block, times_i(block)], 0)


def finish_kernel(pos, g, w, pq, out):
    rows = w.shape[0]
    lane = lax.broadcasted_iota(jnp.int32, (HALF, WIDE), 1)
    left = lane < HALF
    g00, g01, g11 = g[0:HALF, :], g[HALF : 2 * HALF, :], g[2 * HALF : 3 * HALF, :]
    zero = jnp.zeros((HALF, WIDE), F32)

    up_r = jnp.concatenate(
        [jnp.where(left, g00, pltpu.roll(g01, HALF, 1)), jnp.where(left, 0.0, pltpu.roll(g11, HALF, 1))], 0
    )
    up_i = jnp.concatenate([jnp.where(left, pltpu.roll(g00, HALF, 1), g01), jnp.where(left, 0.0, g11)], 0)
    low = jnp.concatenate([zero, jnp.where(left, 1.0, 0.0)], 0)
    tr = up_r + low * jnp.transpose(up_r)
    ti = up_i - low * jnp.transpose(up_i)
    rr, ri = inverse_factor(tr, ti)
    which = pos[0]

    @pl.when(which >= 2)
    def _():
        m = g[3 * HALF : 5 * HALF, :]
        n = dot(rr, m, precision=HIGHEST) + dot(ri, times_i(m), precision=HIGHEST)
        k = dot_t(rr, n, precision=HIGHEST) - dot_t(ri, times_i(n), precision=HIGHEST)
        e_hi, e_lo = split(jnp.concatenate([embed(k[:HALF]), embed(k[HALF:])], 0))
        p01 = jnp.concatenate([pq[:, 0].reshape(rows, WIDE), pq[:, 1].reshape(rows, WIDE)], 1)
        out[...] = w[...] - (dot(p01, e_hi) + dot(p01, e_lo))

    @pl.when(which < 2)
    def _():
        rt, it = jnp.transpose(rr), jnp.transpose(ri)
        full = lax.broadcasted_iota(jnp.int32, (WIDE, WIDE), 1) < HALF
        first = jnp.where(full, rt, -pltpu.roll(it, HALF, 1))
        second = jnp.where(full, pltpu.roll(rt, HALF, 1), -it)
        is_first = which == 0
        own = jnp.where(is_first, first[:HALF], second[HALF:])
        other = jnp.where(is_first, 0.0, second[:HALF])
        o_hi, o_lo = split(embed(other))
        p0 = pq[:, 0].reshape(rows, WIDE)
        out[...] = dot(w[...], embed(own), precision=HIGHEST) + dot(p0, o_hi) + dot(p0, o_lo)


def finish(pos, g, w, pq):
    spec = pl.BlockSpec(memory_space=VM)
    return pl.pallas_call(
        finish_kernel,
        out_shape=jax.ShapeDtypeStruct(w.shape, F32),
        in_specs=[pl.BlockSpec(memory_space=SM), spec, spec, spec],
        out_specs=spec,
        compiler_params=pltpu.CompilerParams(vmem_limit_bytes=40 << 20),
        name="finish",
    )(pos, g, w, pq)


def swap(x, axes):
    return lax.all_to_all(x, axes, 0, 0, tiled=True)


def copies(x, count):
    return jnp.broadcast_to(x[None], (count,) + x.shape).reshape((count * x.shape[0],) + x.shape[1:])


def sum_pieces(x, count):
    return jnp.sum(x.reshape((count, -1) + x.shape[1:]), axis=0)


def slab_sum(x, inner, outer):
    near, far = lax.axis_size(inner), lax.axis_size(outer)
    piece = sum_pieces(swap(x, inner), near)
    piece = sum_pieces(swap(copies(piece, far), outer), far)
    return swap(copies(piece, near), inner)


def thirds(x):
    a = lax.reduce_precision(x, 8, 7)
    b = lax.reduce_precision(x - a, 8, 7)
    return jnp.concatenate([a, b, x - a - b], axis=0).astype(BF16).T


def body(vectors, hop_table, block_kind, block_phase, phase_angles, centre, half_width):
    slab = ("y", "x", "core")
    count = lax.axis_size(slab)
    me = lax.axis_index(slab)
    rows = vectors.shape[0]
    table = jnp.concatenate([block_kind - 8, block_phase[:, None]], axis=1)

    def packet(part, info):
        extra = jnp.zeros((META, WIDE), F32).at[:2, :3].set(info.astype(F32))
        return jnp.concatenate([part.astype(BF16), extra.astype(BF16)], axis=0)

    up = packet(vectors[rows // 2 :], table[2:])
    down = packet(vectors[: rows // 2], table[:2])
    left = lax.ppermute(up, slab, [(i, i + 1) for i in range(count - 1)])
    right = lax.ppermute(down, slab, [(i + 1, i) for i in range(count - 1)])
    wide = hop_table.astype(F32)
    turned = jnp.transpose(hop_table, (0, 2, 1))
    sym = ((wide + turned.astype(F32)) * 0.5).astype(BF16)
    cos_t = thirds(jnp.cos(phase_angles))
    sin_t = thirds(jnp.sin(phase_angles))

    def info(packed):
        return packed[rows // 2 : rows // 2 + 2, :3].astype(jnp.int32)

    meta = jnp.concatenate([info(left), table, info(right)], axis=0) + jnp.array([8, 8, 0], jnp.int32)
    nums = jnp.stack(
        [centre[0], 1.0 / half_width[0], (me > 0).astype(F32), (me < count - 1).astype(F32)]
    )
    w, w_hi = chebyshev(meta.reshape(-1), nums, vectors, left, right, hop_table, turned, sym, cos_t, sin_t)

    panels = lax.axis_size("panel")
    chunk = rows // panels
    mine = swap(w_hi, "panel")[: 2 * chunk]
    pq = swap(copies(mine, panels), "panel").reshape(panels, 2, chunk, WIDE)
    g = slab_sum(gram(w, pq), ("x", "core"), "y")
    pos = lax.axis_index("panel").astype(jnp.int32).reshape(1)
    return finish(pos, g, w, pq)


def solution(mesh):
    panels = mesh.shape["panel"]
    devices = np.asarray(mesh.devices).reshape(8, 4, 2, panels)
    fine = Mesh(devices, ("y", "x", "core", "panel"))
    slab = ("y", "x", "core")
    in_specs = (P(slab, "panel"), P(), P(slab, None), P(slab), P(), P(), P())
    return jax.shard_map(body, mesh=fine, in_specs=in_specs, out_specs=P(slab, "panel"), check_vma=False)
```

time: 1300 us -> 115 us (0.09)
  blocking collectives: 979 us -> 63.3 us
  waiting for transfers between devices: 165 us -> 5.61 us
  other arithmetic: 55.3 us -> 4.92 us
  local copies, waits for them, and re-layouts: 43.4 us -> 6.28 us
  matrix products: 19.2 us -> 0 us
  Pallas kernels: 0 us -> 15.8 us
  between operations: 15.2 us -> 1.5 us
    psum x4 -> x0, blocking collectives: 979 us -> none  [the longest x2 491 us: body(): coef_real, coef_imag = lax.psum((coef_real, coef_imag), 'slab')]
    psum x2 -> x0, waiting for transfers between devices: 163 us -> none  [spread(): return lax.psum(kept, axis)]
    all_to_all x0 -> x4, blocking collectives: none -> 63.3 us  [swap(): return lax.all_to_all(x, axes, 0, 0, tiled=True)]
    another operation x16 -> x4, other arithmetic: 45.8 us -> 1.17 us  [the longest x6 24.8 us: cholesky_inverse(): factor = jnp.linalg.cholesky(embedded)]
    reshape x6 -> x0, local copies, waits for them, and re-layouts: 19.2 us -> none  [the longest x2 11 us: cholesky_inverse(): pieces = inverse.reshape(order_size, 2, order_size, 2)]
    dot_general x19 -> x0, matrix products: 18.6 us -> none  [the longest x4 7.39 us: times_embedded(): jnp.dot(field_data, jnp.concatenate([upper_half, lower_half], axis=0), pr...]
    pallas_call x0 -> x3, Pallas kernels: none -> 15.8 us  [the longest x1 12.9 us: finish(): pl.pallas_call(finish_kernel, out_shape=jax.ShapeDtypeStruct(w.shape, F32...]
  transfers between devices with their start and end apart: 8 -> 3, of which waited for: 4 -> 1; matrix products, arithmetic and copies ran while one was open for 1% -> 3% of each run, Pallas kernels for 0% -> 0%
where the time goes in v1:
time: 115 us; the launch traced here: 114 us
  blocking collectives  63.3 us (55%)
  starting transfers between devices  16.6 us (14%)
  Pallas kernels  15.8 us (14%)
  local copies, waits for them, and re-layouts  6.28 us (5%)
  waiting for transfers between devices  5.61 us (5%)
  other arithmetic  4.92 us (4%)
  between operations  1.5 us (1%)
    all_to_all x4, blocking collectives, swap(): return lax.all_to_all(x, axes, 0, 0, tiled=True)  63.3 us
    pallas_call x1, Pallas kernels, finish(): pl.pallas_call(finish_kernel, out_shape=jax.ShapeDtypeStruct(w.shape, F32...  12.9 us
    ppermute x1, starting transfers between devices, body(): right = lax.ppermute(down, slab, [(i + 1, i) for i in range(count - 1)])  8.77 us
    all_to_all x1, starting transfers between devices, swap(): return lax.all_to_all(x, axes, 0, 0, tiled=True)  5.94 us
    all_to_all x1, waiting for transfers between devices, swap(): return lax.all_to_all(x, axes, 0, 0, tiled=True)  5.6 us
    unnamed x14, local copies, waits for them, and re-layouts  2.87 us
    pallas_call x1, Pallas kernels, chebyshev(): pl.pallas_call(filter_kernel, out_shape=(jax.ShapeDtypeStruct(v.shape, F3...  2.36 us
  transfers between devices with their start and end apart: 3, of which 1 were waited for; matrix products, arithmetic and copies ran while one was open for 3% of the time, Pallas kernels for 0%

profile of v1, /device:TPU:1, one launch (start us, length us, event | category | flops | bytes accessed | tf_op | source)
XLA Modules:
  0.0 114.0 jit_solution(7431069041911101433)
XLA Ops:
  0.0 0.0 copy-start.5
  0.0 0.0 copy-start
  0.0 0.8 copy.25
  0.8 0.8 copy.24
  1.6 0.0 copy-start.4
  1.6 0.1 pad_add_fusion
  1.7 0.5 copy-done.4
  2.2 1.1 convert.32
  3.3 0.7 fusion.3
  4.0 8.8 %collective-permute-start.1 = (bf16[528,128]{1,0:T(8,128)(2,1)}, bf16[528,128]{1,0:T(8,128)(2,1)S(1)}, u32[]{:S(2)}, u32[]{:S(2)}) collective-permute-start(bf16[528,128]{1,0:T(8,128)(2,1)} %fusion.3), channel_id=1, source_target_pairs={{8,0},{16,8},{24,16},{32,24},{40,32},{48,40},{56,48},{64,56},{72,6... | collective-permute-start | bytes 405512 | tf_op jit(solution)/shard_map/ppermute | solution.py:286
  12.8 0.7 fusion.2
  13.4 1.9 %collective-permute-start = (bf16[528,128]{1,0:T(8,128)(2,1)}, bf16[528,128]{1,0:T(8,128)(2,1)S(1)}, u32[]{:S(2)}, u32[]{:S(2)}) collective-permute-start(bf16[528,128]{1,0:T(8,128)(2,1)} %fusion.2), channel_id=1, source_target_pairs={{0,8},{8,16},{16,24},{24,32},{32,40},{40,48},{48,56},{56,64},{64,7... | collective-permute-start | bytes 405512 | tf_op jit(solution)/shard_map/ppermute | solution.py:285
  15.3 0.0 copy-done.5
  15.3 0.1 fusion.7
  15.4 0.0 copy-done
  15.4 0.5 copy.26
  16.0 0.3 multiply_convert_fusion.sym
  16.3 0.6 pad_maximum_fusion.1
  18.2 0.1 copy.27
  18.4 0.9 copy.28
  19.3 0.1 pad_maximum_fusion.2.nums
  19.3 0.0 collective-permute-done.1.right
  19.4 0.0 collective-permute-done.left
  19.4 1.4 %add_add_fusion = s32[8,3]{1,0:T(8,128)} fusion(s32[2,3]{1,0:T(2,128)S(1)} %slice_convert_fusion, s32[4,1]{1,0:T(4,128)S(1)} %copy.25, s32[4,2]{1,0:T(4,128)} %copy-done.4, s32[2,3]{1,0:T(2,128)S(1)} %slice_convert_fusion.1, s32[3]{0:T(128)} %constant.84.clone), kind=kLoop, calls=%fused_computation.18 | loop fusion | flops 96 | bytes 204 | tf_op jit(solution)/shard_map/add | solution.py:296
  20.7 0.8 add.32.meta
  21.5 0.0 copy-start.1
  21.5 1.0 copy-done.1
  22.5 2.4 %chebyshev.1 = (f32[1024,128]{1,0:T(8,128)S(1)}, bf16[1024,128]{1,0:T(8,128)(2,1)S(1)}) custom-call(s32[24]{0:T(128)S(1)} %add.32.meta, f32[4]{0:T(128)S(1)} %pad_maximum_fusion.2.nums, f32[1024,128]{1,0:T(8,128)S(1)} %copy-done.1, bf16[528,128]{1,0:T(8,128)(2,1)S(1)} %collective-permute-done.left, bf16[528,128]{1,0:T(8,128)(2,1)S(1)} %collective-permute-done.1.right, ...), custom_call_target="tpu_custom_call" | custom-call | tf_op jit(solution)/shard_map/chebyshev/pallas_call | solution.py:104
  24.9 0.0 copy-start.2
  24.9 18.0 %all_to_all.38 = bf16[8,128,128]{2,1,0:T(8,128)(2,1)S(1)} all-to-all(bf16[8,128,128]{2,1,0:T(8,128)(2,1)S(1)} %bitcast.20), channel_id=1, replica_groups=mesh['y'=8,'x'=4,'core'=2,'panel'=8] {'panel'}, dimensions={0} | all-to-all | bytes 524288 | tf_op jit(solution)/shard_map/all_to_all | solution.py:248
  42.9 0.1 broadcast_in_dim.12
  43.0 20.3 %all_to_all.39 = bf16[8,256,128]{2,1,0:T(8,128)(2,1)S(1)} all-to-all(bf16[8,256,128]{2,1,0:T(8,128)(2,1)S(1)} %broadcast_in_dim.12), channel_id=1, replica_groups=mesh['y'=8,'x'=4,'core'=2,'panel'=8] {'panel'}, dimensions={0} | all-to-all | bytes 1048576 | tf_op jit(solution)/shard_map/all_to_all | solution.py:248
  63.3 0.0 copy-done.2
  63.3 0.5 gram.1
  63.9 0.0 copy-start.3
  63.9 10.3 %all_to_all.40 = f32[8,40,128]{2,1,0:T(8,128)S(1)} all-to-all(f32[8,40,128]{2,1,0:T(8,128)S(1)} %bitcast.17), channel_id=1, replica_groups=mesh['y'=8,'x'=4,'core'=2,'panel'=8] {'x','core'}, dimensions={0} | all-to-all | bytes 327680 | tf_op jit(solution)/shard_map/all_to_all | solution.py:248
  74.2 14.7 %all_to_all.41 = f32[8,40,128]{2,1,0:T(8,128)S(1)} all-to-all(f32[8,40,128]{2,1,0:T(8,128)S(1)} %broadcast_in_dim.13), channel_id=1, replica_groups=mesh['y'=8,'x'=4,'core'=2,'panel'=8] {'y'}, dimensions={0} | all-to-all | bytes 327680 | tf_op jit(solution)/shard_map/all_to_all | solution.py:248
  88.9 0.7 broadcast_in_dim.28
  89.6 5.9 %all-to-all-start.4 = ((f32[8,40,128]{2,1,0:T(8,128)}), f32[8,40,128]{2,1,0:T(8,128)S(1)}, u32[]{:S(2)}, u32[]{:S(2)}) async-start(f32[8,40,128]{2,1,0:T(8,128)} %broadcast_in_dim.28), calls=%async_computation.4 | async-start | bytes 327680 | tf_op jit(solution)/shard_map/all_to_all | solution.py:248
  95.5 5.6 %all-to-all-done.4 = f32[8,40,128]{2,1,0:T(8,128)S(1)} async-done(((f32[8,40,128]{2,1,0:T(8,128)}), f32[8,40,128]{2,1,0:T(8,128)S(1)}, u32[]{:S(2)}, u32[]{:S(2)}) %all-to-all-start.4) | async-done | bytes 163872 | tf_op jit(solution)/shard_map/all_to_all | solution.py:248
  101.1 0.0 copy-done.3
  101.1 12.9 %finish.1 = f32[1024,128]{1,0:T(8,128)} custom-call(s32[1]{0:T(128)} %bitcast.pos, f32[320,128]{1,0:T(8,128)S(1)} %bitcast.16, f32[1024,128]{1,0:T(8,128)S(1)} %copy-done.3, bf16[8,2,128,128]{3,2,1,0:T(8,128)(2,1)S(1)} %bitcast.15), custom_call_target="tpu_custom_call" | custom-call | tf_op jit(solution)/shard_map/finish/pallas_call | solution.py:237
  (11 shorter events, 0.1 us)
Async XLA Ops:
  0.0 15.3 %copy-start.5 = (f32[16,256]{1,0:T(8,128)S(1)}, f32[16,256]{1,0:T(8,128)}, u32[]{:S(2)}) copy-start(f32[16,256]{1,0:T(8,128)} %param.16) | copy-start | bytes 49156
  0.0 15.4 %copy-start = (bf16[8,256,256]{2,1,0:T(8,128)(2,1)S(1)}, bf16[8,256,256]{2,1,0:T(8,128)(2,1)}, u32[]{:S(2)}) copy-start(bf16[8,256,256]{2,1,0:T(8,128)(2,1)} %hop.1) | copy-start | bytes 3145732
  1.6 0.6 copy-start.4
  4.0 15.4 %collective-permute-start.1 = (bf16[528,128]{1,0:T(8,128)(2,1)}, bf16[528,128]{1,0:T(8,128)(2,1)S(1)}, u32[]{:S(2)}, u32[]{:S(2)}) collective-permute-start(bf16[528,128]{1,0:T(8,128)(2,1)} %fusion.3), channel_id=1, source_target_pairs={{8,0},{16,8},{24,16},{32,24},{40,32},{48,40},{56,48},{64,56},{72,6... | collective-permute-start | bytes 405512 | tf_op jit(solution)/shard_map/ppermute | solution.py:286
  13.4 5.9 %collective-permute-start = (bf16[528,128]{1,0:T(8,128)(2,1)}, bf16[528,128]{1,0:T(8,128)(2,1)S(1)}, u32[]{:S(2)}, u32[]{:S(2)}) collective-permute-start(bf16[528,128]{1,0:T(8,128)(2,1)} %fusion.2), channel_id=1, source_target_pairs={{0,8},{8,16},{16,24},{24,32},{32,40},{40,48},{48,56},{56,64},{64,7... | collective-permute-start | bytes 405512 | tf_op jit(solution)/shard_map/ppermute | solution.py:285
  21.5 1.0 copy-start.1
  24.9 38.4 %copy-start.2 = (f32[1024,128]{1,0:T(8,128)}, f32[1024,128]{1,0:T(8,128)S(1)}, u32[]{:S(2)}) copy-start(f32[1024,128]{1,0:T(8,128)S(1)} %get-tuple-element.31.w) | copy-start | bytes 1572868
  63.9 37.2 %copy-start.3 = (f32[1024,128]{1,0:T(8,128)S(1)}, f32[1024,128]{1,0:T(8,128)}, u32[]{:S(2)}) copy-start(f32[1024,128]{1,0:T(8,128)} %copy-done.2) | copy-start | bytes 1572868
  89.6 11.5 %all-to-all-start.4 = ((f32[8,40,128]{2,1,0:T(8,128)}), f32[8,40,128]{2,1,0:T(8,128)S(1)}, u32[]{:S(2)}, u32[]{:S(2)}) async-start(f32[8,40,128]{2,1,0:T(8,128)} %broadcast_in_dim.28), calls=%async_computation.4 | async-start | bytes 327680 | tf_op jit(solution)/shard_map/all_to_all | solution.py:248

commit v2 on v1

--- a/solution.py
+++ b/solution.py
@@ -1,3 +1,5 @@
+import functools
+
 import jax
 import jax.numpy as jnp
 import numpy as np
@@ -13,6 +15,12 @@
 WIDE = 128
 HALF = 64
 META = 16
+STEPS = (
+    [(0, 1), (4, 5), (1, 2), (5, 6)],
+    [(0, 7), (4, 3), (1, 0), (5, 4)],
+    [(0, 6), (4, 2), (1, 3), (5, 7)],
+)
+HELD = ((0, 1, 3, 2, 0, 1, 3, 2), (2, 0, 1, 3, 2, 0, 1, 3))
 VM = pltpu.VMEM
 SM = pltpu.SMEM
 
@@ -118,34 +126,49 @@
     )(meta, nums, v, left, right, hop, hop_t, sym, cos_t, sin_t)
 
 
-def gram_kernel(w, pq, out):
-    rows = w.shape[0]
-    p0 = pq[:, 0].reshape(rows, WIDE)
-    p1 = pq[:, 1].reshape(rows, WIDE)
+def gram_kernel(pos, w, own, first, second, third, p01, out):
+    which = pos[0]
+    for src, ref in enumerate((own, first, second, third)):
+        for panel in range(2):
+            here = [z for z in range(8) if HELD[panel][z] == src]
+            hit = functools.reduce(jnp.logical_or, [which == z for z in here])
+
+            @pl.when(hit)
+            def _(ref=ref, panel=panel):
+                p01[:, panel * WIDE : (panel + 1) * WIDE] = ref[...]
+
+    both = p01[...]
     w_hi, w_lo = split(w[...])
-    prod = dot_t(jnp.concatenate([p0, p1], 1), jnp.concatenate([p0, p1, w_hi, w_lo], 1))
+    prod = dot_t(both, jnp.concatenate([both, w_hi, w_lo], 1))
 
     def inner(a, b):
         d = prod[a * WIDE : (a + 1) * WIDE, b * WIDE : (b + 1) * WIDE]
         return d[:HALF] + lane_sign(1.0) * pltpu.roll(d[HALF:], HALF, 1)
 
-    out[0:HALF, :] = inner(0, 0)
+    row = lax.broadcasted_iota(jnp.int32, (HALF, WIDE), 0)
+    lane = lax.broadcasted_iota(jnp.int32, (HALF, WIDE), 1)
+    col = jnp.where(lane < HALF, lane, lane - HALF)
+    g00, g11 = inner(0, 0), inner(1, 1)
+    diag = jnp.where(lane < HALF, g00, pltpu.roll(g11, HALF, 1))
+    out[0:HALF, :] = jnp.where(col > row, g00, jnp.where(col < row, g11, diag))
     out[HALF : 2 * HALF, :] = inner(0, 1)
-    out[2 * HALF : 3 * HALF, :] = inner(1, 1)
-    out[3 * HALF : 4 * HALF, :] = inner(0, 2) + inner(0, 3)
-    out[4 * HALF : 5 * HALF, :] = inner(1, 2) + inner(1, 3)
-
-
-def gram(w, pq):
+    out[2 * HALF : 3 * HALF, :] = inner(0, 2) + inner(0, 3)
+    out[3 * HALF : 4 * HALF, :] = inner(1, 2) + inner(1, 3)
+
+
+def gram(pos, w, parts):
     spec = pl.BlockSpec(memory_space=VM)
     return pl.pallas_call(
         gram_kernel,
-        out_shape=jax.ShapeDtypeStruct((5 * HALF, WIDE), F32),
-        in_specs=[spec, spec],
-        out_specs=spec,
+        out_shape=(
+            jax.ShapeDtypeStruct((w.shape[0], 2 * WIDE), BF16),
+            jax.ShapeDtypeStruct((4 * HALF, WIDE), F32),
+        ),
+        in_specs=[pl.BlockSpec(memory_space=SM)] + [spec] * 5,
+        out_specs=(spec, spec),
         compiler_params=pltpu.CompilerParams(vmem_limit_bytes=32 << 20),
         name="gram",
-    )(w, pq)
+    )(pos, w, *parts)
 
 
 def inverse_factor(tr, ti):
@@ -192,31 +215,33 @@
     return jnp.concatenate([block, times_i(block)], 0)
 
 
-def finish_kernel(pos, g, w, pq, out):
-    rows = w.shape[0]
+def finish_kernel(pos, g, w, p01, out):
+    row = lax.broadcasted_iota(jnp.int32, (HALF, WIDE), 0)
     lane = lax.broadcasted_iota(jnp.int32, (HALF, WIDE), 1)
     left = lane < HALF
-    g00, g01, g11 = g[0:HALF, :], g[HALF : 2 * HALF, :], g[2 * HALF : 3 * HALF, :]
-    zero = jnp.zeros((HALF, WIDE), F32)
-
-    up_r = jnp.concatenate(
-        [jnp.where(left, g00, pltpu.roll(g01, HALF, 1)), jnp.where(left, 0.0, pltpu.roll(g11, HALF, 1))], 0
-    )
-    up_i = jnp.concatenate([jnp.where(left, pltpu.roll(g00, HALF, 1), g01), jnp.where(left, 0.0, g11)], 0)
-    low = jnp.concatenate([zero, jnp.where(left, 1.0, 0.0)], 0)
-    tr = up_r + low * jnp.transpose(up_r)
-    ti = up_i - low * jnp.transpose(up_i)
+    col = jnp.where(left, lane, lane - HALF)
+    c, g01 = g[0:HALF, :], g[HALF : 2 * HALF, :]
+    c_turn, g01_turn = pltpu.roll(c, HALF, 1), pltpu.roll(g01, HALF, 1)
+    above, below, diag = col > row, col < row, col == row
+
+    def stack(top_left, top_right, low_right):
+        return jnp.concatenate([jnp.where(left, top_left, top_right), jnp.where(left, 0.0, low_right)], 0)
+
+    once_r = stack(jnp.where(above, c, 0.0), g01_turn, jnp.where(below, c_turn, 0.0))
+    once_i = stack(jnp.where(above, c_turn, 0.0), g01, jnp.where(below, c, 0.0))
+    pivots = jnp.where(diag, c, 0.0)
+    tr = once_r + jnp.transpose(once_r) + stack(pivots, 0.0, pivots)
+    ti = once_i - jnp.transpose(once_i)
     rr, ri = inverse_factor(tr, ti)
     which = pos[0]
 
     @pl.when(which >= 2)
     def _():
-        m = g[3 * HALF : 5 * HALF, :]
+        m = g[2 * HALF : 4 * HALF, :]
         n = dot(rr, m, precision=HIGHEST) + dot(ri, times_i(m), precision=HIGHEST)
         k = dot_t(rr, n, precision=HIGHEST) - dot_t(ri, times_i(n), precision=HIGHEST)
         e_hi, e_lo = split(jnp.concatenate([embed(k[:HALF]), embed(k[HALF:])], 0))
-        p01 = jnp.concatenate([pq[:, 0].reshape(rows, WIDE), pq[:, 1].reshape(rows, WIDE)], 1)
-        out[...] = w[...] - (dot(p01, e_hi) + dot(p01, e_lo))
+        out[...] = w[...] - (dot(p01[...], e_hi) + dot(p01[...], e_lo))
 
     @pl.when(which < 2)
     def _():
@@ -228,11 +253,11 @@
         own = jnp.where(is_first, first[:HALF], second[HALF:])
         other = jnp.where(is_first, 0.0, second[:HALF])
         o_hi, o_lo = split(embed(other))
-        p0 = pq[:, 0].reshape(rows, WIDE)
+        p0 = p01[:, :WIDE]
         out[...] = dot(w[...], embed(own), precision=HIGHEST) + dot(p0, o_hi) + dot(p0, o_lo)
 
 
-def finish(pos, g, w, pq):
+def finish(pos, g, w, p01):
     spec = pl.BlockSpec(memory_space=VM)
     return pl.pallas_call(
         finish_kernel,
@@ -241,7 +266,7 @@
         out_specs=spec,
         compiler_params=pltpu.CompilerParams(vmem_limit_bytes=40 << 20),
         name="finish",
-    )(pos, g, w, pq)
+    )(pos, g, w, p01)
 
 
 def swap(x, axes):
@@ -256,11 +281,15 @@
     return jnp.sum(x.reshape((count, -1) + x.shape[1:]), axis=0)
 
 
-def slab_sum(x, inner, outer):
-    near, far = lax.axis_size(inner), lax.axis_size(outer)
-    piece = sum_pieces(swap(x, inner), near)
-    piece = sum_pieces(swap(copies(piece, far), outer), far)
-    return swap(copies(piece, near), inner)
+def slab_sum(x, axes):
+    count = lax.axis_size(axes)
+    return swap(copies(sum_pieces(swap(x, axes), count), count), axes)
+
+
+def spread(w_hi, pos):
+    far = lax.ppermute(w_hi, "panel", [(0, 4), (1, 5)])
+    own = jnp.where(pos >= 4, far, w_hi)
+    return (own,) + tuple(lax.ppermute(own, "panel", pairs) for pairs in STEPS)
 
 
 def thirds(x):
@@ -299,13 +328,10 @@
     )
     w, w_hi = chebyshev(meta.reshape(-1), nums, vectors, left, right, hop_table, turned, sym, cos_t, sin_t)
 
-    panels = lax.axis_size("panel")
-    chunk = rows // panels
-    mine = swap(w_hi, "panel")[: 2 * chunk]
-    pq = swap(copies(mine, panels), "panel").reshape(panels, 2, chunk, WIDE)
-    g = slab_sum(gram(w, pq), ("x", "core"), "y")
-    pos = lax.axis_index("panel").astype(jnp.int32).reshape(1)
-    return finish(pos, g, w, pq)
+    pos = lax.axis_index("panel").astype(jnp.int32)
+    spot = pos.reshape(1)
+    p01, part = gram(spot, w, spread(w_hi, pos))
+    return finish(spot, slab_sum(part, slab), w, p01)
 
 
 def solution(mesh):

time: 115 us -> 110 us (0.957)
  the two profiles are of different devices: /device:TPU:1 before, /device:TPU:129 now
where the time goes in v2:
time: 110 us; the launch traced here: 109 us
  blocking collectives  37.2 us (34%)
  waiting for transfers between devices  31.6 us (29%)
  Pallas kernels  16.3 us (15%)
  starting transfers between devices  9.63 us (9%)
  local copies, waits for them, and re-layouts  8.26 us (8%)
  other arithmetic  4.4 us (4%)
  between operations  1.53 us (1%)
    all_to_all x2, blocking collectives, swap(): return lax.all_to_all(x, axes, 0, 0, tiled=True)  37.2 us
    ppermute x3, waiting for transfers between devices, spread(): lax.ppermute(own, 'panel', pairs)  31.6 us
    pallas_call x1, Pallas kernels, finish(): pl.pallas_call(finish_kernel, out_shape=jax.ShapeDtypeStruct(w.shape, F32...  13.2 us
    unnamed x22, local copies, waits for them, and re-layouts  6.35 us
    ppermute x3, starting transfers between devices, spread(): lax.ppermute(own, 'panel', pairs)  3.26 us
    ppermute x1, starting transfers between devices, body(): left = lax.ppermute(up, slab, [(i, i + 1) for i in range(count - 1)])  3 us
    ppermute x1, starting transfers between devices, body(): right = lax.ppermute(down, slab, [(i + 1, i) for i in range(count - 1)])  2.57 us
    pallas_call x1, Pallas kernels, chebyshev(): pl.pallas_call(filter_kernel, out_shape=(jax.ShapeDtypeStruct(v.shape, F3...  2.35 us
  transfers between devices with their start and end apart: 6, of which 2 were waited for; matrix products, arithmetic and copies ran while one was open for 3% of the time, Pallas kernels for 0%

profile of v2, /device:TPU:129, one launch (start us, length us, event | category | flops | bytes accessed | tf_op | source)
XLA Modules:
  0.0 109.0 jit_solution(10131672731520506102)
XLA Ops:
  0.0 0.0 copy-start.9
  0.0 0.0 copy-start
  0.0 0.9 copy.19
  0.9 0.0 copy-start.8
  0.9 0.7 copy.20
  1.6 0.1 pad_add_fusion
  1.7 1.1 convert.32
  2.8 0.7 fusion.3
  3.5 2.6 %collective-permute-start.1 = (bf16[528,128]{1,0:T(8,128)(2,1)}, bf16[528,128]{1,0:T(8,128)(2,1)S(1)}, u32[]{:S(2)}, u32[]{:S(2)}) collective-permute-start(bf16[528,128]{1,0:T(8,128)(2,1)} %fusion.3), channel_id=1, source_target_pairs={{8,0},{16,8},{24,16},{32,24},{40,32},{48,40},{56,48},{64,56},{72,6... | collective-permute-start | bytes 405512 | tf_op jit(solution)/shard_map/ppermute | solution.py:315
  6.0 0.7 fusion.2
  6.7 3.0 %collective-permute-start = (bf16[528,128]{1,0:T(8,128)(2,1)}, bf16[528,128]{1,0:T(8,128)(2,1)S(1)}, u32[]{:S(2)}, u32[]{:S(2)}) collective-permute-start(bf16[528,128]{1,0:T(8,128)(2,1)} %fusion.2), channel_id=1, source_target_pairs={{0,8},{8,16},{16,24},{24,32},{32,40},{40,48},{48,56},{56,64},{64,7... | collective-permute-start | bytes 405512 | tf_op jit(solution)/shard_map/ppermute | solution.py:314
  9.7 0.0 copy-done.8
  9.7 0.0 copy-done.9
  9.7 0.1 fusion.7
  9.8 0.0 copy-done
  9.8 0.5 copy.21
  10.4 0.3 multiply_convert_fusion.sym
  10.7 0.6 pad_maximum_fusion.1
  11.3 0.1 copy.22
  11.5 0.9 copy.23
  13.7 0.1 pad_maximum_fusion.2.nums
  13.7 0.0 collective-permute-done.1.right
  13.7 0.0 copy-start.4
  13.8 0.7 copy-done.4
  14.4 0.0 collective-permute-done.left
  14.4 0.7 copy-done.6
  15.1 0.7 add_add_fusion
  15.8 0.1 add.32.meta
  15.9 1.0 copy-done.1
  17.0 0.9 copy-done.5
  17.9 0.9 copy-done.7
  18.8 2.3 %chebyshev.1 = (f32[1024,128]{1,0:T(8,128)S(1)}, bf16[1024,128]{1,0:T(8,128)(2,1)S(1)}) custom-call(s32[24]{0:T(128)S(1)} %add.32.meta, f32[4]{0:T(128)S(1)} %pad_maximum_fusion.2.nums, f32[1024,128]{1,0:T(8,128)S(1)} %copy-done.1, bf16[528,128]{1,0:T(8,128)(2,1)S(1)} %copy-done.7, bf16[528,128]{1,0:T(8,128)(2,1)S(1)} %copy-done.5, ...), custom_call_target="tpu_custom_call" | custom-call | tf_op jit(solution)/shard_map/chebyshev/pallas_call | solution.py:112
  21.1 0.0 copy-start.2
  21.1 0.8 copy-done.2
  21.9 0.8 collective-permute-start.2
  22.7 0.0 collective-permute-done.2
  22.8 1.3 %collective-permute-start.3 = (bf16[1024,128]{1,0:T(8,128)(2,1)S(1)}, bf16[1024,128]{1,0:T(8,128)(2,1)S(1)}, u32[]{:S(2)}, u32[]{:S(2)}) collective-permute-start(bf16[1024,128]{1,0:T(8,128)(2,1)S(1)} %broadcast_select_fusion.own), channel_id=1, source_target_pairs={{0,1},{4,5},{1,2},{5,6},{8,9},{12,13},{9,10},{13,14},{16,17},{20,2... | collective-permute-start | bytes 786440 | tf_op jit(solution)/shard_map/ppermute | solution.py:292
  24.1 0.7 collective-permute-start.4
  24.8 1.3 %collective-permute-start.5 = (bf16[1024,128]{1,0:T(8,128)(2,1)S(1)}, bf16[1024,128]{1,0:T(8,128)(2,1)S(1)}, u32[]{:S(2)}, u32[]{:S(2)}) collective-permute-start(bf16[1024,128]{1,0:T(8,128)(2,1)S(1)} %broadcast_select_fusion.own), channel_id=1, source_target_pairs={{0,6},{4,2},{1,3},{5,7},{8,14},{12,10},{9,11},{13,15},{16,22},{20,... | collective-permute-start | bytes 786440 | tf_op jit(solution)/shard_map/ppermute | solution.py:292
  26.1 19.7 %collective-permute-done.3.first = bf16[1024,128]{1,0:T(8,128)(2,1)S(1)} collective-permute-done((bf16[1024,128]{1,0:T(8,128)(2,1)S(1)}, bf16[1024,128]{1,0:T(8,128)(2,1)S(1)}, u32[]{:S(2)}, u32[]{:S(2)}) %collective-permute-start.3) | collective-permute-done | bytes 262176 | tf_op jit(solution)/shard_map/ppermute | solution.py:292
  45.7 0.0 collective-permute-done.4.second
  45.7 12.0 %collective-permute-done.5.third = bf16[1024,128]{1,0:T(8,128)(2,1)S(1)} collective-permute-done((bf16[1024,128]{1,0:T(8,128)(2,1)S(1)}, bf16[1024,128]{1,0:T(8,128)(2,1)S(1)}, u32[]{:S(2)}, u32[]{:S(2)}) %collective-permute-start.5) | collective-permute-done | bytes 262176 | tf_op jit(solution)/shard_map/ppermute | solution.py:292
  57.7 0.0 copy-done.3
  57.7 0.7 gram.1
  58.4 22.3 %all_to_all.17 = f32[64,4,128]{2,1,0:T(4,128)S(1)} all-to-all(f32[64,4,128]{2,1,0:T(4,128)S(1)} %bitcast.14), channel_id=1, replica_groups=mesh['y'=8,'x'=4,'core'=2,'panel'=8] {'y','x','core'}, dimensions={0} | all-to-all | bytes 262144 | tf_op jit(solution)/shard_map/all_to_all | solution.py:273
  80.7 0.1 reduce_sum.9
  80.8 14.9 %all_to_all.18 = f32[64,4,128]{2,1,0:T(4,128)S(1)} all-to-all(f32[64,4,128]{2,1,0:T(4,128)S(1)} %broadcast_in_dim.5), channel_id=1, replica_groups=mesh['y'=8,'x'=4,'core'=2,'panel'=8] {'y','x','core'}, dimensions={0} | all-to-all | bytes 262144 | tf_op jit(solution)/shard_map/all_to_all | solution.py:273
  95.7 13.2 %finish.1 = f32[1024,128]{1,0:T(8,128)} custom-call(s32[1]{0:T(128)} %bitcast.pos, f32[256,128]{1,0:T(8,128)S(1)} %bitcast.11, f32[1024,128]{1,0:T(8,128)S(1)} %copy-done.3, bf16[1024,256]{1,0:T(8,128)(2,1)S(1)} %get-tuple-element.36.p01), custom_call_target="tpu_custom_call" | custom-call | tf_op jit(solution)/shard_map/finish/pallas_call | solution.py:262
  (14 shorter events, 0.1 us)
Async XLA Ops:
  0.0 9.7 %copy-start.9 = (f32[16,256]{1,0:T(8,128)S(1)}, f32[16,256]{1,0:T(8,128)}, u32[]{:S(2)}) copy-start(f32[16,256]{1,0:T(8,128)} %param.16) | copy-start | bytes 49156
  0.0 9.8 %copy-start = (bf16[8,256,256]{2,1,0:T(8,128)(2,1)S(1)}, bf16[8,256,256]{2,1,0:T(8,128)(2,1)}, u32[]{:S(2)}) copy-start(bf16[8,256,256]{2,1,0:T(8,128)(2,1)} %hop.1) | copy-start | bytes 3145732
  0.9 8.9 %copy-start.8 = (s32[4,2]{1,0:T(4,128)}, s32[4,2]{1,0:T(4,128)S(1)}, u32[]{:S(2)}) copy-start(s32[4,2]{1,0:T(4,128)S(1)} %broadcast_add_fusion) | copy-start | bytes 100
  3.5 10.3 %collective-permute-start.1 = (bf16[528,128]{1,0:T(8,128)(2,1)}, bf16[528,128]{1,0:T(8,128)(2,1)S(1)}, u32[]{:S(2)}, u32[]{:S(2)}) collective-permute-start(bf16[528,128]{1,0:T(8,128)(2,1)} %fusion.3), channel_id=1, source_target_pairs={{8,0},{16,8},{24,16},{32,24},{40,32},{48,40},{56,48},{64,56},{72,6... | collective-permute-start | bytes 405512 | tf_op jit(solution)/shard_map/ppermute | solution.py:315
  6.7 7.7 %collective-permute-start = (bf16[528,128]{1,0:T(8,128)(2,1)}, bf16[528,128]{1,0:T(8,128)(2,1)S(1)}, u32[]{:S(2)}, u32[]{:S(2)}) collective-permute-start(bf16[528,128]{1,0:T(8,128)(2,1)} %fusion.2), channel_id=1, source_target_pairs={{0,8},{8,16},{16,24},{24,32},{32,40},{40,48},{48,56},{56,64},{64,7... | collective-permute-start | bytes 405512 | tf_op jit(solution)/shard_map/ppermute | solution.py:314
  13.7 0.7 copy-start.4
  14.4 0.7 copy-start.6
  15.9 1.0 copy-start.1
  17.0 0.9 copy-start.5
  17.9 0.9 copy-start.7
  21.1 0.8 copy-start.2
  21.9 35.8 %copy-start.3 = (f32[1024,128]{1,0:T(8,128)S(1)}, f32[1024,128]{1,0:T(8,128)}, u32[]{:S(2)}) copy-start(f32[1024,128]{1,0:T(8,128)} %copy-done.2) | copy-start | bytes 1572868
  21.9 0.8 collective-permute-start.2
  22.8 22.9 %collective-permute-start.3 = (bf16[1024,128]{1,0:T(8,128)(2,1)S(1)}, bf16[1024,128]{1,0:T(8,128)(2,1)S(1)}, u32[]{:S(2)}, u32[]{:S(2)}) collective-permute-start(bf16[1024,128]{1,0:T(8,128)(2,1)S(1)} %broadcast_select_fusion.own), channel_id=1, source_target_pairs={{0,1},{4,5},{1,2},{5,6},{8,9},{12,13},{9,10},{13,14},{16,17},{20,2... | collective-permute-start | bytes 786440 | tf_op jit(solution)/shard_map/ppermute | solution.py:292
  24.1 21.6 %collective-permute-start.4 = (bf16[1024,128]{1,0:T(8,128)(2,1)S(1)}, bf16[1024,128]{1,0:T(8,128)(2,1)S(1)}, u32[]{:S(2)}, u32[]{:S(2)}) collective-permute-start(bf16[1024,128]{1,0:T(8,128)(2,1)S(1)} %broadcast_select_fusion.own), channel_id=1, source_target_pairs={{0,7},{4,3},{1,0},{5,4},{8,15},{12,11},{9,8},{13,12},{16,23},{20,1... | collective-permute-start | bytes 786440 | tf_op jit(solution)/shard_map/ppermute | solution.py:292
  24.8 32.9 %collective-permute-start.5 = (bf16[1024,128]{1,0:T(8,128)(2,1)S(1)}, bf16[1024,128]{1,0:T(8,128)(2,1)S(1)}, u32[]{:S(2)}, u32[]{:S(2)}) collective-permute-start(bf16[1024,128]{1,0:T(8,128)(2,1)S(1)} %broadcast_select_fusion.own), channel_id=1, source_target_pairs={{0,6},{4,2},{1,3},{5,7},{8,14},{12,10},{9,11},{13,15},{16,22},{20,... | collective-permute-start | bytes 786440 | tf_op jit(solution)/shard_map/ppermute | solution.py:292

commit v3 on v2

--- a/solution.py
+++ b/solution.py
@@ -15,12 +15,13 @@
 WIDE = 128
 HALF = 64
 META = 16
+MISSING = 8
 STEPS = (
-    [(0, 1), (4, 5), (1, 2), (5, 6)],
-    [(0, 7), (4, 3), (1, 0), (5, 4)],
-    [(0, 6), (4, 2), (1, 3), (5, 7)],
+    [(0, 1), (3, 4), (1, 2), (6, 7)],
+    [(0, 7), (3, 2), (1, 0), (6, 5)],
+    [(0, 6), (3, 5), (1, 3), (6, 4)],
 )
-HELD = ((0, 1, 3, 2, 0, 1, 3, 2), (2, 0, 1, 3, 2, 0, 1, 3))
+HELD = ((0, 1, 2, 0, 1, 3, 3, 2), (2, 0, 1, 3, 3, 2, 0, 1))
 VM = pltpu.VMEM
 SM = pltpu.SMEM
 
@@ -47,21 +48,71 @@
     return hi, (x - hi.astype(F32)).astype(BF16)
 
 
-def filter_kernel(meta, nums, v, left, right, hop, hop_t, sym, cos_t, sin_t, w, w_hi, cosb, sinb, z, y1, y1b):
-    centre, inv_h, has_left, has_right = nums[0], nums[1], nums[2], nums[3]
+def pack_kernel(v, kinds, phase, up, down, tile):
+    half = v.shape[0] // 2
+    down[:half, :] = v[:half, :].astype(BF16)
+    up[:half, :] = v[half:, :].astype(BF16)
+    tile[...] = jnp.zeros(tile.shape, F32)
+    tile[0:2, 0:4] = (kinds[...] - MISSING).astype(F32)
+    tile[2:3, 0:4] = phase[...].astype(F32)
+    tile[3:4, :] = jnp.ones((1, WIDE), F32)
+    info = tile[...].astype(BF16)
+    down[half:, :] = info
+    up[half:, :] = info
+
+
+def pack(v, kinds, phase):
+    spec = pl.BlockSpec(memory_space=VM)
+    shape = jax.ShapeDtypeStruct((v.shape[0] // 2 + META, WIDE), BF16)
+    return pl.pallas_call(
+        pack_kernel,
+        out_shape=(shape, shape),
+        in_specs=[spec] * 3,
+        out_specs=(spec, spec),
+        scratch_shapes=[VM((META, WIDE), F32)],
+        compiler_params=pltpu.CompilerParams(vmem_limit_bytes=16 << 20),
+        name="pack",
+    )(v, kinds, phase)
+
+
+def filter_kernel(
+    kinds, phase, shift, width, v, sides, hop, hop_t, sym, cos_t, sin_t,
+    w, w_hi, cosb, sinb, z, y1, y1b,
+):
+    half = v.shape[0] // 2
+    left, right = sides.at[0 : half + META], sides.at[half + META :]
+    centre = shift[0]
+    inv_h = 1.0 / jnp.broadcast_to(width[0], (1, WIDE))
     pick = lax.broadcasted_iota(jnp.int32, (cos_t.shape[1], WIDE), 0) % 16
+    tile_l = left[half : half + META, :].astype(F32)
+    tile_r = right[half : half + META, :].astype(F32)
+    row = lax.broadcasted_iota(jnp.int32, (META, WIDE), 0)
+    lane = lax.broadcasted_iota(jnp.int32, (META, WIDE), 1)
+
+    def item(tile, i, j):
+        return jnp.sum(jnp.where((row == i) & (lane == j), tile, 0.0)).astype(jnp.int32)
+
+    own = {-1: item(tile_l, 0, 3) + MISSING, 4: item(tile_r, 0, 0) + MISSING}
+    ahead_of = {r: item(tile_l, 1, 4 + r) + MISSING for r in (-2, -1)}
+    ahead_of[4] = item(tile_r, 1, 0) + MISSING
+    own.update({r: kinds[0, r] for r in range(4)})
+    ahead_of.update({r: kinds[1, r] for r in range(4)})
+    pattern = {r: tile_l[2:3, 4 + r : 5 + r].astype(jnp.int32) for r in (-2, -1)}
+    pattern[4] = tile_r[2:3, 0:1].astype(jnp.int32)
+    pattern.update({r: phase[0, r] for r in range(4)})
+    has_left, has_right = tile_l[3:4, :], tile_r[3:4, :]
 
     def own_kind(r):
-        return meta[3 * (r + 2)]
+        return own[r]
 
     def next_kind(r):
-        return meta[3 * (r + 2) + 1]
+        return ahead_of[r]
 
     def flag(kind):
-        return jnp.where(kind < 8, 1.0, 0.0).astype(F32)
+        return jnp.where(kind < MISSING, 1.0, 0.0).astype(F32)
 
     for r in range(-2, 5):
-        hot = jnp.where(pick == meta[3 * (r + 2) + 2], 1.0, 0.0).astype(BF16)
+        hot = jnp.where(pick == pattern[r], 1.0, 0.0).astype(BF16)
         cosb[r + 2] = dot(cos_t[...], hot)
         sinb[r + 2] = dot(sin_t[...], hot)
 
@@ -106,13 +157,13 @@
         w_hi[r * BLK : (r + 1) * BLK, :] = y.astype(BF16)
 
 
-def chebyshev(meta, nums, v, left, right, hop, hop_t, sym, cos_t, sin_t):
+def chebyshev(*args):
     spec = pl.BlockSpec(memory_space=VM)
     smem = pl.BlockSpec(memory_space=SM)
     return pl.pallas_call(
         filter_kernel,
-        out_shape=(jax.ShapeDtypeStruct(v.shape, F32), jax.ShapeDtypeStruct(v.shape, BF16)),
-        in_specs=[smem, smem] + [spec] * 8,
+        out_shape=(jax.ShapeDtypeStruct(args[4].shape, F32), jax.ShapeDtypeStruct(args[4].shape, BF16)),
+        in_specs=[smem] * 4 + [spec] * 7,
         out_specs=(spec, spec),
         scratch_shapes=[
             VM((7, BLK, WIDE), F32),
@@ -121,9 +172,9 @@
             VM((4, BLK, WIDE), F32),
             VM((6, BLK, WIDE), BF16),
         ],
-        compiler_params=pltpu.CompilerParams(vmem_limit_bytes=40 << 20),
+        compiler_params=pltpu.CompilerParams(vmem_limit_bytes=16 << 20),
         name="chebyshev",
-    )(meta, nums, v, left, right, hop, hop_t, sym, cos_t, sin_t)
+    )(*args)
 
 
 def gram_kernel(pos, w, own, first, second, third, p01, out):
@@ -166,7 +217,7 @@
         ),
         in_specs=[pl.BlockSpec(memory_space=SM)] + [spec] * 5,
         out_specs=(spec, spec),
-        compiler_params=pltpu.CompilerParams(vmem_limit_bytes=32 << 20),
+        compiler_params=pltpu.CompilerParams(vmem_limit_bytes=16 << 20),
         name="gram",
     )(pos, w, *parts)
 
@@ -264,7 +315,7 @@
         out_shape=jax.ShapeDtypeStruct(w.shape, F32),
         in_specs=[pl.BlockSpec(memory_space=SM), spec, spec, spec],
         out_specs=spec,
-        compiler_params=pltpu.CompilerParams(vmem_limit_bytes=40 << 20),
+        compiler_params=pltpu.CompilerParams(vmem_limit_bytes=16 << 20),
         name="finish",
     )(pos, g, w, p01)
 
@@ -287,8 +338,8 @@
 
 
 def spread(w_hi, pos):
-    far = lax.ppermute(w_hi, "panel", [(0, 4), (1, 5)])
-    own = jnp.where(pos >= 4, far, w_hi)
+    far = lax.ppermute(w_hi, "panel", [(0, 3), (1, 6)])
+    own = jnp.where((pos == 3) | (pos == 6), far, w_hi)
     return (own,) + tuple(lax.ppermute(own, "panel", pairs) for pairs in STEPS)
 
 
@@ -301,33 +352,19 @@
 def body(vectors, hop_table, block_kind, block_phase, phase_angles, centre, half_width):
     slab = ("y", "x", "core")
     count = lax.axis_size(slab)
-    me = lax.axis_index(slab)
-    rows = vectors.shape[0]
-    table = jnp.concatenate([block_kind - 8, block_phase[:, None]], axis=1)
-
-    def packet(part, info):
-        extra = jnp.zeros((META, WIDE), F32).at[:2, :3].set(info.astype(F32))
-        return jnp.concatenate([part.astype(BF16), extra.astype(BF16)], axis=0)
-
-    up = packet(vectors[rows // 2 :], table[2:])
-    down = packet(vectors[: rows // 2], table[:2])
+    kinds, phase = block_kind.T, block_phase[None, :]
+    up, down = pack(vectors, kinds, phase)
     left = lax.ppermute(up, slab, [(i, i + 1) for i in range(count - 1)])
     right = lax.ppermute(down, slab, [(i + 1, i) for i in range(count - 1)])
+    sides = jnp.concatenate([left, right], axis=0)
     wide = hop_table.astype(F32)
     turned = jnp.transpose(hop_table, (0, 2, 1))
     sym = ((wide + turned.astype(F32)) * 0.5).astype(BF16)
     cos_t = thirds(jnp.cos(phase_angles))
     sin_t = thirds(jnp.sin(phase_angles))
-
-    def info(packed):
-        return packed[rows // 2 : rows // 2 + 2, :3].astype(jnp.int32)
-
-    meta = jnp.concatenate([info(left), table, info(right)], axis=0) + jnp.array([8, 8, 0], jnp.int32)
-    nums = jnp.stack(
-        [centre[0], 1.0 / half_width[0], (me > 0).astype(F32), (me < count - 1).astype(F32)]
+    w, w_hi = chebyshev(
+        kinds, phase, centre, half_width, vectors, sides, hop_table, turned, sym, cos_t, sin_t
     )
-    w, w_hi = chebyshev(meta.reshape(-1), nums, vectors, left, right, hop_table, turned, sym, cos_t, sin_t)
-
     pos = lax.axis_index("panel").astype(jnp.int32)
     spot = pos.reshape(1)
     p01, part = gram(spot, w, spread(w_hi, pos))

time: 110 us -> 104 us (0.945)
  the two profiles are of different devices: /device:TPU:129 before, /device:TPU:1 now
where the time goes in v3:
time: 104 us
  blocking collectives  38.1 us (37%)
  starting transfers between devices  26.8 us (26%)
  Pallas kernels  16.6 us (16%)
  waiting for transfers between devices  12.3 us (12%)
  local copies, waits for them, and re-layouts  6.83 us (7%)
  between operations  1.53 us (1%)
  other arithmetic  1.43 us (1%)
    all_to_all x2, blocking collectives, swap(): return lax.all_to_all(x, axes, 0, 0, tiled=True)  38.1 us
    pallas_call x1, Pallas kernels, finish(): pl.pallas_call(finish_kernel, out_shape=jax.ShapeDtypeStruct(w.shape, F32...  12.9 us
    ppermute x3, starting transfers between devices, spread(): lax.ppermute(own, 'panel', pairs)  12.5 us
    ppermute x3, waiting for transfers between devices, spread(): lax.ppermute(own, 'panel', pairs)  7.22 us
    ppermute x1, starting transfers between devices, body(): right = lax.ppermute(down, slab, [(i + 1, i) for i in range(count - 1)])  6.21 us
    unnamed x19, local copies, waits for them, and re-layouts  5.79 us
    ppermute x1, waiting for transfers between devices, spread(): far = lax.ppermute(w_hi, 'panel', [(0, 3), (1, 6)])  5.12 us
    ppermute x1, starting transfers between devices, body(): left = lax.ppermute(up, slab, [(i, i + 1) for i in range(count - 1)])  4.5 us
  transfers between devices with their start and end apart: 6, of which 3 were waited for; matrix products, arithmetic and copies ran while one was open for 3% of the time, Pallas kernels for 0%

profile of v3, /device:TPU:1, one launch (start us, length us, event | category | flops | bytes accessed | tf_op | source)
XLA Modules:
  0.0 103.7 jit_solution(11157370221763559642)
XLA Ops:
  0.0 0.0 copy-start.3
  0.0 1.0 %copy-done.3 = f32[1024,128]{1,0:T(8,128)S(1)} copy-done((f32[1024,128]{1,0:T(8,128)S(1)}, f32[1024,128]{1,0:T(8,128)}, u32[]{:S(2)}) %copy-start.3) | copy-done | bytes 524312
  1.0 0.0 copy-start.5
  1.0 0.7 copy-done.5
  1.7 0.0 copy-start.7
  1.7 0.7 copy-done.7
  2.4 0.7 pack.1
  3.1 4.5 %collective-permute-start = (bf16[528,128]{1,0:T(8,128)(2,1)}, bf16[528,128]{1,0:T(8,128)(2,1)}, u32[]{:S(2)}, u32[]{:S(2)}) collective-permute-start(bf16[528,128]{1,0:T(8,128)(2,1)} %get-tuple-element.11), channel_id=1, source_target_pairs={{0,8},{8,16},{16,24},{24,32},{32,40},{40,48},{48,56},{56,64},{64,7... | collective-permute-start | bytes 405512 | tf_op jit(solution)/shard_map/ppermute | solution.py:357
  7.6 6.2 %collective-permute-start.1 = (bf16[528,128]{1,0:T(8,128)(2,1)S(1)}, bf16[528,128]{1,0:T(8,128)(2,1)}, u32[]{:S(2)}, u32[]{:S(2)}) collective-permute-start(bf16[528,128]{1,0:T(8,128)(2,1)S(1)} %get-tuple-element.12), channel_id=1, source_target_pairs={{8,0},{16,8},{24,16},{32,24},{40,32},{48,40},{56,48},{64,56},{72,6... | collective-permute-start | bytes 405512 | tf_op jit(solution)/shard_map/ppermute | solution.py:358
  13.8 0.8 fusion.2
  14.6 0.0 copy-start
  14.6 1.6 %copy.11 = bf16[8,256,256]{1,2,0:T(8,128)(2,1)S(1)} copy(bf16[8,256,256]{2,1,0:T(8,128)(2,1)} %hop.1) | data formatting | bytes 2097152 | tf_op args[1]
  16.2 0.0 copy-done
  16.2 0.0 copy-start.6
  16.2 0.0 copy-start.8
  16.2 0.3 multiply_convert_fusion.sym
  16.6 0.1 copy.12
  16.7 0.1 copy.13
  18.1 0.0 collective-permute-done
  18.1 0.0 collective-permute-done.1
  18.1 1.0 pad_maximum_fusion.sides
  19.1 0.0 copy-done.6
  19.1 0.0 copy-done.8
  19.1 0.0 copy-start.4
  19.2 1.0 copy-done.4
  20.2 2.3 %chebyshev.1 = (f32[1024,128]{1,0:T(8,128)S(1)}, bf16[1024,128]{1,0:T(8,128)(2,1)S(1)}) custom-call(s32[2,4]{1,0:T(2,128)S(1)} %bitcast.15, s32[1,4]{1,0:T(1,128)S(1)} %bitcast.17, f32[1]{0:T(128)S(6)} %copy.14.shift, f32[1]{0:T(128)S(6)} %copy.15.width, f32[1024,128]{1,0:T(8,128)S(1)} %copy-done.4, bf16[1056,128]{1,0:T(8,128)(2,1)S(1)} %pad_maximum_fusion.sides, ...), custom_call_target="tpu_custom_call" | custom-call | tf_op jit(solution)/shard_map/chebyshev/pallas_call | solution.py:163
  22.5 0.0 copy-start.1
  22.5 0.8 copy-done.1
  23.3 0.0 copy-start.2
  23.3 3.6 %collective-permute-start.2 = (bf16[1024,128]{1,0:T(8,128)(2,1)S(1)}, bf16[1024,128]{1,0:T(8,128)(2,1)S(1)}, u32[]{:S(2)}, u32[]{:S(2)}) collective-permute-start(bf16[1024,128]{1,0:T(8,128)(2,1)S(1)} %get-tuple-element.14), channel_id=1, source_target_pairs={{0,3},{1,6},{8,11},{9,14},{16,19},{17,22},{24,27},{25,30},{32,35},... | collective-permute-start | bytes 786440 | tf_op jit(solution)/shard_map/ppermute | solution.py:341
  27.0 5.1 %collective-permute-done.2 = bf16[1024,128]{1,0:T(8,128)(2,1)S(1)} collective-permute-done((bf16[1024,128]{1,0:T(8,128)(2,1)S(1)}, bf16[1024,128]{1,0:T(8,128)(2,1)S(1)}, u32[]{:S(2)}, u32[]{:S(2)}) %collective-permute-start.2) | collective-permute-done | bytes 262176 | tf_op jit(solution)/shard_map/ppermute | solution.py:341
  32.1 6.1 %collective-permute-start.3 = (bf16[1024,128]{1,0:T(8,128)(2,1)S(1)}, bf16[1024,128]{1,0:T(8,128)(2,1)S(1)}, u32[]{:S(2)}, u32[]{:S(2)}) collective-permute-start(bf16[1024,128]{1,0:T(8,128)(2,1)S(1)} %broadcast_select_fusion.own), channel_id=1, source_target_pairs={{0,1},{3,4},{1,2},{6,7},{8,9},{11,12},{9,10},{14,15},{16,17},{19,2... | collective-permute-start | bytes 786440 | tf_op jit(solution)/shard_map/ppermute | solution.py:343
  38.3 1.9 %collective-permute-start.4 = (bf16[1024,128]{1,0:T(8,128)(2,1)S(1)}, bf16[1024,128]{1,0:T(8,128)(2,1)S(1)}, u32[]{:S(2)}, u32[]{:S(2)}) collective-permute-start(bf16[1024,128]{1,0:T(8,128)(2,1)S(1)} %broadcast_select_fusion.own), channel_id=1, source_target_pairs={{0,7},{3,2},{1,0},{6,5},{8,15},{11,10},{9,8},{14,13},{16,23},{19,1... | collective-permute-start | bytes 786440 | tf_op jit(solution)/shard_map/ppermute | solution.py:343
  40.2 4.4 %collective-permute-start.5 = (bf16[1024,128]{1,0:T(8,128)(2,1)S(1)}, bf16[1024,128]{1,0:T(8,128)(2,1)S(1)}, u32[]{:S(2)}, u32[]{:S(2)}) collective-permute-start(bf16[1024,128]{1,0:T(8,128)(2,1)S(1)} %broadcast_select_fusion.own), channel_id=1, source_target_pairs={{0,6},{3,5},{1,3},{6,4},{8,14},{11,13},{9,11},{14,12},{16,22},{19,... | collective-permute-start | bytes 786440 | tf_op jit(solution)/shard_map/ppermute | solution.py:343
  44.6 0.0 collective-permute-done.3.first
  44.6 3.7 %collective-permute-done.4.second = bf16[1024,128]{1,0:T(8,128)(2,1)S(1)} collective-permute-done((bf16[1024,128]{1,0:T(8,128)(2,1)S(1)}, bf16[1024,128]{1,0:T(8,128)(2,1)S(1)}, u32[]{:S(2)}, u32[]{:S(2)}) %collective-permute-start.4) | collective-permute-done | bytes 262176 | tf_op jit(solution)/shard_map/ppermute | solution.py:343
  48.3 3.5 %collective-permute-done.5.third = bf16[1024,128]{1,0:T(8,128)(2,1)S(1)} collective-permute-done((bf16[1024,128]{1,0:T(8,128)(2,1)S(1)}, bf16[1024,128]{1,0:T(8,128)(2,1)S(1)}, u32[]{:S(2)}, u32[]{:S(2)}) %collective-permute-start.5) | collective-permute-done | bytes 262176 | tf_op jit(solution)/shard_map/ppermute | solution.py:343
  51.9 0.0 copy-done.2
  51.9 0.7 gram.1
  52.6 23.1 %all_to_all.17 = f32[64,4,128]{2,1,0:T(4,128)S(1)} all-to-all(f32[64,4,128]{2,1,0:T(4,128)S(1)} %bitcast.13), channel_id=1, replica_groups=mesh['y'=8,'x'=4,'core'=2,'panel'=8] {'y','x','core'}, dimensions={0} | all-to-all | bytes 262144 | tf_op jit(solution)/shard_map/all_to_all | solution.py:324
  75.7 0.1 reduce_sum.9
  75.8 14.9 %all_to_all.18 = f32[64,4,128]{2,1,0:T(4,128)S(1)} all-to-all(f32[64,4,128]{2,1,0:T(4,128)S(1)} %broadcast_in_dim.10), channel_id=1, replica_groups=mesh['y'=8,'x'=4,'core'=2,'panel'=8] {'y','x','core'}, dimensions={0} | all-to-all | bytes 262144 | tf_op jit(solution)/shard_map/all_to_all | solution.py:324
  90.8 12.9 %finish.1 = f32[1024,128]{1,0:T(8,128)} custom-call(s32[1]{0:T(128)} %bitcast.pos, f32[256,128]{1,0:T(8,128)S(1)} %bitcast.10, f32[1024,128]{1,0:T(8,128)S(1)} %copy-done.2, bf16[1024,256]{1,0:T(8,128)(2,1)S(1)} %get-tuple-element.16.p01), custom_call_target="tpu_custom_call" | custom-call | tf_op jit(solution)/shard_map/finish/pallas_call | solution.py:313
  (5 shorter events, 0.1 us)
Async XLA Ops:
  0.0 1.0 %copy-start.3 = (f32[1024,128]{1,0:T(8,128)S(1)}, f32[1024,128]{1,0:T(8,128)}, u32[]{:S(2)}) copy-start(f32[1024,128]{1,0:T(8,128)} %v.3) | copy-start | bytes 1572868
  1.0 0.7 copy-start.5
  1.7 0.7 copy-start.7
  3.1 15.0 %collective-permute-start = (bf16[528,128]{1,0:T(8,128)(2,1)}, bf16[528,128]{1,0:T(8,128)(2,1)}, u32[]{:S(2)}, u32[]{:S(2)}) collective-permute-start(bf16[528,128]{1,0:T(8,128)(2,1)} %get-tuple-element.11), channel_id=1, source_target_pairs={{0,8},{8,16},{16,24},{24,32},{32,40},{40,48},{48,56},{56,64},{64,7... | collective-permute-start | bytes 405512 | tf_op jit(solution)/shard_map/ppermute | solution.py:357
  7.6 10.5 %collective-permute-start.1 = (bf16[528,128]{1,0:T(8,128)(2,1)S(1)}, bf16[528,128]{1,0:T(8,128)(2,1)}, u32[]{:S(2)}, u32[]{:S(2)}) collective-permute-start(bf16[528,128]{1,0:T(8,128)(2,1)S(1)} %get-tuple-element.12), channel_id=1, source_target_pairs={{8,0},{16,8},{24,16},{32,24},{40,32},{48,40},{56,48},{64,56},{72,6... | collective-permute-start | bytes 405512 | tf_op jit(solution)/shard_map/ppermute | solution.py:358
  14.6 1.6 %copy-start = (bf16[8,256,256]{2,1,0:T(8,128)(2,1)S(1)}, bf16[8,256,256]{2,1,0:T(8,128)(2,1)}, u32[]{:S(2)}) copy-start(bf16[8,256,256]{2,1,0:T(8,128)(2,1)} %hop.1) | copy-start | bytes 3145732
  16.2 2.9 %copy-start.6 = (s32[4,2]{0,1:T(2,128)S(1)}, s32[4,2]{0,1:T(2,128)}, u32[]{:S(2)}) copy-start(s32[4,2]{0,1:T(2,128)} %param.9) | copy-start | bytes 100
  16.2 2.9 %copy-start.8 = (s32[4]{0:T(128)S(1)}, s32[4]{0:T(128)}, u32[]{:S(2)}) copy-start(s32[4]{0:T(128)} %param.10) | copy-start | bytes 52
  19.1 1.0 %copy-start.4 = (f32[1024,128]{1,0:T(8,128)S(1)}, f32[1024,128]{1,0:T(8,128)}, u32[]{:S(2)}) copy-start(f32[1024,128]{1,0:T(8,128)} %v.3) | copy-start | bytes 1572868
  22.5 0.8 copy-start.1
  23.3 28.5 %copy-start.2 = (f32[1024,128]{1,0:T(8,128)S(1)}, f32[1024,128]{1,0:T(8,128)}, u32[]{:S(2)}) copy-start(f32[1024,128]{1,0:T(8,128)} %copy-done.1) | copy-start | bytes 1572868
  23.3 8.8 %collective-permute-start.2 = (bf16[1024,128]{1,0:T(8,128)(2,1)S(1)}, bf16[1024,128]{1,0:T(8,128)(2,1)S(1)}, u32[]{:S(2)}, u32[]{:S(2)}) collective-permute-start(bf16[1024,128]{1,0:T(8,128)(2,1)S(1)} %get-tuple-element.14), channel_id=1, source_target_pairs={{0,3},{1,6},{8,11},{9,14},{16,19},{17,22},{24,27},{25,30},{32,35},... | collective-permute-start | bytes 786440 | tf_op jit(solution)/shard_map/ppermute | solution.py:341
  32.1 12.5 %collective-permute-start.3 = (bf16[1024,128]{1,0:T(8,128)(2,1)S(1)}, bf16[1024,128]{1,0:T(8,128)(2,1)S(1)}, u32[]{:S(2)}, u32[]{:S(2)}) collective-permute-start(bf16[1024,128]{1,0:T(8,128)(2,1)S(1)} %broadcast_select_fusion.own), channel_id=1, source_target_pairs={{0,1},{3,4},{1,2},{6,7},{8,9},{11,12},{9,10},{14,15},{16,17},{19,2... | collective-permute-start | bytes 786440 | tf_op jit(solution)/shard_map/ppermute | solution.py:343
  38.3 10.1 %collective-permute-start.4 = (bf16[1024,128]{1,0:T(8,128)(2,1)S(1)}, bf16[1024,128]{1,0:T(8,128)(2,1)S(1)}, u32[]{:S(2)}, u32[]{:S(2)}) collective-permute-start(bf16[1024,128]{1,0:T(8,128)(2,1)S(1)} %broadcast_select_fusion.own), channel_id=1, source_target_pairs={{0,7},{3,2},{1,0},{6,5},{8,15},{11,10},{9,8},{14,13},{16,23},{19,1... | collective-permute-start | bytes 786440 | tf_op jit(solution)/shard_map/ppermute | solution.py:343
  40.2 11.7 %collective-permute-start.5 = (bf16[1024,128]{1,0:T(8,128)(2,1)S(1)}, bf16[1024,128]{1,0:T(8,128)(2,1)S(1)}, u32[]{:S(2)}, u32[]{:S(2)}) collective-permute-start(bf16[1024,128]{1,0:T(8,128)(2,1)S(1)} %broadcast_select_fusion.own), channel_id=1, source_target_pairs={{0,6},{3,5},{1,3},{6,4},{8,14},{11,13},{9,11},{14,12},{16,22},{19,... | collective-permute-start | bytes 786440 | tf_op jit(solution)/shard_map/ppermute | solution.py:343

commit v4 on v3

--- a/solution.py
+++ b/solution.py
@@ -262,11 +262,64 @@
     return jnp.concatenate(out_r, 0), jnp.concatenate(out_i, 0)
 
 
+def wide_dot(x, y):
+    xh, xl = split(x)
+    yh, yl = split(y)
+    return dot(xh, yh) + (dot(xh, yl) + dot(xl, yh))
+
+
+def pair(re, im):
+    return jnp.concatenate([jnp.concatenate([re, im], 1), jnp.concatenate([-im, re], 1)], 0)
+
+
+def refine(tr, ti, root):
+    row = lax.broadcasted_iota(jnp.int32, (WIDE, WIDE), 0)
+    col = lax.broadcasted_iota(jnp.int32, (WIDE, WIDE), 1)
+    one = jnp.where(row == col, 1.0, 0.0)
+    weight = jnp.where(col < row, 1.0, 0.5 * one)
+    down = lax.rsqrt(jnp.sum(one * tr, axis=1, keepdims=True))
+    across = lax.rsqrt(jnp.sum(one * tr, axis=0, keepdims=True))
+    ar, ai = tr * down * across, ti * down * across
+    unit = pair(ar, ai)
+    root[:, :WIDE] = one - jnp.where(col < row, ar, 0.0)
+    root[:, WIDE:] = -jnp.where(col < row, ai, 0.0)
+
+    def cond(carry):
+        step, size = carry
+        return (step < 8) & (size > 1e-6) & (size < 1.0)
+
+    def step(carry):
+        count, _ = carry
+        r = root[...]
+        half = wide_dot(r, unit)
+        rt, it = jnp.transpose(r[:, :WIDE]), jnp.transpose(r[:, WIDE:])
+        e = wide_dot(half, pair(rt, -it))
+        er, ei = e[:, :WIDE] - one, e[:, WIDE:]
+        size = jnp.sum(er * er + ei * ei)
+        fix = jnp.concatenate([weight * er, weight * ei], 1)
+        root[...] = r - wide_dot(fix, pair(r[:, :WIDE], r[:, WIDE:]))
+        return count + 1, size
+
+    count, size = lax.while_loop(cond, step, (jnp.int32(0), jnp.float32(0.5)))
+    good = size <= 1e-6
+
+    @pl.when(good)
+    def _():
+        root[:, :WIDE] = root[:, :WIDE] * across
+        root[:, WIDE:] = root[:, WIDE:] * across
+
+    @pl.when(jnp.logical_not(good))
+    def _():
+        re, im = inverse_factor(tr, ti)
+        root[:, :WIDE] = re
+        root[:, WIDE:] = im
+
+
 def embed(block):
     return jnp.concatenate([block, times_i(block)], 0)
 
 
-def finish_kernel(pos, g, w, p01, out):
+def finish_kernel(pos, g, w, p01, out, root):
     row = lax.broadcasted_iota(jnp.int32, (HALF, WIDE), 0)
     lane = lax.broadcasted_iota(jnp.int32, (HALF, WIDE), 1)
     left = lane < HALF
@@ -283,7 +336,8 @@
     pivots = jnp.where(diag, c, 0.0)
     tr = once_r + jnp.transpose(once_r) + stack(pivots, 0.0, pivots)
     ti = once_i - jnp.transpose(once_i)
-    rr, ri = inverse_factor(tr, ti)
+    refine(tr, ti, root)
+    rr, ri = root[:, :WIDE], root[:, WIDE:]
     which = pos[0]
 
     @pl.when(which >= 2)
@@ -315,6 +369,7 @@
         out_shape=jax.ShapeDtypeStruct(w.shape, F32),
         in_specs=[pl.BlockSpec(memory_space=SM), spec, spec, spec],
         out_specs=spec,
+        scratch_shapes=[VM((WIDE, 2 * WIDE), F32)],
         compiler_params=pltpu.CompilerParams(vmem_limit_bytes=16 << 20),
         name="finish",
     )(pos, g, w, p01)

time: 104 us -> 105 us (level)
  no operation moved by 1% of the time
where the time goes in v4:
time: 105 us; the launch traced here: 104 us
  blocking collectives  38.1 us (36%)
  starting transfers between devices  26.8 us (26%)
  Pallas kernels  17.4 us (17%)
  waiting for transfers between devices  12.3 us (12%)
  local copies, waits for them, and re-layouts  6.83 us (7%)
  between operations  1.53 us (1%)
  other arithmetic  1.43 us (1%)
    all_to_all x2, blocking collectives, swap(): return lax.all_to_all(x, axes, 0, 0, tiled=True)  38.1 us
    pallas_call x1, Pallas kernels, finish(): pl.pallas_call(finish_kernel, out_shape=jax.ShapeDtypeStruct(w.shape, F32...  13.7 us
    ppermute x3, starting transfers between devices, spread(): lax.ppermute(own, 'panel', pairs)  12.5 us
    ppermute x3, waiting for transfers between devices, spread(): lax.ppermute(own, 'panel', pairs)  7.22 us
    ppermute x1, starting transfers between devices, body(): right = lax.ppermute(down, slab, [(i + 1, i) for i in range(count - 1)])  6.21 us
    unnamed x19, local copies, waits for them, and re-layouts  5.79 us
    ppermute x1, waiting for transfers between devices, spread(): far = lax.ppermute(w_hi, 'panel', [(0, 3), (1, 6)])  5.12 us
    ppermute x1, starting transfers between devices, body(): left = lax.ppermute(up, slab, [(i, i + 1) for i in range(count - 1)])  4.5 us
  transfers between devices with their start and end apart: 6, of which 3 were waited for; matrix products, arithmetic and copies ran while one was open for 3% of the time, Pallas kernels for 0%

profile of v4, /device:TPU:1, one launch (start us, length us, event | category | flops | bytes accessed | tf_op | source)
XLA Modules:
  0.0 104.4 jit_solution(11279896968357818375)
XLA Ops:
  0.0 0.0 copy-start.3
  0.0 1.0 copy-done.3
  1.0 0.0 copy-start.5
  1.0 0.7 copy-done.5
  1.7 0.0 copy-start.7
  1.7 0.7 copy-done.7
  2.4 0.7 pack.1
  3.1 4.5 %collective-permute-start = (bf16[528,128]{1,0:T(8,128)(2,1)}, bf16[528,128]{1,0:T(8,128)(2,1)}, u32[]{:S(2)}, u32[]{:S(2)}) collective-permute-start(bf16[528,128]{1,0:T(8,128)(2,1)} %get-tuple-element.11), channel_id=1, source_target_pairs={{0,8},{8,16},{16,24},{24,32},{32,40},{40,48},{48,56},{56,64},{64,7... | collective-permute-start | bytes 405512 | tf_op jit(solution)/shard_map/ppermute | solution.py:412
  7.6 6.2 %collective-permute-start.1 = (bf16[528,128]{1,0:T(8,128)(2,1)S(1)}, bf16[528,128]{1,0:T(8,128)(2,1)}, u32[]{:S(2)}, u32[]{:S(2)}) collective-permute-start(bf16[528,128]{1,0:T(8,128)(2,1)S(1)} %get-tuple-element.12), channel_id=1, source_target_pairs={{8,0},{16,8},{24,16},{32,24},{40,32},{48,40},{56,48},{64,56},{72,6... | collective-permute-start | bytes 405512 | tf_op jit(solution)/shard_map/ppermute | solution.py:413
  13.8 0.8 fusion.2
  14.6 0.0 copy-start
  14.6 1.6 %copy.11 = bf16[8,256,256]{1,2,0:T(8,128)(2,1)S(1)} copy(bf16[8,256,256]{2,1,0:T(8,128)(2,1)} %hop.1) | data formatting | bytes 2097152 | tf_op args[1]
  16.2 0.0 copy-done
  16.2 0.0 copy-start.6
  16.2 0.0 copy-start.8
  16.2 0.3 multiply_convert_fusion.sym
  16.6 0.1 copy.12
  16.7 0.1 copy.13
  18.1 0.0 collective-permute-done
  18.1 0.0 collective-permute-done.1
  18.1 1.0 pad_maximum_fusion.sides
  19.1 0.0 copy-done.6
  19.1 0.0 copy-done.8
  19.1 0.0 copy-start.4
  19.2 1.0 copy-done.4
  20.2 2.3 %chebyshev.1 = (f32[1024,128]{1,0:T(8,128)S(1)}, bf16[1024,128]{1,0:T(8,128)(2,1)S(1)}) custom-call(s32[2,4]{1,0:T(2,128)S(1)} %bitcast.15, s32[1,4]{1,0:T(1,128)S(1)} %bitcast.17, f32[1]{0:T(128)S(6)} %copy.14.shift, f32[1]{0:T(128)S(6)} %copy.15.width, f32[1024,128]{1,0:T(8,128)S(1)} %copy-done.4, bf16[1056,128]{1,0:T(8,128)(2,1)S(1)} %pad_maximum_fusion.sides, ...), custom_call_target="tpu_custom_call" | custom-call | tf_op jit(solution)/shard_map/chebyshev/pallas_call | solution.py:163
  22.5 0.0 copy-start.1
  22.5 0.8 copy-done.1
  23.3 0.0 copy-start.2
  23.3 3.6 %collective-permute-start.2 = (bf16[1024,128]{1,0:T(8,128)(2,1)S(1)}, bf16[1024,128]{1,0:T(8,128)(2,1)S(1)}, u32[]{:S(2)}, u32[]{:S(2)}) collective-permute-start(bf16[1024,128]{1,0:T(8,128)(2,1)S(1)} %get-tuple-element.14), channel_id=1, source_target_pairs={{0,3},{1,6},{8,11},{9,14},{16,19},{17,22},{24,27},{25,30},{32,35},... | collective-permute-start | bytes 786440 | tf_op jit(solution)/shard_map/ppermute | solution.py:396
  27.0 5.1 %collective-permute-done.2 = bf16[1024,128]{1,0:T(8,128)(2,1)S(1)} collective-permute-done((bf16[1024,128]{1,0:T(8,128)(2,1)S(1)}, bf16[1024,128]{1,0:T(8,128)(2,1)S(1)}, u32[]{:S(2)}, u32[]{:S(2)}) %collective-permute-start.2) | collective-permute-done | bytes 262176 | tf_op jit(solution)/shard_map/ppermute | solution.py:396
  32.1 6.1 %collective-permute-start.3 = (bf16[1024,128]{1,0:T(8,128)(2,1)S(1)}, bf16[1024,128]{1,0:T(8,128)(2,1)S(1)}, u32[]{:S(2)}, u32[]{:S(2)}) collective-permute-start(bf16[1024,128]{1,0:T(8,128)(2,1)S(1)} %broadcast_select_fusion.own), channel_id=1, source_target_pairs={{0,1},{3,4},{1,2},{6,7},{8,9},{11,12},{9,10},{14,15},{16,17},{19,2... | collective-permute-start | bytes 786440 | tf_op jit(solution)/shard_map/ppermute | solution.py:398
  38.3 1.9 %collective-permute-start.4 = (bf16[1024,128]{1,0:T(8,128)(2,1)S(1)}, bf16[1024,128]{1,0:T(8,128)(2,1)S(1)}, u32[]{:S(2)}, u32[]{:S(2)}) collective-permute-start(bf16[1024,128]{1,0:T(8,128)(2,1)S(1)} %broadcast_select_fusion.own), channel_id=1, source_target_pairs={{0,7},{3,2},{1,0},{6,5},{8,15},{11,10},{9,8},{14,13},{16,23},{19,1... | collective-permute-start | bytes 786440 | tf_op jit(solution)/shard_map/ppermute | solution.py:398
  40.2 4.4 %collective-permute-start.5 = (bf16[1024,128]{1,0:T(8,128)(2,1)S(1)}, bf16[1024,128]{1,0:T(8,128)(2,1)S(1)}, u32[]{:S(2)}, u32[]{:S(2)}) collective-permute-start(bf16[1024,128]{1,0:T(8,128)(2,1)S(1)} %broadcast_select_fusion.own), channel_id=1, source_target_pairs={{0,6},{3,5},{1,3},{6,4},{8,14},{11,13},{9,11},{14,12},{16,22},{19,... | collective-permute-start | bytes 786440 | tf_op jit(solution)/shard_map/ppermute | solution.py:398
  44.6 0.0 collective-permute-done.3.first
  44.6 3.7 %collective-permute-done.4.second = bf16[1024,128]{1,0:T(8,128)(2,1)S(1)} collective-permute-done((bf16[1024,128]{1,0:T(8,128)(2,1)S(1)}, bf16[1024,128]{1,0:T(8,128)(2,1)S(1)}, u32[]{:S(2)}, u32[]{:S(2)}) %collective-permute-start.4) | collective-permute-done | bytes 262176 | tf_op jit(solution)/shard_map/ppermute | solution.py:398
  48.3 3.5 %collective-permute-done.5.third = bf16[1024,128]{1,0:T(8,128)(2,1)S(1)} collective-permute-done((bf16[1024,128]{1,0:T(8,128)(2,1)S(1)}, bf16[1024,128]{1,0:T(8,128)(2,1)S(1)}, u32[]{:S(2)}, u32[]{:S(2)}) %collective-permute-start.5) | collective-permute-done | bytes 262176 | tf_op jit(solution)/shard_map/ppermute | solution.py:398
  51.9 0.0 copy-done.2
  51.9 0.7 gram.1
  52.6 23.1 %all_to_all.17 = f32[64,4,128]{2,1,0:T(4,128)S(1)} all-to-all(f32[64,4,128]{2,1,0:T(4,128)S(1)} %bitcast.13), channel_id=1, replica_groups=mesh['y'=8,'x'=4,'core'=2,'panel'=8] {'y','x','core'}, dimensions={0} | all-to-all | bytes 262144 | tf_op jit(solution)/shard_map/all_to_all | solution.py:379
  75.7 0.1 reduce_sum.9
  75.8 14.9 %all_to_all.18 = f32[64,4,128]{2,1,0:T(4,128)S(1)} all-to-all(f32[64,4,128]{2,1,0:T(4,128)S(1)} %broadcast_in_dim.10), channel_id=1, replica_groups=mesh['y'=8,'x'=4,'core'=2,'panel'=8] {'y','x','core'}, dimensions={0} | all-to-all | bytes 262144 | tf_op jit(solution)/shard_map/all_to_all | solution.py:379
  90.8 13.7 %finish.1 = f32[1024,128]{1,0:T(8,128)} custom-call(s32[1]{0:T(128)} %bitcast.pos, f32[256,128]{1,0:T(8,128)S(1)} %bitcast.10, f32[1024,128]{1,0:T(8,128)S(1)} %copy-done.2, bf16[1024,256]{1,0:T(8,128)(2,1)S(1)} %get-tuple-element.16.p01), custom_call_target="tpu_custom_call" | custom-call | tf_op jit(solution)/shard_map/finish/pallas_call | solution.py:367
  (5 shorter events, 0.1 us)
Async XLA Ops:
  0.0 1.0 copy-start.3
  1.0 0.7 copy-start.5
  1.7 0.7 copy-start.7
  3.1 15.0 %collective-permute-start = (bf16[528,128]{1,0:T(8,128)(2,1)}, bf16[528,128]{1,0:T(8,128)(2,1)}, u32[]{:S(2)}, u32[]{:S(2)}) collective-permute-start(bf16[528,128]{1,0:T(8,128)(2,1)} %get-tuple-element.11), channel_id=1, source_target_pairs={{0,8},{8,16},{16,24},{24,32},{32,40},{40,48},{48,56},{56,64},{64,7... | collective-permute-start | bytes 405512 | tf_op jit(solution)/shard_map/ppermute | solution.py:412
  7.6 10.5 %collective-permute-start.1 = (bf16[528,128]{1,0:T(8,128)(2,1)S(1)}, bf16[528,128]{1,0:T(8,128)(2,1)}, u32[]{:S(2)}, u32[]{:S(2)}) collective-permute-start(bf16[528,128]{1,0:T(8,128)(2,1)S(1)} %get-tuple-element.12), channel_id=1, source_target_pairs={{8,0},{16,8},{24,16},{32,24},{40,32},{48,40},{56,48},{64,56},{72,6... | collective-permute-start | bytes 405512 | tf_op jit(solution)/shard_map/ppermute | solution.py:413
  14.6 1.6 %copy-start = (bf16[8,256,256]{2,1,0:T(8,128)(2,1)S(1)}, bf16[8,256,256]{2,1,0:T(8,128)(2,1)}, u32[]{:S(2)}) copy-start(bf16[8,256,256]{2,1,0:T(8,128)(2,1)} %hop.1) | copy-start | bytes 3145732
  16.2 2.9 %copy-start.6 = (s32[4,2]{0,1:T(2,128)S(1)}, s32[4,2]{0,1:T(2,128)}, u32[]{:S(2)}) copy-start(s32[4,2]{0,1:T(2,128)} %param.9) | copy-start | bytes 100
  16.2 2.9 %copy-start.8 = (s32[4]{0:T(128)S(1)}, s32[4]{0:T(128)}, u32[]{:S(2)}) copy-start(s32[4]{0:T(128)} %param.10) | copy-start | bytes 52
  19.1 1.0 %copy-start.4 = (f32[1024,128]{1,0:T(8,128)S(1)}, f32[1024,128]{1,0:T(8,128)}, u32[]{:S(2)}) copy-start(f32[1024,128]{1,0:T(8,128)} %v.3) | copy-start | bytes 1572868
  22.5 0.8 copy-start.1
  23.3 28.5 %copy-start.2 = (f32[1024,128]{1,0:T(8,128)S(1)}, f32[1024,128]{1,0:T(8,128)}, u32[]{:S(2)}) copy-start(f32[1024,128]{1,0:T(8,128)} %copy-done.1) | copy-start | bytes 1572868
  23.3 8.8 %collective-permute-start.2 = (bf16[1024,128]{1,0:T(8,128)(2,1)S(1)}, bf16[1024,128]{1,0:T(8,128)(2,1)S(1)}, u32[]{:S(2)}, u32[]{:S(2)}) collective-permute-start(bf16[1024,128]{1,0:T(8,128)(2,1)S(1)} %get-tuple-element.14), channel_id=1, source_target_pairs={{0,3},{1,6},{8,11},{9,14},{16,19},{17,22},{24,27},{25,30},{32,35},... | collective-permute-start | bytes 786440 | tf_op jit(solution)/shard_map/ppermute | solution.py:396
  32.1 12.5 %collective-permute-start.3 = (bf16[1024,128]{1,0:T(8,128)(2,1)S(1)}, bf16[1024,128]{1,0:T(8,128)(2,1)S(1)}, u32[]{:S(2)}, u32[]{:S(2)}) collective-permute-start(bf16[1024,128]{1,0:T(8,128)(2,1)S(1)} %broadcast_select_fusion.own), channel_id=1, source_target_pairs={{0,1},{3,4},{1,2},{6,7},{8,9},{11,12},{9,10},{14,15},{16,17},{19,2... | collective-permute-start | bytes 786440 | tf_op jit(solution)/shard_map/ppermute | solution.py:398
  38.3 10.1 %collective-permute-start.4 = (bf16[1024,128]{1,0:T(8,128)(2,1)S(1)}, bf16[1024,128]{1,0:T(8,128)(2,1)S(1)}, u32[]{:S(2)}, u32[]{:S(2)}) collective-permute-start(bf16[1024,128]{1,0:T(8,128)(2,1)S(1)} %broadcast_select_fusion.own), channel_id=1, source_target_pairs={{0,7},{3,2},{1,0},{6,5},{8,15},{11,10},{9,8},{14,13},{16,23},{19,1... | collective-permute-start | bytes 786440 | tf_op jit(solution)/shard_map/ppermute | solution.py:398
  40.2 11.7 %collective-permute-start.5 = (bf16[1024,128]{1,0:T(8,128)(2,1)S(1)}, bf16[1024,128]{1,0:T(8,128)(2,1)S(1)}, u32[]{:S(2)}, u32[]{:S(2)}) collective-permute-start(bf16[1024,128]{1,0:T(8,128)(2,1)S(1)} %broadcast_select_fusion.own), channel_id=1, source_target_pairs={{0,6},{3,5},{1,3},{6,4},{8,14},{11,13},{9,11},{14,12},{16,22},{19,... | collective-permute-start | bytes 786440 | tf_op jit(solution)/shard_map/ppermute | solution.py:398

commit v5 on v4

--- a/solution.py
+++ b/solution.py
@@ -70,19 +70,19 @@
         in_specs=[spec] * 3,
         out_specs=(spec, spec),
         scratch_shapes=[VM((META, WIDE), F32)],
-        compiler_params=pltpu.CompilerParams(vmem_limit_bytes=16 << 20),
         name="pack",
     )(v, kinds, phase)
 
 
 def filter_kernel(
-    kinds, phase, shift, width, v, sides, hop, hop_t, sym, cos_t, sin_t,
-    w, w_hi, cosb, sinb, z, y1, y1b,
+    kinds, phase, shift, width, base, sides, hop, hop_t, sym, cos_t, sin_t,
+    w, w_hi, vb, cosb, sinb, z, y1, y1b,
 ):
-    half = v.shape[0] // 2
+    half = base.shape[0] // 2
     left, right = sides.at[0 : half + META], sides.at[half + META :]
     centre = shift[0]
-    inv_h = 1.0 / jnp.broadcast_to(width[0], (1, WIDE))
+    h = jnp.broadcast_to(width[0], (1, WIDE))
+    inv_h = 1.0 / h
     pick = lax.broadcasted_iota(jnp.int32, (cos_t.shape[1], WIDE), 0) % 16
     tile_l = left[half : half + META, :].astype(F32)
     tile_r = right[half : half + META, :].astype(F32)
@@ -121,7 +121,7 @@
             return left[(r + 2) * BLK : (r + 3) * BLK, :]
         if r > 3:
             return right[(r - 4) * BLK : (r - 3) * BLK, :]
-        return v[r * BLK : (r + 1) * BLK, :].astype(BF16)
+        return vb[r * BLK : (r + 1) * BLK, :]
 
     def y_row(r):
         return y1b[r + 1]
@@ -137,11 +137,12 @@
         total += cosb[r + 2] * ahead + sinb[r + 2] * times_i(ahead)
         return total + flag(kb) * dot(hop_t[jnp.minimum(kb, 7)], z[r + 1])
 
+    vb[...] = (h * base[...]).astype(BF16)
     for r in range(-2, 4):
         z[r + 2] = back_phase(v_row(r), r)
     for r in range(-1, 5):
-        vr = v[r * BLK : (r + 1) * BLK, :] if 0 <= r < 4 else v_row(r).astype(F32)
-        y = (hop_row(r, v_row) - centre * vr) * inv_h
+        scaled = base[r * BLK : (r + 1) * BLK, :] if 0 <= r < 4 else v_row(r).astype(F32) * inv_h
+        y = hop_row(r, v_row) * inv_h - centre * scaled
         if r == -1:
             y = y * has_left
         if r == 4:
@@ -152,7 +153,7 @@
     for r in range(-1, 4):
         z[r + 2] = back_phase(y_row(r), r)
     for r in range(4):
-        y = (2.0 * inv_h) * (hop_row(r, y_row) - centre * y1[r]) - v[r * BLK : (r + 1) * BLK, :]
+        y = (2.0 * inv_h) * (hop_row(r, y_row) - centre * y1[r]) - h * base[r * BLK : (r + 1) * BLK, :]
         w[r * BLK : (r + 1) * BLK, :] = y
         w_hi[r * BLK : (r + 1) * BLK, :] = y.astype(BF16)
 
@@ -166,6 +167,7 @@
         in_specs=[smem] * 4 + [spec] * 7,
         out_specs=(spec, spec),
         scratch_shapes=[
+            VM(args[4].shape, BF16),
             VM((7, BLK, WIDE), F32),
             VM((7, BLK, WIDE), F32),
             VM((6, BLK, WIDE), BF16),
@@ -411,6 +413,7 @@
     up, down = pack(vectors, kinds, phase)
     left = lax.ppermute(up, slab, [(i, i + 1) for i in range(count - 1)])
     right = lax.ppermute(down, slab, [(i + 1, i) for i in range(count - 1)])
+    base = vectors / half_width[0]
     sides = jnp.concatenate([left, right], axis=0)
     wide = hop_table.astype(F32)
     turned = jnp.transpose(hop_table, (0, 2, 1))
@@ -418,7 +421,7 @@
     cos_t = thirds(jnp.cos(phase_angles))
     sin_t = thirds(jnp.sin(phase_angles))
     w, w_hi = chebyshev(
-        kinds, phase, centre, half_width, vectors, sides, hop_table, turned, sym, cos_t, sin_t
+        kinds, phase, centre, half_width, base, sides, hop_table, turned, sym, cos_t, sin_t
     )
     pos = lax.axis_index("panel").astype(jnp.int32)
     spot = pos.reshape(1)

time: 105 us -> 101 us (0.962)
  local copies, waits for them, and re-layouts: 6.83 us -> 2.64 us
  waiting for transfers between devices: 12.3 us -> 10.9 us
  blocking collectives: 38.1 us -> 39.4 us
  Pallas kernels: 17.4 us -> 18.6 us
    unnamed x19 -> x9, local copies, waits for them, and re-layouts: 5.79 us -> 1.59 us
    all_to_all x2, blocking collectives: 38.1 us -> 39.4 us  [swap(): return lax.all_to_all(x, axes, 0, 0, tiled=True)]
    pallas_call x1, Pallas kernels: 0.69 us -> 1.8 us  [pack(): pl.pallas_call(pack_kernel, out_shape=(shape, shape), in_specs=[spec] * 3...]
where the time goes in v5:
time: 101 us; the launch traced here: 100 us
  blocking collectives  39.4 us (39%)
  starting transfers between devices  26.7 us (26%)
  Pallas kernels  18.6 us (18%)
  waiting for transfers between devices  10.9 us (11%)
  local copies, waits for them, and re-layouts  2.64 us (3%)
  between operations  1.54 us (2%)
    all_to_all x2, blocking collectives, swap(): return lax.all_to_all(x, axes, 0, 0, tiled=True)  39.4 us
    pallas_call x1, Pallas kernels, finish(): pl.pallas_call(finish_kernel, out_shape=jax.ShapeDtypeStruct(w.shape, F32...  13.7 us
    ppermute x3, starting transfers between devices, spread(): lax.ppermute(own, 'panel', pairs)  12.5 us
    ppermute x3, waiting for transfers between devices, spread(): lax.ppermute(own, 'panel', pairs)  6.46 us
    ppermute x1, starting transfers between devices, body(): right = lax.ppermute(down, slab, [(i + 1, i) for i in range(count - 1)])  5.57 us
    ppermute x1, starting transfers between devices, body(): left = lax.ppermute(up, slab, [(i, i + 1) for i in range(count - 1)])  4.5 us
    ppermute x1, waiting for transfers between devices, spread(): far = lax.ppermute(w_hi, 'panel', [(0, 3), (1, 6)])  4.45 us
    ppermute x1, starting transfers between devices, spread(): far = lax.ppermute(w_hi, 'panel', [(0, 3), (1, 6)])  4.17 us
  transfers between devices with their start and end apart: 6, of which 3 were waited for; matrix products, arithmetic and copies ran while one was open for 3% of the time, Pallas kernels for 0%

profile of v5, /device:TPU:1, one launch (start us, length us, event | category | flops | bytes accessed | tf_op | source)
XLA Modules:
  0.0 100.4 jit_solution(16368170787490560533)
XLA Ops:
  0.0 1.8 %pack.1 = (bf16[528,128]{1,0:T(8,128)(2,1)}, bf16[528,128]{1,0:T(8,128)(2,1)}) custom-call(f32[1024,128]{1,0:T(8,128)} %v.1, s32[2,4]{1,0:T(2,128)} %bitcast.16, s32[1,4]{1,0:T(1,128)} %bitcast.18), custom_call_target="tpu_custom_call" | custom-call | tf_op jit(solution)/shard_map/pack/pallas_call | solution.py:67
  1.8 4.5 %collective-permute-start = (bf16[528,128]{1,0:T(8,128)(2,1)}, bf16[528,128]{1,0:T(8,128)(2,1)S(1)}, u32[]{:S(2)}, u32[]{:S(2)}) collective-permute-start(bf16[528,128]{1,0:T(8,128)(2,1)} %get-tuple-element.11), channel_id=1, source_target_pairs={{0,8},{8,16},{16,24},{24,32},{32,40},{40,48},{48,56},{56,64},{64,7... | collective-permute-start | bytes 405512 | tf_op jit(solution)/shard_map/ppermute | solution.py:414
  6.3 5.6 %collective-permute-start.1 = (bf16[528,128]{1,0:T(8,128)(2,1)}, bf16[528,128]{1,0:T(8,128)(2,1)S(1)}, u32[]{:S(2)}, u32[]{:S(2)}) collective-permute-start(bf16[528,128]{1,0:T(8,128)(2,1)} %get-tuple-element.12), channel_id=1, source_target_pairs={{8,0},{16,8},{24,16},{32,24},{40,32},{48,40},{56,48},{64,56},{72,6... | collective-permute-start | bytes 405512 | tf_op jit(solution)/shard_map/ppermute | solution.py:415
  11.9 0.8 fusion.2
  12.7 0.1 copy.12
  12.8 0.1 copy.13
  13.0 0.0 copy-start
  13.0 1.6 %copy.11 = bf16[8,256,256]{1,2,0:T(8,128)(2,1)S(1)} copy(bf16[8,256,256]{2,1,0:T(8,128)(2,1)} %hop.1) | data formatting | bytes 2097152 | tf_op args[1]
  14.5 0.0 copy-done
  14.6 0.0 copy-start.3
  14.6 0.3 multiply_convert_fusion.sym
  14.9 0.0 copy-start.1
  14.9 0.0 copy-start.2
  16.2 0.0 copy-done.3
  16.3 0.0 collective-permute-done
  16.3 0.0 collective-permute-done.1
  16.3 0.0 copy-done.1
  16.3 0.0 copy-done.2
  16.3 2.4 %chebyshev.1 = (f32[1024,128]{1,0:T(8,128)S(1)}, bf16[1024,128]{1,0:T(8,128)(2,1)S(1)}) custom-call(s32[2,4]{1,0:T(2,128)S(1)} %bitcast.17, s32[1,4]{1,0:T(1,128)S(1)} %bitcast.19, f32[1]{0:T(128)S(6)} %copy.14.shift, f32[1]{0:T(128)} %copy.15.width, f32[1024,128]{1,0:T(8,128)S(1)} %broadcast_divide_fusion.base, ...), custom_call_target="tpu_custom_call" | custom-call | tf_op jit(solution)/shard_map/chebyshev/pallas_call | solution.py:164
  18.8 4.2 %collective-permute-start.2 = (bf16[1024,128]{1,0:T(8,128)(2,1)S(1)}, bf16[1024,128]{1,0:T(8,128)(2,1)S(1)}, u32[]{:S(2)}, u32[]{:S(2)}) collective-permute-start(bf16[1024,128]{1,0:T(8,128)(2,1)S(1)} %get-tuple-element.14), channel_id=1, source_target_pairs={{0,3},{1,6},{8,11},{9,14},{16,19},{17,22},{24,27},{25,30},{32,35},... | collective-permute-start | bytes 786440 | tf_op jit(solution)/shard_map/ppermute | solution.py:398
  23.0 4.5 %collective-permute-done.2 = bf16[1024,128]{1,0:T(8,128)(2,1)S(1)} collective-permute-done((bf16[1024,128]{1,0:T(8,128)(2,1)S(1)}, bf16[1024,128]{1,0:T(8,128)(2,1)S(1)}, u32[]{:S(2)}, u32[]{:S(2)}) %collective-permute-start.2) | collective-permute-done | bytes 262176 | tf_op jit(solution)/shard_map/ppermute | solution.py:398
  27.5 6.2 %collective-permute-start.3 = (bf16[1024,128]{1,0:T(8,128)(2,1)S(1)}, bf16[1024,128]{1,0:T(8,128)(2,1)S(1)}, u32[]{:S(2)}, u32[]{:S(2)}) collective-permute-start(bf16[1024,128]{1,0:T(8,128)(2,1)S(1)} %broadcast_select_fusion.own), channel_id=1, source_target_pairs={{0,1},{3,4},{1,2},{6,7},{8,9},{11,12},{9,10},{14,15},{16,17},{19,2... | collective-permute-start | bytes 786440 | tf_op jit(solution)/shard_map/ppermute | solution.py:400
  33.6 1.9 %collective-permute-start.4 = (bf16[1024,128]{1,0:T(8,128)(2,1)S(1)}, bf16[1024,128]{1,0:T(8,128)(2,1)S(1)}, u32[]{:S(2)}, u32[]{:S(2)}) collective-permute-start(bf16[1024,128]{1,0:T(8,128)(2,1)S(1)} %broadcast_select_fusion.own), channel_id=1, source_target_pairs={{0,7},{3,2},{1,0},{6,5},{8,15},{11,10},{9,8},{14,13},{16,23},{19,1... | collective-permute-start | bytes 786440 | tf_op jit(solution)/shard_map/ppermute | solution.py:400
  35.5 4.4 %collective-permute-start.5 = (bf16[1024,128]{1,0:T(8,128)(2,1)S(1)}, bf16[1024,128]{1,0:T(8,128)(2,1)S(1)}, u32[]{:S(2)}, u32[]{:S(2)}) collective-permute-start(bf16[1024,128]{1,0:T(8,128)(2,1)S(1)} %broadcast_select_fusion.own), channel_id=1, source_target_pairs={{0,6},{3,5},{1,3},{6,4},{8,14},{11,13},{9,11},{14,12},{16,22},{19,... | collective-permute-start | bytes 786440 | tf_op jit(solution)/shard_map/ppermute | solution.py:400
  40.0 0.0 collective-permute-done.3.first
  40.0 3.0 %collective-permute-done.4.second = bf16[1024,128]{1,0:T(8,128)(2,1)S(1)} collective-permute-done((bf16[1024,128]{1,0:T(8,128)(2,1)S(1)}, bf16[1024,128]{1,0:T(8,128)(2,1)S(1)}, u32[]{:S(2)}, u32[]{:S(2)}) %collective-permute-start.4) | collective-permute-done | bytes 262176 | tf_op jit(solution)/shard_map/ppermute | solution.py:400
  43.0 3.4 %collective-permute-done.5.third = bf16[1024,128]{1,0:T(8,128)(2,1)S(1)} collective-permute-done((bf16[1024,128]{1,0:T(8,128)(2,1)S(1)}, bf16[1024,128]{1,0:T(8,128)(2,1)S(1)}, u32[]{:S(2)}, u32[]{:S(2)}) %collective-permute-start.5) | collective-permute-done | bytes 262176 | tf_op jit(solution)/shard_map/ppermute | solution.py:400
  46.4 0.7 gram.1
  47.2 24.5 %all_to_all.17 = f32[64,4,128]{2,1,0:T(4,128)S(1)} all-to-all(f32[64,4,128]{2,1,0:T(4,128)S(1)} %bitcast.15), channel_id=1, replica_groups=mesh['y'=8,'x'=4,'core'=2,'panel'=8] {'y','x','core'}, dimensions={0} | all-to-all | bytes 262144 | tf_op jit(solution)/shard_map/all_to_all | solution.py:381
  71.7 0.1 reduce_sum.9
  71.8 14.9 %all_to_all.18 = f32[64,4,128]{2,1,0:T(4,128)S(1)} all-to-all(f32[64,4,128]{2,1,0:T(4,128)S(1)} %broadcast_in_dim.10), channel_id=1, replica_groups=mesh['y'=8,'x'=4,'core'=2,'panel'=8] {'y','x','core'}, dimensions={0} | all-to-all | bytes 262144 | tf_op jit(solution)/shard_map/all_to_all | solution.py:381
  86.7 13.7 %finish.1 = f32[1024,128]{1,0:T(8,128)} custom-call(s32[1]{0:T(128)} %bitcast.pos, f32[256,128]{1,0:T(8,128)S(1)} %bitcast.12, f32[1024,128]{1,0:T(8,128)S(1)} %get-tuple-element.13.w, bf16[1024,256]{1,0:T(8,128)(2,1)S(1)} %get-tuple-element.16.p01), custom_call_target="tpu_custom_call" | custom-call | tf_op jit(solution)/shard_map/finish/pallas_call | solution.py:369
  (7 shorter events, 0.1 us)
Async XLA Ops:
  1.8 14.5 %collective-permute-start = (bf16[528,128]{1,0:T(8,128)(2,1)}, bf16[528,128]{1,0:T(8,128)(2,1)S(1)}, u32[]{:S(2)}, u32[]{:S(2)}) collective-permute-start(bf16[528,128]{1,0:T(8,128)(2,1)} %get-tuple-element.11), channel_id=1, source_target_pairs={{0,8},{8,16},{16,24},{24,32},{32,40},{40,48},{48,56},{56,64},{64,7... | collective-permute-start | bytes 405512 | tf_op jit(solution)/shard_map/ppermute | solution.py:414
  6.3 10.0 %collective-permute-start.1 = (bf16[528,128]{1,0:T(8,128)(2,1)}, bf16[528,128]{1,0:T(8,128)(2,1)S(1)}, u32[]{:S(2)}, u32[]{:S(2)}) collective-permute-start(bf16[528,128]{1,0:T(8,128)(2,1)} %get-tuple-element.12), channel_id=1, source_target_pairs={{8,0},{16,8},{24,16},{32,24},{40,32},{48,40},{56,48},{64,56},{72,6... | collective-permute-start | bytes 405512 | tf_op jit(solution)/shard_map/ppermute | solution.py:415
  13.0 1.6 %copy-start = (bf16[8,256,256]{2,1,0:T(8,128)(2,1)S(1)}, bf16[8,256,256]{2,1,0:T(8,128)(2,1)}, u32[]{:S(2)}) copy-start(bf16[8,256,256]{2,1,0:T(8,128)(2,1)} %hop.1) | copy-start | bytes 3145732
  14.6 1.7 %copy-start.3 = (f32[1024,128]{1,0:T(8,128)S(1)}, f32[1024,128]{1,0:T(8,128)}, u32[]{:S(2)}) copy-start(f32[1024,128]{1,0:T(8,128)} %v.1) | copy-start | bytes 1572868
  14.9 1.4 %copy-start.1 = (s32[4,2]{0,1:T(2,128)S(1)}, s32[4,2]{0,1:T(2,128)}, u32[]{:S(2)}) copy-start(s32[4,2]{0,1:T(2,128)} %param.9) | copy-start | bytes 100
  14.9 1.4 %copy-start.2 = (s32[4]{0:T(128)S(1)}, s32[4]{0:T(128)}, u32[]{:S(2)}) copy-start(s32[4]{0:T(128)} %param.10) | copy-start | bytes 52
  18.8 8.6 %collective-permute-start.2 = (bf16[1024,128]{1,0:T(8,128)(2,1)S(1)}, bf16[1024,128]{1,0:T(8,128)(2,1)S(1)}, u32[]{:S(2)}, u32[]{:S(2)}) collective-permute-start(bf16[1024,128]{1,0:T(8,128)(2,1)S(1)} %get-tuple-element.14), channel_id=1, source_target_pairs={{0,3},{1,6},{8,11},{9,14},{16,19},{17,22},{24,27},{25,30},{32,35},... | collective-permute-start | bytes 786440 | tf_op jit(solution)/shard_map/ppermute | solution.py:398
  27.5 12.5 %collective-permute-start.3 = (bf16[1024,128]{1,0:T(8,128)(2,1)S(1)}, bf16[1024,128]{1,0:T(8,128)(2,1)S(1)}, u32[]{:S(2)}, u32[]{:S(2)}) collective-permute-start(bf16[1024,128]{1,0:T(8,128)(2,1)S(1)} %broadcast_select_fusion.own), channel_id=1, source_target_pairs={{0,1},{3,4},{1,2},{6,7},{8,9},{11,12},{9,10},{14,15},{16,17},{19,2... | collective-permute-start | bytes 786440 | tf_op jit(solution)/shard_map/ppermute | solution.py:400
  33.6 9.4 %collective-permute-start.4 = (bf16[1024,128]{1,0:T(8,128)(2,1)S(1)}, bf16[1024,128]{1,0:T(8,128)(2,1)S(1)}, u32[]{:S(2)}, u32[]{:S(2)}) collective-permute-start(bf16[1024,128]{1,0:T(8,128)(2,1)S(1)} %broadcast_select_fusion.own), channel_id=1, source_target_pairs={{0,7},{3,2},{1,0},{6,5},{8,15},{11,10},{9,8},{14,13},{16,23},{19,1... | collective-permute-start | bytes 786440 | tf_op jit(solution)/shard_map/ppermute | solution.py:400
  35.5 10.9 %collective-permute-start.5 = (bf16[1024,128]{1,0:T(8,128)(2,1)S(1)}, bf16[1024,128]{1,0:T(8,128)(2,1)S(1)}, u32[]{:S(2)}, u32[]{:S(2)}) collective-permute-start(bf16[1024,128]{1,0:T(8,128)(2,1)S(1)} %broadcast_select_fusion.own), channel_id=1, source_target_pairs={{0,6},{3,5},{1,3},{6,4},{8,14},{11,13},{9,11},{14,12},{16,22},{19,... | collective-permute-start | bytes 786440 | tf_op jit(solution)/shard_map/ppermute | solution.py:400

commit v6 on v5

--- a/solution.py
+++ b/solution.py
@@ -265,8 +265,11 @@
 
 
 def wide_dot(x, y):
-    xh, xl = split(x)
-    yh, yl = split(y)
+    return split_dot(split(x), split(y))
+
+
+def split_dot(x, y):
+    (xh, xl), (yh, yl) = x, y
     return dot(xh, yh) + (dot(xh, yl) + dot(xl, yh))
 
 
@@ -282,18 +285,18 @@
     down = lax.rsqrt(jnp.sum(one * tr, axis=1, keepdims=True))
     across = lax.rsqrt(jnp.sum(one * tr, axis=0, keepdims=True))
     ar, ai = tr * down * across, ti * down * across
-    unit = pair(ar, ai)
+    unit = split(pair(ar, ai))
     root[:, :WIDE] = one - jnp.where(col < row, ar, 0.0)
     root[:, WIDE:] = -jnp.where(col < row, ai, 0.0)
 
     def cond(carry):
         step, size = carry
-        return (step < 8) & (size > 1e-6) & (size < 1.0)
+        return (step < 8) & (size > 1e-5) & (size < 1.0)
 
     def step(carry):
         count, _ = carry
         r = root[...]
-        half = wide_dot(r, unit)
+        half = split_dot(split(r), unit)
         rt, it = jnp.transpose(r[:, :WIDE]), jnp.transpose(r[:, WIDE:])
         e = wide_dot(half, pair(rt, -it))
         er, ei = e[:, :WIDE] - one, e[:, WIDE:]
@@ -303,7 +306,7 @@
         return count + 1, size
 
     count, size = lax.while_loop(cond, step, (jnp.int32(0), jnp.float32(0.5)))
-    good = size <= 1e-6
+    good = size <= 1e-5
 
     @pl.when(good)
     def _():
@@ -345,8 +348,8 @@
     @pl.when(which >= 2)
     def _():
         m = g[2 * HALF : 4 * HALF, :]
-        n = dot(rr, m, precision=HIGHEST) + dot(ri, times_i(m), precision=HIGHEST)
-        k = dot_t(rr, n, precision=HIGHEST) - dot_t(ri, times_i(n), precision=HIGHEST)
+        n = wide_dot(root[...], embed(m))
+        k = wide_dot(jnp.concatenate([jnp.transpose(rr), -jnp.transpose(ri)], 1), embed(n))
         e_hi, e_lo = split(jnp.concatenate([embed(k[:HALF]), embed(k[HALF:])], 0))
         out[...] = w[...] - (dot(p01[...], e_hi) + dot(p01[...], e_lo))
 
@@ -389,9 +392,11 @@
     return jnp.sum(x.reshape((count, -1) + x.shape[1:]), axis=0)
 
 
-def slab_sum(x, axes):
-    count = lax.axis_size(axes)
-    return swap(copies(sum_pieces(swap(x, axes), count), count), axes)
+def slab_sum(x, inner, outer):
+    near, far = lax.axis_size(inner), lax.axis_size(outer)
+    piece = sum_pieces(swap(x, inner), near)
+    piece = sum_pieces(swap(copies(piece, far), outer), far)
+    return swap(copies(piece, near), inner)
 
 
 def spread(w_hi, pos):
@@ -426,7 +431,7 @@
     pos = lax.axis_index("panel").astype(jnp.int32)
     spot = pos.reshape(1)
     p01, part = gram(spot, w, spread(w_hi, pos))
-    return finish(spot, slab_sum(part, slab), w, p01)
+    return finish(spot, slab_sum(part, ("x", "core"), "y"), w, p01)
 
 
 def solution(mesh):

time: 101 us -> 98.7 us (0.977)
  blocking collectives: 39.4 us -> 37.4 us
    all_to_all x2 -> x3, blocking collectives: 39.4 us -> 37.4 us  [swap(): return lax.all_to_all(x, axes, 0, 0, tiled=True)]
where the time goes in v6:
time: 98.7 us; the launch traced here: 98.3 us
  blocking collectives  37.4 us (38%)
  starting transfers between devices  26.7 us (27%)
  Pallas kernels  18.6 us (19%)
  waiting for transfers between devices  10.9 us (11%)
  local copies, waits for them, and re-layouts  2.64 us (3%)
  between operations  1.55 us (2%)
    all_to_all x3, blocking collectives, swap(): return lax.all_to_all(x, axes, 0, 0, tiled=True)  37.4 us
    pallas_call x1, Pallas kernels, finish(): pl.pallas_call(finish_kernel, out_shape=jax.ShapeDtypeStruct(w.shape, F32...  13.7 us
    ppermute x3, starting transfers between devices, spread(): lax.ppermute(own, 'panel', pairs)  12.5 us
    ppermute x3, waiting for transfers between devices, spread(): lax.ppermute(own, 'panel', pairs)  6.45 us
    ppermute x1, starting transfers between devices, body(): right = lax.ppermute(down, slab, [(i + 1, i) for i in range(count - 1)])  5.57 us
    ppermute x1, starting transfers between devices, body(): left = lax.ppermute(up, slab, [(i, i + 1) for i in range(count - 1)])  4.5 us
    ppermute x1, waiting for transfers between devices, spread(): far = lax.ppermute(w_hi, 'panel', [(0, 3), (1, 6)])  4.46 us
    ppermute x1, starting transfers between devices, spread(): far = lax.ppermute(w_hi, 'panel', [(0, 3), (1, 6)])  4.16 us
  transfers between devices with their start and end apart: 6, of which 3 were waited for; matrix products, arithmetic and copies ran while one was open for 3% of the time, Pallas kernels for 0%

profile of v6, /device:TPU:1, one launch (start us, length us, event | category | flops | bytes accessed | tf_op | source)
XLA Modules:
  0.0 98.3 jit_solution(14664420872334775008)
XLA Ops:
  0.0 1.8 %pack.1 = (bf16[528,128]{1,0:T(8,128)(2,1)}, bf16[528,128]{1,0:T(8,128)(2,1)}) custom-call(f32[1024,128]{1,0:T(8,128)} %v.1, s32[2,4]{1,0:T(2,128)} %bitcast.16, s32[1,4]{1,0:T(1,128)} %bitcast.18), custom_call_target="tpu_custom_call" | custom-call | tf_op jit(solution)/shard_map/pack/pallas_call | solution.py:67
  1.8 4.5 %collective-permute-start = (bf16[528,128]{1,0:T(8,128)(2,1)}, bf16[528,128]{1,0:T(8,128)(2,1)S(1)}, u32[]{:S(2)}, u32[]{:S(2)}) collective-permute-start(bf16[528,128]{1,0:T(8,128)(2,1)} %get-tuple-element.11), channel_id=1, source_target_pairs={{0,8},{8,16},{16,24},{24,32},{32,40},{40,48},{48,56},{56,64},{64,7... | collective-permute-start | bytes 405512 | tf_op jit(solution)/shard_map/ppermute | solution.py:419
  6.3 5.6 %collective-permute-start.1 = (bf16[528,128]{1,0:T(8,128)(2,1)}, bf16[528,128]{1,0:T(8,128)(2,1)S(1)}, u32[]{:S(2)}, u32[]{:S(2)}) collective-permute-start(bf16[528,128]{1,0:T(8,128)(2,1)} %get-tuple-element.12), channel_id=1, source_target_pairs={{8,0},{16,8},{24,16},{32,24},{40,32},{48,40},{56,48},{64,56},{72,6... | collective-permute-start | bytes 405512 | tf_op jit(solution)/shard_map/ppermute | solution.py:420
  11.9 0.8 fusion.2
  12.7 0.1 copy.15
  12.8 0.1 copy.16
  12.9 0.0 copy-start
  13.0 1.6 %copy.14 = bf16[8,256,256]{1,2,0:T(8,128)(2,1)S(1)} copy(bf16[8,256,256]{2,1,0:T(8,128)(2,1)} %hop.1) | data formatting | bytes 2097152 | tf_op args[1]
  14.5 0.0 copy-done
  14.5 0.0 copy-start.3
  14.6 0.3 multiply_convert_fusion.sym
  14.9 0.0 copy-start.1
  14.9 0.0 copy-start.2
  16.2 0.0 copy-done.3
  16.3 0.0 collective-permute-done
  16.3 0.0 collective-permute-done.1
  16.3 0.0 copy-done.1
  16.3 0.0 copy-done.2
  16.3 2.4 %chebyshev.1 = (f32[1024,128]{1,0:T(8,128)S(1)}, bf16[1024,128]{1,0:T(8,128)(2,1)S(1)}) custom-call(s32[2,4]{1,0:T(2,128)S(1)} %bitcast.17, s32[1,4]{1,0:T(1,128)S(1)} %bitcast.19, f32[1]{0:T(128)S(6)} %copy.17.shift, f32[1]{0:T(128)} %copy.18.width, f32[1024,128]{1,0:T(8,128)S(1)} %broadcast_divide_fusion.base, ...), custom_call_target="tpu_custom_call" | custom-call | tf_op jit(solution)/shard_map/chebyshev/pallas_call | solution.py:164
  18.8 4.2 %collective-permute-start.2 = (bf16[1024,128]{1,0:T(8,128)(2,1)S(1)}, bf16[1024,128]{1,0:T(8,128)(2,1)S(1)}, u32[]{:S(2)}, u32[]{:S(2)}) collective-permute-start(bf16[1024,128]{1,0:T(8,128)(2,1)S(1)} %get-tuple-element.14), channel_id=1, source_target_pairs={{0,3},{1,6},{8,11},{9,14},{16,19},{17,22},{24,27},{25,30},{32,35},... | collective-permute-start | bytes 786440 | tf_op jit(solution)/shard_map/ppermute | solution.py:403
  22.9 4.5 %collective-permute-done.2 = bf16[1024,128]{1,0:T(8,128)(2,1)S(1)} collective-permute-done((bf16[1024,128]{1,0:T(8,128)(2,1)S(1)}, bf16[1024,128]{1,0:T(8,128)(2,1)S(1)}, u32[]{:S(2)}, u32[]{:S(2)}) %collective-permute-start.2) | collective-permute-done | bytes 262176 | tf_op jit(solution)/shard_map/ppermute | solution.py:403
  27.4 6.1 %collective-permute-start.3 = (bf16[1024,128]{1,0:T(8,128)(2,1)S(1)}, bf16[1024,128]{1,0:T(8,128)(2,1)S(1)}, u32[]{:S(2)}, u32[]{:S(2)}) collective-permute-start(bf16[1024,128]{1,0:T(8,128)(2,1)S(1)} %broadcast_select_fusion.own), channel_id=1, source_target_pairs={{0,1},{3,4},{1,2},{6,7},{8,9},{11,12},{9,10},{14,15},{16,17},{19,2... | collective-permute-start | bytes 786440 | tf_op jit(solution)/shard_map/ppermute | solution.py:405
  33.6 1.9 %collective-permute-start.4 = (bf16[1024,128]{1,0:T(8,128)(2,1)S(1)}, bf16[1024,128]{1,0:T(8,128)(2,1)S(1)}, u32[]{:S(2)}, u32[]{:S(2)}) collective-permute-start(bf16[1024,128]{1,0:T(8,128)(2,1)S(1)} %broadcast_select_fusion.own), channel_id=1, source_target_pairs={{0,7},{3,2},{1,0},{6,5},{8,15},{11,10},{9,8},{14,13},{16,23},{19,1... | collective-permute-start | bytes 786440 | tf_op jit(solution)/shard_map/ppermute | solution.py:405
  35.5 4.4 %collective-permute-start.5 = (bf16[1024,128]{1,0:T(8,128)(2,1)S(1)}, bf16[1024,128]{1,0:T(8,128)(2,1)S(1)}, u32[]{:S(2)}, u32[]{:S(2)}) collective-permute-start(bf16[1024,128]{1,0:T(8,128)(2,1)S(1)} %broadcast_select_fusion.own), channel_id=1, source_target_pairs={{0,6},{3,5},{1,3},{6,4},{8,14},{11,13},{9,11},{14,12},{16,22},{19,... | collective-permute-start | bytes 786440 | tf_op jit(solution)/shard_map/ppermute | solution.py:405
  40.0 0.0 collective-permute-done.3.first
  40.0 3.0 %collective-permute-done.4.second = bf16[1024,128]{1,0:T(8,128)(2,1)S(1)} collective-permute-done((bf16[1024,128]{1,0:T(8,128)(2,1)S(1)}, bf16[1024,128]{1,0:T(8,128)(2,1)S(1)}, u32[]{:S(2)}, u32[]{:S(2)}) %collective-permute-start.4) | collective-permute-done | bytes 262176 | tf_op jit(solution)/shard_map/ppermute | solution.py:405
  43.0 3.4 %collective-permute-done.5.third = bf16[1024,128]{1,0:T(8,128)(2,1)S(1)} collective-permute-done((bf16[1024,128]{1,0:T(8,128)(2,1)S(1)}, bf16[1024,128]{1,0:T(8,128)(2,1)S(1)}, u32[]{:S(2)}, u32[]{:S(2)}) %collective-permute-start.5) | collective-permute-done | bytes 262176 | tf_op jit(solution)/shard_map/ppermute | solution.py:405
  46.4 0.7 gram.1
  47.1 12.2 %all_to_all.23 = f32[8,32,128]{2,1,0:T(8,128)S(1)} all-to-all(f32[8,32,128]{2,1,0:T(8,128)S(1)} %bitcast.15), channel_id=1, replica_groups=mesh['y'=8,'x'=4,'core'=2,'panel'=8] {'x','core'}, dimensions={0} | all-to-all | bytes 262144 | tf_op jit(solution)/shard_map/all_to_all | solution.py:384
  59.4 15.1 %all_to_all.24 = f32[8,32,128]{2,1,0:T(8,128)S(1)} all-to-all(f32[8,32,128]{2,1,0:T(8,128)S(1)} %broadcast_in_dim.7), channel_id=1, replica_groups=mesh['y'=8,'x'=4,'core'=2,'panel'=8] {'y'}, dimensions={0} | all-to-all | bytes 262144 | tf_op jit(solution)/shard_map/all_to_all | solution.py:384
  74.5 10.0 %all_to_all.25 = f32[8,32,128]{2,1,0:T(8,128)S(1)} all-to-all(f32[8,32,128]{2,1,0:T(8,128)S(1)} %broadcast_in_dim.8), channel_id=1, replica_groups=mesh['y'=8,'x'=4,'core'=2,'panel'=8] {'x','core'}, dimensions={0} | all-to-all | bytes 262144 | tf_op jit(solution)/shard_map/all_to_all | solution.py:384
  84.6 13.7 %finish.1 = f32[1024,128]{1,0:T(8,128)} custom-call(s32[1]{0:T(128)} %bitcast.pos, f32[256,128]{1,0:T(8,128)S(1)} %bitcast.12, f32[1024,128]{1,0:T(8,128)S(1)} %get-tuple-element.13.w, bf16[1024,256]{1,0:T(8,128)(2,1)S(1)} %get-tuple-element.16.p01), custom_call_target="tpu_custom_call" | custom-call | tf_op jit(solution)/shard_map/finish/pallas_call | solution.py:372
  (10 shorter events, 0.2 us)
Async XLA Ops:
  1.8 14.5 %collective-permute-start = (bf16[528,128]{1,0:T(8,128)(2,1)}, bf16[528,128]{1,0:T(8,128)(2,1)S(1)}, u32[]{:S(2)}, u32[]{:S(2)}) collective-permute-start(bf16[528,128]{1,0:T(8,128)(2,1)} %get-tuple-element.11), channel_id=1, source_target_pairs={{0,8},{8,16},{16,24},{24,32},{32,40},{40,48},{48,56},{56,64},{64,7... | collective-permute-start | bytes 405512 | tf_op jit(solution)/shard_map/ppermute | solution.py:419
  6.3 10.0 %collective-permute-start.1 = (bf16[528,128]{1,0:T(8,128)(2,1)}, bf16[528,128]{1,0:T(8,128)(2,1)S(1)}, u32[]{:S(2)}, u32[]{:S(2)}) collective-permute-start(bf16[528,128]{1,0:T(8,128)(2,1)} %get-tuple-element.12), channel_id=1, source_target_pairs={{8,0},{16,8},{24,16},{32,24},{40,32},{48,40},{56,48},{64,56},{72,6... | collective-permute-start | bytes 405512 | tf_op jit(solution)/shard_map/ppermute | solution.py:420
  12.9 1.6 %copy-start = (bf16[8,256,256]{2,1,0:T(8,128)(2,1)S(1)}, bf16[8,256,256]{2,1,0:T(8,128)(2,1)}, u32[]{:S(2)}) copy-start(bf16[8,256,256]{2,1,0:T(8,128)(2,1)} %hop.1) | copy-start | bytes 3145732
  14.5 1.7 %copy-start.3 = (f32[1024,128]{1,0:T(8,128)S(1)}, f32[1024,128]{1,0:T(8,128)}, u32[]{:S(2)}) copy-start(f32[1024,128]{1,0:T(8,128)} %v.1) | copy-start | bytes 1572868
  14.9 1.4 %copy-start.1 = (s32[4,2]{0,1:T(2,128)S(1)}, s32[4,2]{0,1:T(2,128)}, u32[]{:S(2)}) copy-start(s32[4,2]{0,1:T(2,128)} %param.9) | copy-start | bytes 100
  14.9 1.4 %copy-start.2 = (s32[4]{0:T(128)S(1)}, s32[4]{0:T(128)}, u32[]{:S(2)}) copy-start(s32[4]{0:T(128)} %param.10) | copy-start | bytes 52
  18.8 8.6 %collective-permute-start.2 = (bf16[1024,128]{1,0:T(8,128)(2,1)S(1)}, bf16[1024,128]{1,0:T(8,128)(2,1)S(1)}, u32[]{:S(2)}, u32[]{:S(2)}) collective-permute-start(bf16[1024,128]{1,0:T(8,128)(2,1)S(1)} %get-tuple-element.14), channel_id=1, source_target_pairs={{0,3},{1,6},{8,11},{9,14},{16,19},{17,22},{24,27},{25,30},{32,35},... | collective-permute-start | bytes 786440 | tf_op jit(solution)/shard_map/ppermute | solution.py:403
  27.4 12.5 %collective-permute-start.3 = (bf16[1024,128]{1,0:T(8,128)(2,1)S(1)}, bf16[1024,128]{1,0:T(8,128)(2,1)S(1)}, u32[]{:S(2)}, u32[]{:S(2)}) collective-permute-start(bf16[1024,128]{1,0:T(8,128)(2,1)S(1)} %broadcast_select_fusion.own), channel_id=1, source_target_pairs={{0,1},{3,4},{1,2},{6,7},{8,9},{11,12},{9,10},{14,15},{16,17},{19,2... | collective-permute-start | bytes 786440 | tf_op jit(solution)/shard_map/ppermute | solution.py:405
  33.6 9.4 %collective-permute-start.4 = (bf16[1024,128]{1,0:T(8,128)(2,1)S(1)}, bf16[1024,128]{1,0:T(8,128)(2,1)S(1)}, u32[]{:S(2)}, u32[]{:S(2)}) collective-permute-start(bf16[1024,128]{1,0:T(8,128)(2,1)S(1)} %broadcast_select_fusion.own), channel_id=1, source_target_pairs={{0,7},{3,2},{1,0},{6,5},{8,15},{11,10},{9,8},{14,13},{16,23},{19,1... | collective-permute-start | bytes 786440 | tf_op jit(solution)/shard_map/ppermute | solution.py:405
  35.5 10.9 %collective-permute-start.5 = (bf16[1024,128]{1,0:T(8,128)(2,1)S(1)}, bf16[1024,128]{1,0:T(8,128)(2,1)S(1)}, u32[]{:S(2)}, u32[]{:S(2)}) collective-permute-start(bf16[1024,128]{1,0:T(8,128)(2,1)S(1)} %broadcast_select_fusion.own), channel_id=1, source_target_pairs={{0,6},{3,5},{1,3},{6,4},{8,14},{11,13},{9,11},{14,12},{16,22},{19,... | collective-permute-start | bytes 786440 | tf_op jit(solution)/shard_map/ppermute | solution.py:405

commit v7 on v6

--- a/solution.py
+++ b/solution.py
@@ -203,10 +203,10 @@
     col = jnp.where(lane < HALF, lane, lane - HALF)
     g00, g11 = inner(0, 0), inner(1, 1)
     diag = jnp.where(lane < HALF, g00, pltpu.roll(g11, HALF, 1))
-    out[0:HALF, :] = jnp.where(col > row, g00, jnp.where(col < row, g11, diag))
-    out[HALF : 2 * HALF, :] = inner(0, 1)
-    out[2 * HALF : 3 * HALF, :] = inner(0, 2) + inner(0, 3)
-    out[3 * HALF : 4 * HALF, :] = inner(1, 2) + inner(1, 3)
+    out[0:HALF, :] = jnp.where(col > row, g00, jnp.where(col < row, g11, diag)).astype(BF16)
+    out[HALF : 2 * HALF, :] = inner(0, 1).astype(BF16)
+    out[2 * HALF : 3 * HALF, :] = (inner(0, 2) + inner(0, 3)).astype(BF16)
+    out[3 * HALF : 4 * HALF, :] = (inner(1, 2) + inner(1, 3)).astype(BF16)
 
 
 def gram(pos, w, parts):
@@ -215,7 +215,7 @@
         gram_kernel,
         out_shape=(
             jax.ShapeDtypeStruct((w.shape[0], 2 * WIDE), BF16),
-            jax.ShapeDtypeStruct((4 * HALF, WIDE), F32),
+            jax.ShapeDtypeStruct((4 * HALF, WIDE), BF16),
         ),
         in_specs=[pl.BlockSpec(memory_space=SM)] + [spec] * 5,
         out_specs=(spec, spec),
@@ -389,7 +389,7 @@
 
 
 def sum_pieces(x, count):
-    return jnp.sum(x.reshape((count, -1) + x.shape[1:]), axis=0)
+    return jnp.sum(x.reshape((count, -1) + x.shape[1:]).astype(F32), axis=0)
 
 
 def slab_sum(x, inner, outer):

time: 98.7 us -> 98.2 us (level)
  no operation moved by 1% of the time
where the time goes in v7:
time: 98.2 us; the launch traced here: 97.8 us
  blocking collectives  36.9 us (38%)
  starting transfers between devices  26.7 us (27%)
  Pallas kernels  18.6 us (19%)
  waiting for transfers between devices  10.9 us (11%)
  local copies, waits for them, and re-layouts  2.64 us (3%)
  between operations  1.55 us (2%)
    all_to_all x3, blocking collectives, swap(): return lax.all_to_all(x, axes, 0, 0, tiled=True)  36.9 us
    pallas_call x1, Pallas kernels, finish(): pl.pallas_call(finish_kernel, out_shape=jax.ShapeDtypeStruct(w.shape, F32...  13.7 us
    ppermute x3, starting transfers between devices, spread(): lax.ppermute(own, 'panel', pairs)  12.5 us
    ppermute x3, waiting for transfers between devices, spread(): lax.ppermute(own, 'panel', pairs)  6.45 us
    ppermute x1, starting transfers between devices, body(): right = lax.ppermute(down, slab, [(i + 1, i) for i in range(count - 1)])  5.57 us
    ppermute x1, starting transfers between devices, body(): left = lax.ppermute(up, slab, [(i, i + 1) for i in range(count - 1)])  4.5 us
    ppermute x1, waiting for transfers between devices, spread(): far = lax.ppermute(w_hi, 'panel', [(0, 3), (1, 6)])  4.46 us
    ppermute x1, starting transfers between devices, spread(): far = lax.ppermute(w_hi, 'panel', [(0, 3), (1, 6)])  4.16 us
  transfers between devices with their start and end apart: 6, of which 3 were waited for; matrix products, arithmetic and copies ran while one was open for 3% of the time, Pallas kernels for 0%

profile of v7, /device:TPU:1, one launch (start us, length us, event | category | flops | bytes accessed | tf_op | source)
XLA Modules:
  0.0 97.8 jit_solution(10027576673911619856)
XLA Ops:
  0.0 1.8 %pack.1 = (bf16[528,128]{1,0:T(8,128)(2,1)}, bf16[528,128]{1,0:T(8,128)(2,1)}) custom-call(f32[1024,128]{1,0:T(8,128)} %v.1, s32[2,4]{1,0:T(2,128)} %bitcast.16, s32[1,4]{1,0:T(1,128)} %bitcast.18), custom_call_target="tpu_custom_call" | custom-call | tf_op jit(solution)/shard_map/pack/pallas_call | solution.py:67
  1.8 4.5 %collective-permute-start = (bf16[528,128]{1,0:T(8,128)(2,1)}, bf16[528,128]{1,0:T(8,128)(2,1)S(1)}, u32[]{:S(2)}, u32[]{:S(2)}) collective-permute-start(bf16[528,128]{1,0:T(8,128)(2,1)} %get-tuple-element.11), channel_id=1, source_target_pairs={{0,8},{8,16},{16,24},{24,32},{32,40},{40,48},{48,56},{56,64},{64,7... | collective-permute-start | bytes 405512 | tf_op jit(solution)/shard_map/ppermute | solution.py:419
  6.3 5.6 %collective-permute-start.1 = (bf16[528,128]{1,0:T(8,128)(2,1)}, bf16[528,128]{1,0:T(8,128)(2,1)S(1)}, u32[]{:S(2)}, u32[]{:S(2)}) collective-permute-start(bf16[528,128]{1,0:T(8,128)(2,1)} %get-tuple-element.12), channel_id=1, source_target_pairs={{8,0},{16,8},{24,16},{32,24},{40,32},{48,40},{56,48},{64,56},{72,6... | collective-permute-start | bytes 405512 | tf_op jit(solution)/shard_map/ppermute | solution.py:420
  11.9 0.8 fusion.2
  12.7 0.1 copy.15
  12.8 0.1 copy.16
  12.9 0.0 copy-start
  13.0 1.6 %copy.14 = bf16[8,256,256]{1,2,0:T(8,128)(2,1)S(1)} copy(bf16[8,256,256]{2,1,0:T(8,128)(2,1)} %hop.1) | data formatting | bytes 2097152 | tf_op args[1]
  14.5 0.0 copy-done
  14.5 0.0 copy-start.3
  14.6 0.3 multiply_convert_fusion.sym
  14.9 0.0 copy-start.1
  14.9 0.0 copy-start.2
  16.2 0.0 copy-done.3
  16.3 0.0 collective-permute-done
  16.3 0.0 collective-permute-done.1
  16.3 0.0 copy-done.1
  16.3 0.0 copy-done.2
  16.3 2.4 %chebyshev.1 = (f32[1024,128]{1,0:T(8,128)S(1)}, bf16[1024,128]{1,0:T(8,128)(2,1)S(1)}) custom-call(s32[2,4]{1,0:T(2,128)S(1)} %bitcast.17, s32[1,4]{1,0:T(1,128)S(1)} %bitcast.19, f32[1]{0:T(128)S(6)} %copy.17.shift, f32[1]{0:T(128)} %copy.18.width, f32[1024,128]{1,0:T(8,128)S(1)} %broadcast_divide_fusion.base, ...), custom_call_target="tpu_custom_call" | custom-call | tf_op jit(solution)/shard_map/chebyshev/pallas_call | solution.py:164
  18.8 4.2 %collective-permute-start.2 = (bf16[1024,128]{1,0:T(8,128)(2,1)S(1)}, bf16[1024,128]{1,0:T(8,128)(2,1)S(1)}, u32[]{:S(2)}, u32[]{:S(2)}) collective-permute-start(bf16[1024,128]{1,0:T(8,128)(2,1)S(1)} %get-tuple-element.14), channel_id=1, source_target_pairs={{0,3},{1,6},{8,11},{9,14},{16,19},{17,22},{24,27},{25,30},{32,35},... | collective-permute-start | bytes 786440 | tf_op jit(solution)/shard_map/ppermute | solution.py:403
  22.9 4.5 %collective-permute-done.2 = bf16[1024,128]{1,0:T(8,128)(2,1)S(1)} collective-permute-done((bf16[1024,128]{1,0:T(8,128)(2,1)S(1)}, bf16[1024,128]{1,0:T(8,128)(2,1)S(1)}, u32[]{:S(2)}, u32[]{:S(2)}) %collective-permute-start.2) | collective-permute-done | bytes 262176 | tf_op jit(solution)/shard_map/ppermute | solution.py:403
  27.4 6.1 %collective-permute-start.3 = (bf16[1024,128]{1,0:T(8,128)(2,1)S(1)}, bf16[1024,128]{1,0:T(8,128)(2,1)S(1)}, u32[]{:S(2)}, u32[]{:S(2)}) collective-permute-start(bf16[1024,128]{1,0:T(8,128)(2,1)S(1)} %broadcast_select_fusion.own), channel_id=1, source_target_pairs={{0,1},{3,4},{1,2},{6,7},{8,9},{11,12},{9,10},{14,15},{16,17},{19,2... | collective-permute-start | bytes 786440 | tf_op jit(solution)/shard_map/ppermute | solution.py:405
  33.6 1.9 %collective-permute-start.4 = (bf16[1024,128]{1,0:T(8,128)(2,1)S(1)}, bf16[1024,128]{1,0:T(8,128)(2,1)S(1)}, u32[]{:S(2)}, u32[]{:S(2)}) collective-permute-start(bf16[1024,128]{1,0:T(8,128)(2,1)S(1)} %broadcast_select_fusion.own), channel_id=1, source_target_pairs={{0,7},{3,2},{1,0},{6,5},{8,15},{11,10},{9,8},{14,13},{16,23},{19,1... | collective-permute-start | bytes 786440 | tf_op jit(solution)/shard_map/ppermute | solution.py:405
  35.5 4.4 %collective-permute-start.5 = (bf16[1024,128]{1,0:T(8,128)(2,1)S(1)}, bf16[1024,128]{1,0:T(8,128)(2,1)S(1)}, u32[]{:S(2)}, u32[]{:S(2)}) collective-permute-start(bf16[1024,128]{1,0:T(8,128)(2,1)S(1)} %broadcast_select_fusion.own), channel_id=1, source_target_pairs={{0,6},{3,5},{1,3},{6,4},{8,14},{11,13},{9,11},{14,12},{16,22},{19,... | collective-permute-start | bytes 786440 | tf_op jit(solution)/shard_map/ppermute | solution.py:405
  40.0 0.0 collective-permute-done.3.first
  40.0 3.0 %collective-permute-done.4.second = bf16[1024,128]{1,0:T(8,128)(2,1)S(1)} collective-permute-done((bf16[1024,128]{1,0:T(8,128)(2,1)S(1)}, bf16[1024,128]{1,0:T(8,128)(2,1)S(1)}, u32[]{:S(2)}, u32[]{:S(2)}) %collective-permute-start.4) | collective-permute-done | bytes 262176 | tf_op jit(solution)/shard_map/ppermute | solution.py:405
  43.0 3.4 %collective-permute-done.5.third = bf16[1024,128]{1,0:T(8,128)(2,1)S(1)} collective-permute-done((bf16[1024,128]{1,0:T(8,128)(2,1)S(1)}, bf16[1024,128]{1,0:T(8,128)(2,1)S(1)}, u32[]{:S(2)}, u32[]{:S(2)}) %collective-permute-start.5) | collective-permute-done | bytes 262176 | tf_op jit(solution)/shard_map/ppermute | solution.py:405
  46.4 0.7 gram.1
  47.1 11.8 %all_to_all.23 = bf16[8,32,128]{2,1,0:T(8,128)(2,1)S(1)} all-to-all(bf16[8,32,128]{2,1,0:T(8,128)(2,1)S(1)} %bitcast.15), channel_id=1, replica_groups=mesh['y'=8,'x'=4,'core'=2,'panel'=8] {'x','core'}, dimensions={0} | all-to-all | bytes 131072 | tf_op jit(solution)/shard_map/all_to_all | solution.py:384
  58.9 15.1 %all_to_all.24 = f32[8,32,128]{2,1,0:T(8,128)S(1)} all-to-all(f32[8,32,128]{2,1,0:T(8,128)S(1)} %broadcast_in_dim.7), channel_id=1, replica_groups=mesh['y'=8,'x'=4,'core'=2,'panel'=8] {'y'}, dimensions={0} | all-to-all | bytes 262144 | tf_op jit(solution)/shard_map/all_to_all | solution.py:384
  74.0 10.0 %all_to_all.25 = f32[8,32,128]{2,1,0:T(8,128)S(1)} all-to-all(f32[8,32,128]{2,1,0:T(8,128)S(1)} %broadcast_in_dim.8), channel_id=1, replica_groups=mesh['y'=8,'x'=4,'core'=2,'panel'=8] {'x','core'}, dimensions={0} | all-to-all | bytes 262144 | tf_op jit(solution)/shard_map/all_to_all | solution.py:384
  84.1 13.7 %finish.1 = f32[1024,128]{1,0:T(8,128)} custom-call(s32[1]{0:T(128)} %bitcast.pos, f32[256,128]{1,0:T(8,128)S(1)} %bitcast.12, f32[1024,128]{1,0:T(8,128)S(1)} %get-tuple-element.13.w, bf16[1024,256]{1,0:T(8,128)(2,1)S(1)} %get-tuple-element.16.p01), custom_call_target="tpu_custom_call" | custom-call | tf_op jit(solution)/shard_map/finish/pallas_call | solution.py:372
  (10 shorter events, 0.2 us)
Async XLA Ops:
  1.8 14.5 %collective-permute-start = (bf16[528,128]{1,0:T(8,128)(2,1)}, bf16[528,128]{1,0:T(8,128)(2,1)S(1)}, u32[]{:S(2)}, u32[]{:S(2)}) collective-permute-start(bf16[528,128]{1,0:T(8,128)(2,1)} %get-tuple-element.11), channel_id=1, source_target_pairs={{0,8},{8,16},{16,24},{24,32},{32,40},{40,48},{48,56},{56,64},{64,7... | collective-permute-start | bytes 405512 | tf_op jit(solution)/shard_map/ppermute | solution.py:419
  6.3 10.0 %collective-permute-start.1 = (bf16[528,128]{1,0:T(8,128)(2,1)}, bf16[528,128]{1,0:T(8,128)(2,1)S(1)}, u32[]{:S(2)}, u32[]{:S(2)}) collective-permute-start(bf16[528,128]{1,0:T(8,128)(2,1)} %get-tuple-element.12), channel_id=1, source_target_pairs={{8,0},{16,8},{24,16},{32,24},{40,32},{48,40},{56,48},{64,56},{72,6... | collective-permute-start | bytes 405512 | tf_op jit(solution)/shard_map/ppermute | solution.py:420
  12.9 1.6 %copy-start = (bf16[8,256,256]{2,1,0:T(8,128)(2,1)S(1)}, bf16[8,256,256]{2,1,0:T(8,128)(2,1)}, u32[]{:S(2)}) copy-start(bf16[8,256,256]{2,1,0:T(8,128)(2,1)} %hop.1) | copy-start | bytes 3145732
  14.5 1.7 %copy-start.3 = (f32[1024,128]{1,0:T(8,128)S(1)}, f32[1024,128]{1,0:T(8,128)}, u32[]{:S(2)}) copy-start(f32[1024,128]{1,0:T(8,128)} %v.1) | copy-start | bytes 1572868
  14.9 1.4 %copy-start.1 = (s32[4,2]{0,1:T(2,128)S(1)}, s32[4,2]{0,1:T(2,128)}, u32[]{:S(2)}) copy-start(s32[4,2]{0,1:T(2,128)} %param.9) | copy-start | bytes 100
  14.9 1.4 %copy-start.2 = (s32[4]{0:T(128)S(1)}, s32[4]{0:T(128)}, u32[]{:S(2)}) copy-start(s32[4]{0:T(128)} %param.10) | copy-start | bytes 52
  18.8 8.6 %collective-permute-start.2 = (bf16[1024,128]{1,0:T(8,128)(2,1)S(1)}, bf16[1024,128]{1,0:T(8,128)(2,1)S(1)}, u32[]{:S(2)}, u32[]{:S(2)}) collective-permute-start(bf16[1024,128]{1,0:T(8,128)(2,1)S(1)} %get-tuple-element.14), channel_id=1, source_target_pairs={{0,3},{1,6},{8,11},{9,14},{16,19},{17,22},{24,27},{25,30},{32,35},... | collective-permute-start | bytes 786440 | tf_op jit(solution)/shard_map/ppermute | solution.py:403
  27.4 12.5 %collective-permute-start.3 = (bf16[1024,128]{1,0:T(8,128)(2,1)S(1)}, bf16[1024,128]{1,0:T(8,128)(2,1)S(1)}, u32[]{:S(2)}, u32[]{:S(2)}) collective-permute-start(bf16[1024,128]{1,0:T(8,128)(2,1)S(1)} %broadcast_select_fusion.own), channel_id=1, source_target_pairs={{0,1},{3,4},{1,2},{6,7},{8,9},{11,12},{9,10},{14,15},{16,17},{19,2... | collective-permute-start | bytes 786440 | tf_op jit(solution)/shard_map/ppermute | solution.py:405
  33.6 9.4 %collective-permute-start.4 = (bf16[1024,128]{1,0:T(8,128)(2,1)S(1)}, bf16[1024,128]{1,0:T(8,128)(2,1)S(1)}, u32[]{:S(2)}, u32[]{:S(2)}) collective-permute-start(bf16[1024,128]{1,0:T(8,128)(2,1)S(1)} %broadcast_select_fusion.own), channel_id=1, source_target_pairs={{0,7},{3,2},{1,0},{6,5},{8,15},{11,10},{9,8},{14,13},{16,23},{19,1... | collective-permute-start | bytes 786440 | tf_op jit(solution)/shard_map/ppermute | solution.py:405
  35.5 10.9 %collective-permute-start.5 = (bf16[1024,128]{1,0:T(8,128)(2,1)S(1)}, bf16[1024,128]{1,0:T(8,128)(2,1)S(1)}, u32[]{:S(2)}, u32[]{:S(2)}) collective-permute-start(bf16[1024,128]{1,0:T(8,128)(2,1)S(1)} %broadcast_select_fusion.own), channel_id=1, source_target_pairs={{0,6},{3,5},{1,3},{6,4},{8,14},{11,13},{9,11},{14,12},{16,22},{19,... | collective-permute-start | bytes 786440 | tf_op jit(solution)/shard_map/ppermute | solution.py:405

commit v8 on v6

--- a/solution.py
+++ b/solution.py
@@ -17,11 +17,11 @@
 META = 16
 MISSING = 8
 STEPS = (
+    [(0, 6), (3, 5), (1, 3), (6, 4)],
     [(0, 1), (3, 4), (1, 2), (6, 7)],
     [(0, 7), (3, 2), (1, 0), (6, 5)],
-    [(0, 6), (3, 5), (1, 3), (6, 4)],
 )
-HELD = ((0, 1, 2, 0, 1, 3, 3, 2), (2, 0, 1, 3, 3, 2, 0, 1))
+HELD = ((0, 2, 3, 0, 2, 1, 1, 3), (3, 0, 2, 1, 1, 3, 0, 2))
 VM = pltpu.VMEM
 SM = pltpu.SMEM
 

time: 98.7 us -> 100 us (1.013)
  waiting for transfers between devices: 10.9 us -> 12.4 us
    ppermute x3, waiting for transfers between devices: 6.45 us -> 7.93 us  [spread(): lax.ppermute(own, 'panel', pairs)]
  transfers between devices with their start and end apart: 6 -> 6, of which waited for: 3 -> 4; matrix products, arithmetic and copies ran while one was open for 3% -> 3% of each run, Pallas kernels for 0% -> 0%
where the time goes in v8:
time: 100 us
  blocking collectives  37.1 us (37%)
  starting transfers between devices  27.3 us (27%)
  Pallas kernels  18.6 us (19%)
  waiting for transfers between devices  12.4 us (12%)
  local copies, waits for them, and re-layouts  2.64 us (3%)
  between operations  1.54 us (2%)
    all_to_all x3, blocking collectives, swap(): return lax.all_to_all(x, axes, 0, 0, tiled=True)  37.1 us
    pallas_call x1, Pallas kernels, finish(): pl.pallas_call(finish_kernel, out_shape=jax.ShapeDtypeStruct(w.shape, F32...  13.7 us
    ppermute x3, starting transfers between devices, spread(): lax.ppermute(own, 'panel', pairs)  13.1 us
    ppermute x3, waiting for transfers between devices, spread(): lax.ppermute(own, 'panel', pairs)  7.93 us
    ppermute x1, starting transfers between devices, body(): right = lax.ppermute(down, slab, [(i + 1, i) for i in range(count - 1)])  5.57 us
    ppermute x1, starting transfers between devices, body(): left = lax.ppermute(up, slab, [(i, i + 1) for i in range(count - 1)])  4.5 us
    ppermute x1, waiting for transfers between devices, spread(): far = lax.ppermute(w_hi, 'panel', [(0, 3), (1, 6)])  4.46 us
    ppermute x1, starting transfers between devices, spread(): far = lax.ppermute(w_hi, 'panel', [(0, 3), (1, 6)])  4.16 us
  transfers between devices with their start and end apart: 6, of which 4 were waited for; matrix products, arithmetic and copies ran while one was open for 3% of the time, Pallas kernels for 0%

profile of v8, /device:TPU:1, one launch (start us, length us, event | category | flops | bytes accessed | tf_op | source)
XLA Modules:
  0.0 100.0 jit_solution(1986675637867124267)
XLA Ops:
  0.0 1.8 %pack.1 = (bf16[528,128]{1,0:T(8,128)(2,1)}, bf16[528,128]{1,0:T(8,128)(2,1)}) custom-call(f32[1024,128]{1,0:T(8,128)} %v.1, s32[2,4]{1,0:T(2,128)} %bitcast.16, s32[1,4]{1,0:T(1,128)} %bitcast.18), custom_call_target="tpu_custom_call" | custom-call | tf_op jit(solution)/shard_map/pack/pallas_call | solution.py:67
  1.8 4.5 %collective-permute-start = (bf16[528,128]{1,0:T(8,128)(2,1)}, bf16[528,128]{1,0:T(8,128)(2,1)S(1)}, u32[]{:S(2)}, u32[]{:S(2)}) collective-permute-start(bf16[528,128]{1,0:T(8,128)(2,1)} %get-tuple-element.11), channel_id=1, source_target_pairs={{0,8},{8,16},{16,24},{24,32},{32,40},{40,48},{48,56},{56,64},{64,7... | collective-permute-start | bytes 405512 | tf_op jit(solution)/shard_map/ppermute | solution.py:419
  6.3 5.6 %collective-permute-start.1 = (bf16[528,128]{1,0:T(8,128)(2,1)}, bf16[528,128]{1,0:T(8,128)(2,1)S(1)}, u32[]{:S(2)}, u32[]{:S(2)}) collective-permute-start(bf16[528,128]{1,0:T(8,128)(2,1)} %get-tuple-element.12), channel_id=1, source_target_pairs={{8,0},{16,8},{24,16},{32,24},{40,32},{48,40},{56,48},{64,56},{72,6... | collective-permute-start | bytes 405512 | tf_op jit(solution)/shard_map/ppermute | solution.py:420
  11.9 0.8 fusion.2
  12.7 0.1 copy.15
  12.8 0.1 copy.16
  12.9 0.0 copy-start
  13.0 1.6 %copy.14 = bf16[8,256,256]{1,2,0:T(8,128)(2,1)S(1)} copy(bf16[8,256,256]{2,1,0:T(8,128)(2,1)} %hop.1) | data formatting | bytes 2097152 | tf_op args[1]
  14.5 0.0 copy-done
  14.5 0.0 copy-start.3
  14.6 0.3 multiply_convert_fusion.sym
  14.9 0.0 copy-start.1
  14.9 0.0 copy-start.2
  16.2 0.0 copy-done.3
  16.3 0.0 collective-permute-done
  16.3 0.0 collective-permute-done.1
  16.3 0.0 copy-done.1
  16.3 0.0 copy-done.2
  16.3 2.4 %chebyshev.1 = (f32[1024,128]{1,0:T(8,128)S(1)}, bf16[1024,128]{1,0:T(8,128)(2,1)S(1)}) custom-call(s32[2,4]{1,0:T(2,128)S(1)} %bitcast.17, s32[1,4]{1,0:T(1,128)S(1)} %bitcast.19, f32[1]{0:T(128)S(6)} %copy.17.shift, f32[1]{0:T(128)} %copy.18.width, f32[1024,128]{1,0:T(8,128)S(1)} %broadcast_divide_fusion.base, ...), custom_call_target="tpu_custom_call" | custom-call | tf_op jit(solution)/shard_map/chebyshev/pallas_call | solution.py:164
  18.8 4.2 %collective-permute-start.2 = (bf16[1024,128]{1,0:T(8,128)(2,1)S(1)}, bf16[1024,128]{1,0:T(8,128)(2,1)S(1)}, u32[]{:S(2)}, u32[]{:S(2)}) collective-permute-start(bf16[1024,128]{1,0:T(8,128)(2,1)S(1)} %get-tuple-element.14), channel_id=1, source_target_pairs={{0,3},{1,6},{8,11},{9,14},{16,19},{17,22},{24,27},{25,30},{32,35},... | collective-permute-start | bytes 786440 | tf_op jit(solution)/shard_map/ppermute | solution.py:403
  22.9 4.5 %collective-permute-done.2 = bf16[1024,128]{1,0:T(8,128)(2,1)S(1)} collective-permute-done((bf16[1024,128]{1,0:T(8,128)(2,1)S(1)}, bf16[1024,128]{1,0:T(8,128)(2,1)S(1)}, u32[]{:S(2)}, u32[]{:S(2)}) %collective-permute-start.2) | collective-permute-done | bytes 262176 | tf_op jit(solution)/shard_map/ppermute | solution.py:403
  27.4 9.9 %collective-permute-start.3 = (bf16[1024,128]{1,0:T(8,128)(2,1)S(1)}, bf16[1024,128]{1,0:T(8,128)(2,1)S(1)}, u32[]{:S(2)}, u32[]{:S(2)}) collective-permute-start(bf16[1024,128]{1,0:T(8,128)(2,1)S(1)} %broadcast_select_fusion.own), channel_id=1, source_target_pairs={{0,6},{3,5},{1,3},{6,4},{8,14},{11,13},{9,11},{14,12},{16,22},{19,... | collective-permute-start | bytes 786440 | tf_op jit(solution)/shard_map/ppermute | solution.py:405
  37.3 1.3 %collective-permute-start.4 = (bf16[1024,128]{1,0:T(8,128)(2,1)S(1)}, bf16[1024,128]{1,0:T(8,128)(2,1)S(1)}, u32[]{:S(2)}, u32[]{:S(2)}) collective-permute-start(bf16[1024,128]{1,0:T(8,128)(2,1)S(1)} %broadcast_select_fusion.own), channel_id=1, source_target_pairs={{0,1},{3,4},{1,2},{6,7},{8,9},{11,12},{9,10},{14,15},{16,17},{19,2... | collective-permute-start | bytes 786440 | tf_op jit(solution)/shard_map/ppermute | solution.py:405
  38.6 1.9 %collective-permute-start.5 = (bf16[1024,128]{1,0:T(8,128)(2,1)S(1)}, bf16[1024,128]{1,0:T(8,128)(2,1)S(1)}, u32[]{:S(2)}, u32[]{:S(2)}) collective-permute-start(bf16[1024,128]{1,0:T(8,128)(2,1)S(1)} %broadcast_select_fusion.own), channel_id=1, source_target_pairs={{0,7},{3,2},{1,0},{6,5},{8,15},{11,10},{9,8},{14,13},{16,23},{19,1... | collective-permute-start | bytes 786440 | tf_op jit(solution)/shard_map/ppermute | solution.py:405
  40.6 2.8 %collective-permute-done.3.first = bf16[1024,128]{1,0:T(8,128)(2,1)S(1)} collective-permute-done((bf16[1024,128]{1,0:T(8,128)(2,1)S(1)}, bf16[1024,128]{1,0:T(8,128)(2,1)S(1)}, u32[]{:S(2)}, u32[]{:S(2)}) %collective-permute-start.3) | collective-permute-done | bytes 262176 | tf_op jit(solution)/shard_map/ppermute | solution.py:405
  43.3 0.8 collective-permute-done.4.second
  44.2 4.3 %collective-permute-done.5.third = bf16[1024,128]{1,0:T(8,128)(2,1)S(1)} collective-permute-done((bf16[1024,128]{1,0:T(8,128)(2,1)S(1)}, bf16[1024,128]{1,0:T(8,128)(2,1)S(1)}, u32[]{:S(2)}, u32[]{:S(2)}) %collective-permute-start.5) | collective-permute-done | bytes 262176 | tf_op jit(solution)/shard_map/ppermute | solution.py:405
  48.5 0.7 gram.1
  49.2 12.4 %all_to_all.23 = f32[8,32,128]{2,1,0:T(8,128)S(1)} all-to-all(f32[8,32,128]{2,1,0:T(8,128)S(1)} %bitcast.15), channel_id=1, replica_groups=mesh['y'=8,'x'=4,'core'=2,'panel'=8] {'x','core'}, dimensions={0} | all-to-all | bytes 262144 | tf_op jit(solution)/shard_map/all_to_all | solution.py:384
  61.6 14.7 %all_to_all.24 = f32[8,32,128]{2,1,0:T(8,128)S(1)} all-to-all(f32[8,32,128]{2,1,0:T(8,128)S(1)} %broadcast_in_dim.7), channel_id=1, replica_groups=mesh['y'=8,'x'=4,'core'=2,'panel'=8] {'y'}, dimensions={0} | all-to-all | bytes 262144 | tf_op jit(solution)/shard_map/all_to_all | solution.py:384
  76.3 10.0 %all_to_all.25 = f32[8,32,128]{2,1,0:T(8,128)S(1)} all-to-all(f32[8,32,128]{2,1,0:T(8,128)S(1)} %broadcast_in_dim.8), channel_id=1, replica_groups=mesh['y'=8,'x'=4,'core'=2,'panel'=8] {'x','core'}, dimensions={0} | all-to-all | bytes 262144 | tf_op jit(solution)/shard_map/all_to_all | solution.py:384
  86.3 13.7 %finish.1 = f32[1024,128]{1,0:T(8,128)} custom-call(s32[1]{0:T(128)} %bitcast.pos, f32[256,128]{1,0:T(8,128)S(1)} %bitcast.12, f32[1024,128]{1,0:T(8,128)S(1)} %get-tuple-element.13.w, bf16[1024,256]{1,0:T(8,128)(2,1)S(1)} %get-tuple-element.16.p01), custom_call_target="tpu_custom_call" | custom-call | tf_op jit(solution)/shard_map/finish/pallas_call | solution.py:372
  (10 shorter events, 0.2 us)
Async XLA Ops:
  1.8 14.5 %collective-permute-start = (bf16[528,128]{1,0:T(8,128)(2,1)}, bf16[528,128]{1,0:T(8,128)(2,1)S(1)}, u32[]{:S(2)}, u32[]{:S(2)}) collective-permute-start(bf16[528,128]{1,0:T(8,128)(2,1)} %get-tuple-element.11), channel_id=1, source_target_pairs={{0,8},{8,16},{16,24},{24,32},{32,40},{40,48},{48,56},{56,64},{64,7... | collective-permute-start | bytes 405512 | tf_op jit(solution)/shard_map/ppermute | solution.py:419
  6.3 10.0 %collective-permute-start.1 = (bf16[528,128]{1,0:T(8,128)(2,1)}, bf16[528,128]{1,0:T(8,128)(2,1)S(1)}, u32[]{:S(2)}, u32[]{:S(2)}) collective-permute-start(bf16[528,128]{1,0:T(8,128)(2,1)} %get-tuple-element.12), channel_id=1, source_target_pairs={{8,0},{16,8},{24,16},{32,24},{40,32},{48,40},{56,48},{64,56},{72,6... | collective-permute-start | bytes 405512 | tf_op jit(solution)/shard_map/ppermute | solution.py:420
  12.9 1.6 %copy-start = (bf16[8,256,256]{2,1,0:T(8,128)(2,1)S(1)}, bf16[8,256,256]{2,1,0:T(8,128)(2,1)}, u32[]{:S(2)}) copy-start(bf16[8,256,256]{2,1,0:T(8,128)(2,1)} %hop.1) | copy-start | bytes 3145732
  14.5 1.7 %copy-start.3 = (f32[1024,128]{1,0:T(8,128)S(1)}, f32[1024,128]{1,0:T(8,128)}, u32[]{:S(2)}) copy-start(f32[1024,128]{1,0:T(8,128)} %v.1) | copy-start | bytes 1572868
  14.9 1.4 %copy-start.1 = (s32[4,2]{0,1:T(2,128)S(1)}, s32[4,2]{0,1:T(2,128)}, u32[]{:S(2)}) copy-start(s32[4,2]{0,1:T(2,128)} %param.9) | copy-start | bytes 100
  14.9 1.4 %copy-start.2 = (s32[4]{0:T(128)S(1)}, s32[4]{0:T(128)}, u32[]{:S(2)}) copy-start(s32[4]{0:T(128)} %param.10) | copy-start | bytes 52
  18.8 8.6 %collective-permute-start.2 = (bf16[1024,128]{1,0:T(8,128)(2,1)S(1)}, bf16[1024,128]{1,0:T(8,128)(2,1)S(1)}, u32[]{:S(2)}, u32[]{:S(2)}) collective-permute-start(bf16[1024,128]{1,0:T(8,128)(2,1)S(1)} %get-tuple-element.14), channel_id=1, source_target_pairs={{0,3},{1,6},{8,11},{9,14},{16,19},{17,22},{24,27},{25,30},{32,35},... | collective-permute-start | bytes 786440 | tf_op jit(solution)/shard_map/ppermute | solution.py:403
  27.4 15.9 %collective-permute-start.3 = (bf16[1024,128]{1,0:T(8,128)(2,1)S(1)}, bf16[1024,128]{1,0:T(8,128)(2,1)S(1)}, u32[]{:S(2)}, u32[]{:S(2)}) collective-permute-start(bf16[1024,128]{1,0:T(8,128)(2,1)S(1)} %broadcast_select_fusion.own), channel_id=1, source_target_pairs={{0,6},{3,5},{1,3},{6,4},{8,14},{11,13},{9,11},{14,12},{16,22},{19,... | collective-permute-start | bytes 786440 | tf_op jit(solution)/shard_map/ppermute | solution.py:405
  37.3 6.9 %collective-permute-start.4 = (bf16[1024,128]{1,0:T(8,128)(2,1)S(1)}, bf16[1024,128]{1,0:T(8,128)(2,1)S(1)}, u32[]{:S(2)}, u32[]{:S(2)}) collective-permute-start(bf16[1024,128]{1,0:T(8,128)(2,1)S(1)} %broadcast_select_fusion.own), channel_id=1, source_target_pairs={{0,1},{3,4},{1,2},{6,7},{8,9},{11,12},{9,10},{14,15},{16,17},{19,2... | collective-permute-start | bytes 786440 | tf_op jit(solution)/shard_map/ppermute | solution.py:405
  38.6 9.9 %collective-permute-start.5 = (bf16[1024,128]{1,0:T(8,128)(2,1)S(1)}, bf16[1024,128]{1,0:T(8,128)(2,1)S(1)}, u32[]{:S(2)}, u32[]{:S(2)}) collective-permute-start(bf16[1024,128]{1,0:T(8,128)(2,1)S(1)} %broadcast_select_fusion.own), channel_id=1, source_target_pairs={{0,7},{3,2},{1,0},{6,5},{8,15},{11,10},{9,8},{14,13},{16,23},{19,1... | collective-permute-start | bytes 786440 | tf_op jit(solution)/shard_map/ppermute | solution.py:405

commit v9 on v8

--- a/solution.py
+++ b/solution.py
@@ -17,11 +17,11 @@
 META = 16
 MISSING = 8
 STEPS = (
+    [(0, 7), (3, 4), (1, 2), (6, 5)],
+    [(0, 1), (3, 2), (1, 0), (6, 7)],
     [(0, 6), (3, 5), (1, 3), (6, 4)],
-    [(0, 1), (3, 4), (1, 2), (6, 7)],
-    [(0, 7), (3, 2), (1, 0), (6, 5)],
 )
-HELD = ((0, 2, 3, 0, 2, 1, 1, 3), (3, 0, 2, 1, 1, 3, 0, 2))
+HELD = ((0, 2, 2, 0, 1, 3, 3, 1), (2, 0, 1, 3, 3, 1, 0, 2))
 VM = pltpu.VMEM
 SM = pltpu.SMEM
 

time: 100 us -> 97.6 us (0.976)
  waiting for transfers between devices: 12.4 us -> 10 us
    ppermute x3, waiting for transfers between devices: 7.93 us -> 5.54 us  [spread(): lax.ppermute(own, 'panel', pairs)]
  transfers between devices with their start and end apart: 6 -> 6, of which waited for: 4 -> 3; matrix products, arithmetic and copies ran while one was open for 3% -> 3% of each run, Pallas kernels for 0% -> 0%
where the time goes in v9:
time: 97.6 us; the launch traced here: 97.2 us
  blocking collectives  37.1 us (38%)
  starting transfers between devices  26.8 us (27%)
  Pallas kernels  18.6 us (19%)
  waiting for transfers between devices  10 us (10%)
  local copies, waits for them, and re-layouts  2.64 us (3%)
  between operations  1.55 us (2%)
    all_to_all x3, blocking collectives, swap(): return lax.all_to_all(x, axes, 0, 0, tiled=True)  37.1 us
    pallas_call x1, Pallas kernels, finish(): pl.pallas_call(finish_kernel, out_shape=jax.ShapeDtypeStruct(w.shape, F32...  13.7 us
    ppermute x3, starting transfers between devices, spread(): lax.ppermute(own, 'panel', pairs)  12.6 us
    ppermute x1, starting transfers between devices, body(): right = lax.ppermute(down, slab, [(i + 1, i) for i in range(count - 1)])  5.57 us
    ppermute x3, waiting for transfers between devices, spread(): lax.ppermute(own, 'panel', pairs)  5.54 us
    ppermute x1, starting transfers between devices, body(): left = lax.ppermute(up, slab, [(i, i + 1) for i in range(count - 1)])  4.5 us
    ppermute x1, waiting for transfers between devices, spread(): far = lax.ppermute(w_hi, 'panel', [(0, 3), (1, 6)])  4.46 us
    ppermute x1, starting transfers between devices, spread(): far = lax.ppermute(w_hi, 'panel', [(0, 3), (1, 6)])  4.16 us
  transfers between devices with their start and end apart: 6, of which 3 were waited for; matrix products, arithmetic and copies ran while one was open for 3% of the time, Pallas kernels for 0%

profile of v9, /device:TPU:1, one launch (start us, length us, event | category | flops | bytes accessed | tf_op | source)
XLA Modules:
  0.0 97.2 jit_solution(13104006738900186815)
XLA Ops:
  0.0 1.8 %pack.1 = (bf16[528,128]{1,0:T(8,128)(2,1)}, bf16[528,128]{1,0:T(8,128)(2,1)}) custom-call(f32[1024,128]{1,0:T(8,128)} %v.1, s32[2,4]{1,0:T(2,128)} %bitcast.16, s32[1,4]{1,0:T(1,128)} %bitcast.18), custom_call_target="tpu_custom_call" | custom-call | tf_op jit(solution)/shard_map/pack/pallas_call | solution.py:67
  1.8 4.5 %collective-permute-start = (bf16[528,128]{1,0:T(8,128)(2,1)}, bf16[528,128]{1,0:T(8,128)(2,1)S(1)}, u32[]{:S(2)}, u32[]{:S(2)}) collective-permute-start(bf16[528,128]{1,0:T(8,128)(2,1)} %get-tuple-element.11), channel_id=1, source_target_pairs={{0,8},{8,16},{16,24},{24,32},{32,40},{40,48},{48,56},{56,64},{64,7... | collective-permute-start | bytes 405512 | tf_op jit(solution)/shard_map/ppermute | solution.py:419
  6.3 5.6 %collective-permute-start.1 = (bf16[528,128]{1,0:T(8,128)(2,1)}, bf16[528,128]{1,0:T(8,128)(2,1)S(1)}, u32[]{:S(2)}, u32[]{:S(2)}) collective-permute-start(bf16[528,128]{1,0:T(8,128)(2,1)} %get-tuple-element.12), channel_id=1, source_target_pairs={{8,0},{16,8},{24,16},{32,24},{40,32},{48,40},{56,48},{64,56},{72,6... | collective-permute-start | bytes 405512 | tf_op jit(solution)/shard_map/ppermute | solution.py:420
  11.9 0.8 fusion.2
  12.7 0.1 copy.15
  12.8 0.1 copy.16
  12.9 0.0 copy-start
  13.0 1.6 %copy.14 = bf16[8,256,256]{1,2,0:T(8,128)(2,1)S(1)} copy(bf16[8,256,256]{2,1,0:T(8,128)(2,1)} %hop.1) | data formatting | bytes 2097152 | tf_op args[1]
  14.5 0.0 copy-done
  14.5 0.0 copy-start.3
  14.6 0.3 multiply_convert_fusion.sym
  14.9 0.0 copy-start.1
  14.9 0.0 copy-start.2
  16.2 0.0 copy-done.3
  16.3 0.0 collective-permute-done
  16.3 0.0 collective-permute-done.1
  16.3 0.0 copy-done.1
  16.3 0.0 copy-done.2
  16.3 2.4 %chebyshev.1 = (f32[1024,128]{1,0:T(8,128)S(1)}, bf16[1024,128]{1,0:T(8,128)(2,1)S(1)}) custom-call(s32[2,4]{1,0:T(2,128)S(1)} %bitcast.17, s32[1,4]{1,0:T(1,128)S(1)} %bitcast.19, f32[1]{0:T(128)S(6)} %copy.17.shift, f32[1]{0:T(128)} %copy.18.width, f32[1024,128]{1,0:T(8,128)S(1)} %broadcast_divide_fusion.base, ...), custom_call_target="tpu_custom_call" | custom-call | tf_op jit(solution)/shard_map/chebyshev/pallas_call | solution.py:164
  18.8 4.2 %collective-permute-start.2 = (bf16[1024,128]{1,0:T(8,128)(2,1)S(1)}, bf16[1024,128]{1,0:T(8,128)(2,1)S(1)}, u32[]{:S(2)}, u32[]{:S(2)}) collective-permute-start(bf16[1024,128]{1,0:T(8,128)(2,1)S(1)} %get-tuple-element.14), channel_id=1, source_target_pairs={{0,3},{1,6},{8,11},{9,14},{16,19},{17,22},{24,27},{25,30},{32,35},... | collective-permute-start | bytes 786440 | tf_op jit(solution)/shard_map/ppermute | solution.py:403
  22.9 4.5 %collective-permute-done.2 = bf16[1024,128]{1,0:T(8,128)(2,1)S(1)} collective-permute-done((bf16[1024,128]{1,0:T(8,128)(2,1)S(1)}, bf16[1024,128]{1,0:T(8,128)(2,1)S(1)}, u32[]{:S(2)}, u32[]{:S(2)}) %collective-permute-start.2) | collective-permute-done | bytes 262176 | tf_op jit(solution)/shard_map/ppermute | solution.py:403
  27.4 1.3 %collective-permute-start.3 = (bf16[1024,128]{1,0:T(8,128)(2,1)S(1)}, bf16[1024,128]{1,0:T(8,128)(2,1)S(1)}, u32[]{:S(2)}, u32[]{:S(2)}) collective-permute-start(bf16[1024,128]{1,0:T(8,128)(2,1)S(1)} %broadcast_select_fusion.own), channel_id=1, source_target_pairs={{0,7},{3,4},{1,2},{6,5},{8,15},{11,12},{9,10},{14,13},{16,23},{19,... | collective-permute-start | bytes 786440 | tf_op jit(solution)/shard_map/ppermute | solution.py:405
  28.8 6.2 %collective-permute-start.4 = (bf16[1024,128]{1,0:T(8,128)(2,1)S(1)}, bf16[1024,128]{1,0:T(8,128)(2,1)S(1)}, u32[]{:S(2)}, u32[]{:S(2)}) collective-permute-start(bf16[1024,128]{1,0:T(8,128)(2,1)S(1)} %broadcast_select_fusion.own), channel_id=1, source_target_pairs={{0,1},{3,2},{1,0},{6,7},{8,9},{11,10},{9,8},{14,15},{16,17},{19,18... | collective-permute-start | bytes 786440 | tf_op jit(solution)/shard_map/ppermute | solution.py:405
  34.9 5.1 %collective-permute-start.5 = (bf16[1024,128]{1,0:T(8,128)(2,1)S(1)}, bf16[1024,128]{1,0:T(8,128)(2,1)S(1)}, u32[]{:S(2)}, u32[]{:S(2)}) collective-permute-start(bf16[1024,128]{1,0:T(8,128)(2,1)S(1)} %broadcast_select_fusion.own), channel_id=1, source_target_pairs={{0,6},{3,5},{1,3},{6,4},{8,14},{11,13},{9,11},{14,12},{16,22},{19,... | collective-permute-start | bytes 786440 | tf_op jit(solution)/shard_map/ppermute | solution.py:405
  40.1 0.0 collective-permute-done.3.first
  40.1 0.3 collective-permute-done.4.second
  40.3 5.3 %collective-permute-done.5.third = bf16[1024,128]{1,0:T(8,128)(2,1)S(1)} collective-permute-done((bf16[1024,128]{1,0:T(8,128)(2,1)S(1)}, bf16[1024,128]{1,0:T(8,128)(2,1)S(1)}, u32[]{:S(2)}, u32[]{:S(2)}) %collective-permute-start.5) | collective-permute-done | bytes 262176 | tf_op jit(solution)/shard_map/ppermute | solution.py:405
  45.6 0.7 gram.1
  46.3 12.4 %all_to_all.23 = f32[8,32,128]{2,1,0:T(8,128)S(1)} all-to-all(f32[8,32,128]{2,1,0:T(8,128)S(1)} %bitcast.15), channel_id=1, replica_groups=mesh['y'=8,'x'=4,'core'=2,'panel'=8] {'x','core'}, dimensions={0} | all-to-all | bytes 262144 | tf_op jit(solution)/shard_map/all_to_all | solution.py:384
  58.7 14.7 %all_to_all.24 = f32[8,32,128]{2,1,0:T(8,128)S(1)} all-to-all(f32[8,32,128]{2,1,0:T(8,128)S(1)} %broadcast_in_dim.7), channel_id=1, replica_groups=mesh['y'=8,'x'=4,'core'=2,'panel'=8] {'y'}, dimensions={0} | all-to-all | bytes 262144 | tf_op jit(solution)/shard_map/all_to_all | solution.py:384
  73.4 10.0 %all_to_all.25 = f32[8,32,128]{2,1,0:T(8,128)S(1)} all-to-all(f32[8,32,128]{2,1,0:T(8,128)S(1)} %broadcast_in_dim.8), channel_id=1, replica_groups=mesh['y'=8,'x'=4,'core'=2,'panel'=8] {'x','core'}, dimensions={0} | all-to-all | bytes 262144 | tf_op jit(solution)/shard_map/all_to_all | solution.py:384
  83.5 13.7 %finish.1 = f32[1024,128]{1,0:T(8,128)} custom-call(s32[1]{0:T(128)} %bitcast.pos, f32[256,128]{1,0:T(8,128)S(1)} %bitcast.12, f32[1024,128]{1,0:T(8,128)S(1)} %get-tuple-element.13.w, bf16[1024,256]{1,0:T(8,128)(2,1)S(1)} %get-tuple-element.16.p01), custom_call_target="tpu_custom_call" | custom-call | tf_op jit(solution)/shard_map/finish/pallas_call | solution.py:372
  (10 shorter events, 0.2 us)
Async XLA Ops:
  1.8 14.5 %collective-permute-start = (bf16[528,128]{1,0:T(8,128)(2,1)}, bf16[528,128]{1,0:T(8,128)(2,1)S(1)}, u32[]{:S(2)}, u32[]{:S(2)}) collective-permute-start(bf16[528,128]{1,0:T(8,128)(2,1)} %get-tuple-element.11), channel_id=1, source_target_pairs={{0,8},{8,16},{16,24},{24,32},{32,40},{40,48},{48,56},{56,64},{64,7... | collective-permute-start | bytes 405512 | tf_op jit(solution)/shard_map/ppermute | solution.py:419
  6.3 10.0 %collective-permute-start.1 = (bf16[528,128]{1,0:T(8,128)(2,1)}, bf16[528,128]{1,0:T(8,128)(2,1)S(1)}, u32[]{:S(2)}, u32[]{:S(2)}) collective-permute-start(bf16[528,128]{1,0:T(8,128)(2,1)} %get-tuple-element.12), channel_id=1, source_target_pairs={{8,0},{16,8},{24,16},{32,24},{40,32},{48,40},{56,48},{64,56},{72,6... | collective-permute-start | bytes 405512 | tf_op jit(solution)/shard_map/ppermute | solution.py:420
  12.9 1.6 %copy-start = (bf16[8,256,256]{2,1,0:T(8,128)(2,1)S(1)}, bf16[8,256,256]{2,1,0:T(8,128)(2,1)}, u32[]{:S(2)}) copy-start(bf16[8,256,256]{2,1,0:T(8,128)(2,1)} %hop.1) | copy-start | bytes 3145732
  14.5 1.7 %copy-start.3 = (f32[1024,128]{1,0:T(8,128)S(1)}, f32[1024,128]{1,0:T(8,128)}, u32[]{:S(2)}) copy-start(f32[1024,128]{1,0:T(8,128)} %v.1) | copy-start | bytes 1572868
  14.9 1.4 %copy-start.1 = (s32[4,2]{0,1:T(2,128)S(1)}, s32[4,2]{0,1:T(2,128)}, u32[]{:S(2)}) copy-start(s32[4,2]{0,1:T(2,128)} %param.9) | copy-start | bytes 100
  14.9 1.4 %copy-start.2 = (s32[4]{0:T(128)S(1)}, s32[4]{0:T(128)}, u32[]{:S(2)}) copy-start(s32[4]{0:T(128)} %param.10) | copy-start | bytes 52
  18.8 8.6 %collective-permute-start.2 = (bf16[1024,128]{1,0:T(8,128)(2,1)S(1)}, bf16[1024,128]{1,0:T(8,128)(2,1)S(1)}, u32[]{:S(2)}, u32[]{:S(2)}) collective-permute-start(bf16[1024,128]{1,0:T(8,128)(2,1)S(1)} %get-tuple-element.14), channel_id=1, source_target_pairs={{0,3},{1,6},{8,11},{9,14},{16,19},{17,22},{24,27},{25,30},{32,35},... | collective-permute-start | bytes 786440 | tf_op jit(solution)/shard_map/ppermute | solution.py:403
  27.4 12.6 %collective-permute-start.3 = (bf16[1024,128]{1,0:T(8,128)(2,1)S(1)}, bf16[1024,128]{1,0:T(8,128)(2,1)S(1)}, u32[]{:S(2)}, u32[]{:S(2)}) collective-permute-start(bf16[1024,128]{1,0:T(8,128)(2,1)S(1)} %broadcast_select_fusion.own), channel_id=1, source_target_pairs={{0,7},{3,4},{1,2},{6,5},{8,15},{11,12},{9,10},{14,13},{16,23},{19,... | collective-permute-start | bytes 786440 | tf_op jit(solution)/shard_map/ppermute | solution.py:405
  28.8 11.6 %collective-permute-start.4 = (bf16[1024,128]{1,0:T(8,128)(2,1)S(1)}, bf16[1024,128]{1,0:T(8,128)(2,1)S(1)}, u32[]{:S(2)}, u32[]{:S(2)}) collective-permute-start(bf16[1024,128]{1,0:T(8,128)(2,1)S(1)} %broadcast_select_fusion.own), channel_id=1, source_target_pairs={{0,1},{3,2},{1,0},{6,7},{8,9},{11,10},{9,8},{14,15},{16,17},{19,18... | collective-permute-start | bytes 786440 | tf_op jit(solution)/shard_map/ppermute | solution.py:405
  34.9 10.7 %collective-permute-start.5 = (bf16[1024,128]{1,0:T(8,128)(2,1)S(1)}, bf16[1024,128]{1,0:T(8,128)(2,1)S(1)}, u32[]{:S(2)}, u32[]{:S(2)}) collective-permute-start(bf16[1024,128]{1,0:T(8,128)(2,1)S(1)} %broadcast_select_fusion.own), channel_id=1, source_target_pairs={{0,6},{3,5},{1,3},{6,4},{8,14},{11,13},{9,11},{14,12},{16,22},{19,... | collective-permute-start | bytes 786440 | tf_op jit(solution)/shard_map/ppermute | solution.py:405

commit v10 on v9

--- a/solution.py
+++ b/solution.py
@@ -18,10 +18,10 @@
 MISSING = 8
 STEPS = (
     [(0, 7), (3, 4), (1, 2), (6, 5)],
-    [(0, 1), (3, 2), (1, 0), (6, 7)],
-    [(0, 6), (3, 5), (1, 3), (6, 4)],
+    [(0, 1), (3, 5), (1, 0), (6, 4)],
+    [(0, 6), (3, 2), (1, 3), (6, 7)],
 )
-HELD = ((0, 2, 2, 0, 1, 3, 3, 1), (2, 0, 1, 3, 3, 1, 0, 2))
+HELD = ((0, 2, 3, 0, 1, 2, 3, 1), (2, 0, 1, 3, 2, 1, 0, 3))
 VM = pltpu.VMEM
 SM = pltpu.SMEM
 

time: 97.6 us -> 97.6 us (level)
  no operation moved by 1% of the time
where the time goes in v10:
time: 97.6 us; the launch traced here: 97.2 us
  blocking collectives  37.1 us (38%)
  starting transfers between devices  26.8 us (27%)
  Pallas kernels  18.6 us (19%)
  waiting for transfers between devices  10 us (10%)
  local copies, waits for them, and re-layouts  2.64 us (3%)
  between operations  1.55 us (2%)
    all_to_all x3, blocking collectives, swap(): return lax.all_to_all(x, axes, 0, 0, tiled=True)  37.1 us
    pallas_call x1, Pallas kernels, finish(): pl.pallas_call(finish_kernel, out_shape=jax.ShapeDtypeStruct(w.shape, F32...  13.7 us
    ppermute x3, starting transfers between devices, spread(): lax.ppermute(own, 'panel', pairs)  12.6 us
    ppermute x1, starting transfers between devices, body(): right = lax.ppermute(down, slab, [(i + 1, i) for i in range(count - 1)])  5.57 us
    ppermute x3, waiting for transfers between devices, spread(): lax.ppermute(own, 'panel', pairs)  5.54 us
    ppermute x1, starting transfers between devices, body(): left = lax.ppermute(up, slab, [(i, i + 1) for i in range(count - 1)])  4.5 us
    ppermute x1, waiting for transfers between devices, spread(): far = lax.ppermute(w_hi, 'panel', [(0, 3), (1, 6)])  4.46 us
    ppermute x1, starting transfers between devices, spread(): far = lax.ppermute(w_hi, 'panel', [(0, 3), (1, 6)])  4.16 us
  transfers between devices with their start and end apart: 6, of which 3 were waited for; matrix products, arithmetic and copies ran while one was open for 3% of the time, Pallas kernels for 0%

profile of v10, /device:TPU:1, one launch (start us, length us, event | category | flops | bytes accessed | tf_op | source)
XLA Modules:
  0.0 97.2 jit_solution(6537805716441705359)
XLA Ops:
  0.0 1.8 %pack.1 = (bf16[528,128]{1,0:T(8,128)(2,1)}, bf16[528,128]{1,0:T(8,128)(2,1)}) custom-call(f32[1024,128]{1,0:T(8,128)} %v.1, s32[2,4]{1,0:T(2,128)} %bitcast.16, s32[1,4]{1,0:T(1,128)} %bitcast.18), custom_call_target="tpu_custom_call" | custom-call | tf_op jit(solution)/shard_map/pack/pallas_call | solution.py:67
  1.8 4.5 %collective-permute-start = (bf16[528,128]{1,0:T(8,128)(2,1)}, bf16[528,128]{1,0:T(8,128)(2,1)S(1)}, u32[]{:S(2)}, u32[]{:S(2)}) collective-permute-start(bf16[528,128]{1,0:T(8,128)(2,1)} %get-tuple-element.11), channel_id=1, source_target_pairs={{0,8},{8,16},{16,24},{24,32},{32,40},{40,48},{48,56},{56,64},{64,7... | collective-permute-start | bytes 405512 | tf_op jit(solution)/shard_map/ppermute | solution.py:419
  6.3 5.6 %collective-permute-start.1 = (bf16[528,128]{1,0:T(8,128)(2,1)}, bf16[528,128]{1,0:T(8,128)(2,1)S(1)}, u32[]{:S(2)}, u32[]{:S(2)}) collective-permute-start(bf16[528,128]{1,0:T(8,128)(2,1)} %get-tuple-element.12), channel_id=1, source_target_pairs={{8,0},{16,8},{24,16},{32,24},{40,32},{48,40},{56,48},{64,56},{72,6... | collective-permute-start | bytes 405512 | tf_op jit(solution)/shard_map/ppermute | solution.py:420
  11.9 0.8 fusion.2
  12.7 0.1 copy.15
  12.8 0.1 copy.16
  12.9 0.0 copy-start
  13.0 1.6 %copy.14 = bf16[8,256,256]{1,2,0:T(8,128)(2,1)S(1)} copy(bf16[8,256,256]{2,1,0:T(8,128)(2,1)} %hop.1) | data formatting | bytes 2097152 | tf_op args[1]
  14.5 0.0 copy-done
  14.5 0.0 copy-start.3
  14.6 0.3 multiply_convert_fusion.sym
  14.9 0.0 copy-start.1
  14.9 0.0 copy-start.2
  16.2 0.0 copy-done.3
  16.3 0.0 collective-permute-done
  16.3 0.0 collective-permute-done.1
  16.3 0.0 copy-done.1
  16.3 0.0 copy-done.2
  16.3 2.4 %chebyshev.1 = (f32[1024,128]{1,0:T(8,128)S(1)}, bf16[1024,128]{1,0:T(8,128)(2,1)S(1)}) custom-call(s32[2,4]{1,0:T(2,128)S(1)} %bitcast.17, s32[1,4]{1,0:T(1,128)S(1)} %bitcast.19, f32[1]{0:T(128)S(6)} %copy.17.shift, f32[1]{0:T(128)} %copy.18.width, f32[1024,128]{1,0:T(8,128)S(1)} %broadcast_divide_fusion.base, ...), custom_call_target="tpu_custom_call" | custom-call | tf_op jit(solution)/shard_map/chebyshev/pallas_call | solution.py:164
  18.8 4.2 %collective-permute-start.2 = (bf16[1024,128]{1,0:T(8,128)(2,1)S(1)}, bf16[1024,128]{1,0:T(8,128)(2,1)S(1)}, u32[]{:S(2)}, u32[]{:S(2)}) collective-permute-start(bf16[1024,128]{1,0:T(8,128)(2,1)S(1)} %get-tuple-element.14), channel_id=1, source_target_pairs={{0,3},{1,6},{8,11},{9,14},{16,19},{17,22},{24,27},{25,30},{32,35},... | collective-permute-start | bytes 786440 | tf_op jit(solution)/shard_map/ppermute | solution.py:403
  22.9 4.5 %collective-permute-done.2 = bf16[1024,128]{1,0:T(8,128)(2,1)S(1)} collective-permute-done((bf16[1024,128]{1,0:T(8,128)(2,1)S(1)}, bf16[1024,128]{1,0:T(8,128)(2,1)S(1)}, u32[]{:S(2)}, u32[]{:S(2)}) %collective-permute-start.2) | collective-permute-done | bytes 262176 | tf_op jit(solution)/shard_map/ppermute | solution.py:403
  27.4 1.3 %collective-permute-start.3 = (bf16[1024,128]{1,0:T(8,128)(2,1)S(1)}, bf16[1024,128]{1,0:T(8,128)(2,1)S(1)}, u32[]{:S(2)}, u32[]{:S(2)}) collective-permute-start(bf16[1024,128]{1,0:T(8,128)(2,1)S(1)} %broadcast_select_fusion.own), channel_id=1, source_target_pairs={{0,7},{3,4},{1,2},{6,5},{8,15},{11,12},{9,10},{14,13},{16,23},{19,... | collective-permute-start | bytes 786440 | tf_op jit(solution)/shard_map/ppermute | solution.py:405
  28.8 6.2 %collective-permute-start.4 = (bf16[1024,128]{1,0:T(8,128)(2,1)S(1)}, bf16[1024,128]{1,0:T(8,128)(2,1)S(1)}, u32[]{:S(2)}, u32[]{:S(2)}) collective-permute-start(bf16[1024,128]{1,0:T(8,128)(2,1)S(1)} %broadcast_select_fusion.own), channel_id=1, source_target_pairs={{0,1},{3,5},{1,0},{6,4},{8,9},{11,13},{9,8},{14,12},{16,17},{19,21... | collective-permute-start | bytes 786440 | tf_op jit(solution)/shard_map/ppermute | solution.py:405
  34.9 5.1 %collective-permute-start.5 = (bf16[1024,128]{1,0:T(8,128)(2,1)S(1)}, bf16[1024,128]{1,0:T(8,128)(2,1)S(1)}, u32[]{:S(2)}, u32[]{:S(2)}) collective-permute-start(bf16[1024,128]{1,0:T(8,128)(2,1)S(1)} %broadcast_select_fusion.own), channel_id=1, source_target_pairs={{0,6},{3,2},{1,3},{6,7},{8,14},{11,10},{9,11},{14,15},{16,22},{19,... | collective-permute-start | bytes 786440 | tf_op jit(solution)/shard_map/ppermute | solution.py:405
  40.1 0.0 collective-permute-done.3.first
  40.1 0.3 collective-permute-done.4.second
  40.3 5.3 %collective-permute-done.5.third = bf16[1024,128]{1,0:T(8,128)(2,1)S(1)} collective-permute-done((bf16[1024,128]{1,0:T(8,128)(2,1)S(1)}, bf16[1024,128]{1,0:T(8,128)(2,1)S(1)}, u32[]{:S(2)}, u32[]{:S(2)}) %collective-permute-start.5) | collective-permute-done | bytes 262176 | tf_op jit(solution)/shard_map/ppermute | solution.py:405
  45.6 0.7 gram.1
  46.3 12.4 %all_to_all.23 = f32[8,32,128]{2,1,0:T(8,128)S(1)} all-to-all(f32[8,32,128]{2,1,0:T(8,128)S(1)} %bitcast.15), channel_id=1, replica_groups=mesh['y'=8,'x'=4,'core'=2,'panel'=8] {'x','core'}, dimensions={0} | all-to-all | bytes 262144 | tf_op jit(solution)/shard_map/all_to_all | solution.py:384
  58.7 14.7 %all_to_all.24 = f32[8,32,128]{2,1,0:T(8,128)S(1)} all-to-all(f32[8,32,128]{2,1,0:T(8,128)S(1)} %broadcast_in_dim.7), channel_id=1, replica_groups=mesh['y'=8,'x'=4,'core'=2,'panel'=8] {'y'}, dimensions={0} | all-to-all | bytes 262144 | tf_op jit(solution)/shard_map/all_to_all | solution.py:384
  73.4 10.0 %all_to_all.25 = f32[8,32,128]{2,1,0:T(8,128)S(1)} all-to-all(f32[8,32,128]{2,1,0:T(8,128)S(1)} %broadcast_in_dim.8), channel_id=1, replica_groups=mesh['y'=8,'x'=4,'core'=2,'panel'=8] {'x','core'}, dimensions={0} | all-to-all | bytes 262144 | tf_op jit(solution)/shard_map/all_to_all | solution.py:384
  83.5 13.7 %finish.1 = f32[1024,128]{1,0:T(8,128)} custom-call(s32[1]{0:T(128)} %bitcast.pos, f32[256,128]{1,0:T(8,128)S(1)} %bitcast.12, f32[1024,128]{1,0:T(8,128)S(1)} %get-tuple-element.13.w, bf16[1024,256]{1,0:T(8,128)(2,1)S(1)} %get-tuple-element.16.p01), custom_call_target="tpu_custom_call" | custom-call | tf_op jit(solution)/shard_map/finish/pallas_call | solution.py:372
  (10 shorter events, 0.2 us)
Async XLA Ops:
  1.8 14.5 %collective-permute-start = (bf16[528,128]{1,0:T(8,128)(2,1)}, bf16[528,128]{1,0:T(8,128)(2,1)S(1)}, u32[]{:S(2)}, u32[]{:S(2)}) collective-permute-start(bf16[528,128]{1,0:T(8,128)(2,1)} %get-tuple-element.11), channel_id=1, source_target_pairs={{0,8},{8,16},{16,24},{24,32},{32,40},{40,48},{48,56},{56,64},{64,7... | collective-permute-start | bytes 405512 | tf_op jit(solution)/shard_map/ppermute | solution.py:419
  6.3 10.0 %collective-permute-start.1 = (bf16[528,128]{1,0:T(8,128)(2,1)}, bf16[528,128]{1,0:T(8,128)(2,1)S(1)}, u32[]{:S(2)}, u32[]{:S(2)}) collective-permute-start(bf16[528,128]{1,0:T(8,128)(2,1)} %get-tuple-element.12), channel_id=1, source_target_pairs={{8,0},{16,8},{24,16},{32,24},{40,32},{48,40},{56,48},{64,56},{72,6... | collective-permute-start | bytes 405512 | tf_op jit(solution)/shard_map/ppermute | solution.py:420
  12.9 1.6 %copy-start = (bf16[8,256,256]{2,1,0:T(8,128)(2,1)S(1)}, bf16[8,256,256]{2,1,0:T(8,128)(2,1)}, u32[]{:S(2)}) copy-start(bf16[8,256,256]{2,1,0:T(8,128)(2,1)} %hop.1) | copy-start | bytes 3145732
  14.5 1.7 %copy-start.3 = (f32[1024,128]{1,0:T(8,128)S(1)}, f32[1024,128]{1,0:T(8,128)}, u32[]{:S(2)}) copy-start(f32[1024,128]{1,0:T(8,128)} %v.1) | copy-start | bytes 1572868
  14.9 1.4 %copy-start.1 = (s32[4,2]{0,1:T(2,128)S(1)}, s32[4,2]{0,1:T(2,128)}, u32[]{:S(2)}) copy-start(s32[4,2]{0,1:T(2,128)} %param.9) | copy-start | bytes 100
  14.9 1.4 %copy-start.2 = (s32[4]{0:T(128)S(1)}, s32[4]{0:T(128)}, u32[]{:S(2)}) copy-start(s32[4]{0:T(128)} %param.10) | copy-start | bytes 52
  18.8 8.6 %collective-permute-start.2 = (bf16[1024,128]{1,0:T(8,128)(2,1)S(1)}, bf16[1024,128]{1,0:T(8,128)(2,1)S(1)}, u32[]{:S(2)}, u32[]{:S(2)}) collective-permute-start(bf16[1024,128]{1,0:T(8,128)(2,1)S(1)} %get-tuple-element.14), channel_id=1, source_target_pairs={{0,3},{1,6},{8,11},{9,14},{16,19},{17,22},{24,27},{25,30},{32,35},... | collective-permute-start | bytes 786440 | tf_op jit(solution)/shard_map/ppermute | solution.py:403
  27.4 12.6 %collective-permute-start.3 = (bf16[1024,128]{1,0:T(8,128)(2,1)S(1)}, bf16[1024,128]{1,0:T(8,128)(2,1)S(1)}, u32[]{:S(2)}, u32[]{:S(2)}) collective-permute-start(bf16[1024,128]{1,0:T(8,128)(2,1)S(1)} %broadcast_select_fusion.own), channel_id=1, source_target_pairs={{0,7},{3,4},{1,2},{6,5},{8,15},{11,12},{9,10},{14,13},{16,23},{19,... | collective-permute-start | bytes 786440 | tf_op jit(solution)/shard_map/ppermute | solution.py:405
  28.8 11.6 %collective-permute-start.4 = (bf16[1024,128]{1,0:T(8,128)(2,1)S(1)}, bf16[1024,128]{1,0:T(8,128)(2,1)S(1)}, u32[]{:S(2)}, u32[]{:S(2)}) collective-permute-start(bf16[1024,128]{1,0:T(8,128)(2,1)S(1)} %broadcast_select_fusion.own), channel_id=1, source_target_pairs={{0,1},{3,5},{1,0},{6,4},{8,9},{11,13},{9,8},{14,12},{16,17},{19,21... | collective-permute-start | bytes 786440 | tf_op jit(solution)/shard_map/ppermute | solution.py:405
  34.9 10.7 %collective-permute-start.5 = (bf16[1024,128]{1,0:T(8,128)(2,1)S(1)}, bf16[1024,128]{1,0:T(8,128)(2,1)S(1)}, u32[]{:S(2)}, u32[]{:S(2)}) collective-permute-start(bf16[1024,128]{1,0:T(8,128)(2,1)S(1)} %broadcast_select_fusion.own), channel_id=1, source_target_pairs={{0,6},{3,2},{1,3},{6,7},{8,14},{11,10},{9,11},{14,15},{16,22},{19,... | collective-permute-start | bytes 786440 | tf_op jit(solution)/shard_map/ppermute | solution.py:405

commit v11 on v10

--- a/solution.py
+++ b/solution.py
@@ -75,7 +75,7 @@
 
 
 def filter_kernel(
-    kinds, phase, shift, width, base, sides, hop, hop_t, sym, cos_t, sin_t,
+    kinds, phase, shift, width, base, sides, hop, hop_t, sym, waves,
     w, w_hi, vb, cosb, sinb, z, y1, y1b,
 ):
     half = base.shape[0] // 2
@@ -83,7 +83,10 @@
     centre = shift[0]
     h = jnp.broadcast_to(width[0], (1, WIDE))
     inv_h = 1.0 / h
-    pick = lax.broadcasted_iota(jnp.int32, (cos_t.shape[1], WIDE), 0) % 16
+    pick = lax.broadcasted_iota(jnp.int32, (waves.shape[1], 2 * WIDE), 0)
+    side = lax.broadcasted_iota(jnp.int32, (waves.shape[1], 2 * WIDE), 1)
+    same = (pick < waves.shape[1] // 2) == (side < WIDE)
+    pick = pick % 16
     tile_l = left[half : half + META, :].astype(F32)
     tile_r = right[half : half + META, :].astype(F32)
     row = lax.broadcasted_iota(jnp.int32, (META, WIDE), 0)
@@ -112,9 +115,10 @@
         return jnp.where(kind < MISSING, 1.0, 0.0).astype(F32)
 
     for r in range(-2, 5):
-        hot = jnp.where(pick == pattern[r], 1.0, 0.0).astype(BF16)
-        cosb[r + 2] = dot(cos_t[...], hot)
-        sinb[r + 2] = dot(sin_t[...], hot)
+        hot = jnp.where(same & (pick == pattern[r]), 1.0, 0.0).astype(BF16)
+        both = dot(waves[...], hot)
+        cosb[r + 2] = both[:, :WIDE]
+        sinb[r + 2] = both[:, WIDE:]
 
     def v_row(r):
         if r < 0:
@@ -164,7 +168,7 @@
     return pl.pallas_call(
         filter_kernel,
         out_shape=(jax.ShapeDtypeStruct(args[4].shape, F32), jax.ShapeDtypeStruct(args[4].shape, BF16)),
-        in_specs=[smem] * 4 + [spec] * 7,
+        in_specs=[smem] * 4 + [spec] * 6,
         out_specs=(spec, spec),
         scratch_shapes=[
             VM(args[4].shape, BF16),
@@ -408,7 +412,7 @@
 def thirds(x):
     a = lax.reduce_precision(x, 8, 7)
     b = lax.reduce_precision(x - a, 8, 7)
-    return jnp.concatenate([a, b, x - a - b], axis=0).astype(BF16).T
+    return [a, b, x - a - b]
 
 
 def body(vectors, hop_table, block_kind, block_phase, phase_angles, centre, half_width):
@@ -423,10 +427,10 @@
     wide = hop_table.astype(F32)
     turned = jnp.transpose(hop_table, (0, 2, 1))
     sym = ((wide + turned.astype(F32)) * 0.5).astype(BF16)
-    cos_t = thirds(jnp.cos(phase_angles))
-    sin_t = thirds(jnp.sin(phase_angles))
+    parts = thirds(jnp.cos(phase_angles)) + thirds(jnp.sin(phase_angles))
+    waves = jnp.concatenate(parts, axis=0).astype(BF16).T
     w, w_hi = chebyshev(
-        kinds, phase, centre, half_width, base, sides, hop_table, turned, sym, cos_t, sin_t
+        kinds, phase, centre, half_width, base, sides, hop_table, turned, sym, waves
     )
     pos = lax.axis_index("panel").astype(jnp.int32)
     spot = pos.reshape(1)

time: 97.6 us -> 100 us (1.025)
  blocking collectives: 37.1 us -> 34.1 us
  other arithmetic: 0.45 us -> 3.19 us
  local copies, waits for them, and re-layouts: 2.64 us -> 4.52 us
  waiting for transfers between devices: 10 us -> 11.1 us
    all_to_all x3, blocking collectives: 37.1 us -> 34.1 us  [swap(): return lax.all_to_all(x, axes, 0, 0, tiled=True)]
    div x1, other arithmetic: 0.04 us -> 1.09 us  [body(): base = vectors / half_width[0]]
    unnamed x9 -> x11, local copies, waits for them, and re-layouts: 1.59 us -> 2.37 us
  transfers between devices with their start and end apart: 6 -> 6, of which waited for: 3 -> 3; matrix products, arithmetic and copies ran while one was open for 3% -> 6% of each run, Pallas kernels for 0% -> 0%
where the time goes in v11:
time: 100 us; the launch traced here: 99.7 us
  blocking collectives  34.1 us (34%)
  starting transfers between devices  26.8 us (27%)
  Pallas kernels  18.5 us (18%)
  waiting for transfers between devices  11.1 us (11%)
  local copies, waits for them, and re-layouts  4.52 us (5%)
  other arithmetic  3.19 us (3%)
  between operations  1.49 us (1%)
    all_to_all x3, blocking collectives, swap(): return lax.all_to_all(x, axes, 0, 0, tiled=True)  34.1 us
    pallas_call x1, Pallas kernels, finish(): pl.pallas_call(finish_kernel, out_shape=jax.ShapeDtypeStruct(w.shape, F32...  13.7 us
    ppermute x3, starting transfers between devices, spread(): lax.ppermute(own, 'panel', pairs)  12.6 us
    ppermute x1, starting transfers between devices, body(): right = lax.ppermute(down, slab, [(i + 1, i) for i in range(count - 1)])  6.22 us
    ppermute x3, waiting for transfers between devices, spread(): lax.ppermute(own, 'panel', pairs)  5.77 us
    ppermute x1, waiting for transfers between devices, spread(): far = lax.ppermute(w_hi, 'panel', [(0, 3), (1, 6)])  5.29 us
    ppermute x1, starting transfers between devices, body(): left = lax.ppermute(up, slab, [(i, i + 1) for i in range(count - 1)])  4.5 us
    ppermute x1, starting transfers between devices, spread(): far = lax.ppermute(w_hi, 'panel', [(0, 3), (1, 6)])  3.46 us
  transfers between devices with their start and end apart: 6, of which 3 were waited for; matrix products, arithmetic and copies ran while one was open for 6% of the time, Pallas kernels for 0%

profile of v11, /device:TPU:1, one launch (start us, length us, event | category | flops | bytes accessed | tf_op | source)
XLA Modules:
  0.0 99.7 jit_solution(10281324721642219895)
XLA Ops:
  0.0 1.8 %pack.1 = (bf16[528,128]{1,0:T(8,128)(2,1)}, bf16[528,128]{1,0:T(8,128)(2,1)}) custom-call(f32[1024,128]{1,0:T(8,128)} %v.1, s32[2,4]{1,0:T(2,128)} %bitcast.14, s32[1,4]{1,0:T(1,128)} %bitcast.16), custom_call_target="tpu_custom_call" | custom-call | tf_op jit(solution)/shard_map/pack/pallas_call | solution.py:67
  1.8 4.5 %collective-permute-start = (bf16[528,128]{1,0:T(8,128)(2,1)}, bf16[528,128]{1,0:T(8,128)(2,1)}, u32[]{:S(2)}, u32[]{:S(2)}) collective-permute-start(bf16[528,128]{1,0:T(8,128)(2,1)} %get-tuple-element.11), channel_id=1, source_target_pairs={{0,8},{8,16},{16,24},{24,32},{32,40},{40,48},{48,56},{56,64},{64,7... | collective-permute-start | bytes 405512 | tf_op jit(solution)/shard_map/ppermute | solution.py:423
  6.3 6.2 %collective-permute-start.1 = (bf16[528,128]{1,0:T(8,128)(2,1)}, bf16[528,128]{1,0:T(8,128)(2,1)}, u32[]{:S(2)}, u32[]{:S(2)}) collective-permute-start(bf16[528,128]{1,0:T(8,128)(2,1)} %get-tuple-element.12), channel_id=1, source_target_pairs={{8,0},{16,8},{24,16},{32,24},{40,32},{48,40},{56,48},{64,56},{72,6... | collective-permute-start | bytes 405512 | tf_op jit(solution)/shard_map/ppermute | solution.py:424
  12.5 0.8 fusion.2
  13.3 0.1 copy.15
  13.4 0.1 copy.17
  13.5 0.0 copy-start
  13.5 1.6 %copy.14 = bf16[8,256,256]{1,2,0:T(8,128)(2,1)S(1)} copy(bf16[8,256,256]{2,1,0:T(8,128)(2,1)} %hop.1) | data formatting | bytes 2097152 | tf_op args[1]
  15.1 0.0 copy-done
  15.1 0.3 multiply_convert_fusion.sym
  16.7 0.7 fusion
  17.5 0.0 copy-start.3
  17.5 0.0 copy-start.4
  17.5 1.1 %concatenate.8 = bf16[96,256]{0,1:T(8,128)(2,1)S(1)} concatenate(bf16[16,256]{0,1:T(8,128)(2,1)} %get-tuple-element.22, bf16[16,256]{0,1:T(8,128)(2,1)S(1)} %get-tuple-element.21, bf16[16,256]{0,1:T(8,128)(2,1)S(1)} %get-tuple-element.20, bf16[16,256]{0,1:T(8,128)(2,1)} %get-tuple-element.25, bf16[16,256]{0,1:T(8,128)(2,1)} %get-tuple-element.26, bf16[16,256]{0,1:T(8,128)(2,1)} %get-tuple-element.27), dimensions={0} | concatenate | bytes 98304 | tf_op jit(solution)/shard_map/concatenate | solution.py:431
  18.6 1.1 %broadcast_divide_fusion.base = f32[1024,128]{1,0:T(8,128)S(1)} fusion(f32[1024,128]{1,0:T(8,128)} %v.1, f32[]{:T(128)} %bitcast.9), kind=kLoop, calls=%fused_computation.2 | loop fusion | flops 131072 | bytes 1048580 | tf_op jit(solution)/shard_map/div | solution.py:425
  19.7 0.0 collective-permute-done
  19.7 0.0 collective-permute-done.1
  19.7 1.0 pad_maximum_fusion.sides
  20.7 0.0 copy-done.3
  20.7 0.0 copy-done.4
  20.7 2.3 %chebyshev.1 = (f32[1024,128]{1,0:T(8,128)S(1)}, bf16[1024,128]{1,0:T(8,128)(2,1)S(1)}) custom-call(s32[2,4]{1,0:T(2,128)S(1)} %bitcast.15, s32[1,4]{1,0:T(1,128)S(1)} %bitcast.17, f32[1]{0:T(128)S(6)} %copy.19.shift, f32[1]{0:T(128)} %copy.20.width, f32[1024,128]{1,0:T(8,128)S(1)} %broadcast_divide_fusion.base, ...), custom_call_target="tpu_custom_call" | custom-call | tf_op jit(solution)/shard_map/chebyshev/pallas_call | solution.py:168
  23.1 0.0 copy-start.1
  23.1 0.8 copy-done.1
  23.9 0.0 copy-start.2
  23.9 3.5 %collective-permute-start.2 = (bf16[1024,128]{1,0:T(8,128)(2,1)S(1)}, bf16[1024,128]{1,0:T(8,128)(2,1)S(1)}, u32[]{:S(2)}, u32[]{:S(2)}) collective-permute-start(bf16[1024,128]{1,0:T(8,128)(2,1)S(1)} %get-tuple-element.14), channel_id=1, source_target_pairs={{0,3},{1,6},{8,11},{9,14},{16,19},{17,22},{24,27},{25,30},{32,35},... | collective-permute-start | bytes 786440 | tf_op jit(solution)/shard_map/ppermute | solution.py:407
  27.4 5.3 %collective-permute-done.2 = bf16[1024,128]{1,0:T(8,128)(2,1)S(1)} collective-permute-done((bf16[1024,128]{1,0:T(8,128)(2,1)S(1)}, bf16[1024,128]{1,0:T(8,128)(2,1)S(1)}, u32[]{:S(2)}, u32[]{:S(2)}) %collective-permute-start.2) | collective-permute-done | bytes 262176 | tf_op jit(solution)/shard_map/ppermute | solution.py:407
  32.7 1.3 %collective-permute-start.3 = (bf16[1024,128]{1,0:T(8,128)(2,1)S(1)}, bf16[1024,128]{1,0:T(8,128)(2,1)S(1)}, u32[]{:S(2)}, u32[]{:S(2)}) collective-permute-start(bf16[1024,128]{1,0:T(8,128)(2,1)S(1)} %broadcast_select_fusion.own), channel_id=1, source_target_pairs={{0,7},{3,4},{1,2},{6,5},{8,15},{11,12},{9,10},{14,13},{16,23},{19,... | collective-permute-start | bytes 786440 | tf_op jit(solution)/shard_map/ppermute | solution.py:409
  34.0 6.2 %collective-permute-start.4 = (bf16[1024,128]{1,0:T(8,128)(2,1)S(1)}, bf16[1024,128]{1,0:T(8,128)(2,1)S(1)}, u32[]{:S(2)}, u32[]{:S(2)}) collective-permute-start(bf16[1024,128]{1,0:T(8,128)(2,1)S(1)} %broadcast_select_fusion.own), channel_id=1, source_target_pairs={{0,1},{3,5},{1,0},{6,4},{8,9},{11,13},{9,8},{14,12},{16,17},{19,21... | collective-permute-start | bytes 786440 | tf_op jit(solution)/shard_map/ppermute | solution.py:409
  40.2 5.1 %collective-permute-start.5 = (bf16[1024,128]{1,0:T(8,128)(2,1)S(1)}, bf16[1024,128]{1,0:T(8,128)(2,1)S(1)}, u32[]{:S(2)}, u32[]{:S(2)}) collective-permute-start(bf16[1024,128]{1,0:T(8,128)(2,1)S(1)} %broadcast_select_fusion.own), channel_id=1, source_target_pairs={{0,6},{3,2},{1,3},{6,7},{8,14},{11,10},{9,11},{14,15},{16,22},{19,... | collective-permute-start | bytes 786440 | tf_op jit(solution)/shard_map/ppermute | solution.py:409
  45.3 0.0 collective-permute-done.3.first
  45.3 1.3 %collective-permute-done.4.second = bf16[1024,128]{1,0:T(8,128)(2,1)S(1)} collective-permute-done((bf16[1024,128]{1,0:T(8,128)(2,1)S(1)}, bf16[1024,128]{1,0:T(8,128)(2,1)S(1)}, u32[]{:S(2)}, u32[]{:S(2)}) %collective-permute-start.4) | collective-permute-done | bytes 262176 | tf_op jit(solution)/shard_map/ppermute | solution.py:409
  46.6 4.4 %collective-permute-done.5.third = bf16[1024,128]{1,0:T(8,128)(2,1)S(1)} collective-permute-done((bf16[1024,128]{1,0:T(8,128)(2,1)S(1)}, bf16[1024,128]{1,0:T(8,128)(2,1)S(1)}, u32[]{:S(2)}, u32[]{:S(2)}) %collective-permute-start.5) | collective-permute-done | bytes 262176 | tf_op jit(solution)/shard_map/ppermute | solution.py:409
  51.1 0.0 copy-done.2
  51.1 0.7 gram.1
  51.8 9.7 %all_to_all.23 = f32[8,32,128]{2,1,0:T(8,128)S(1)} all-to-all(f32[8,32,128]{2,1,0:T(8,128)S(1)} %bitcast.13), channel_id=1, replica_groups=mesh['y'=8,'x'=4,'core'=2,'panel'=8] {'x','core'}, dimensions={0} | all-to-all | bytes 262144 | tf_op jit(solution)/shard_map/all_to_all | solution.py:388
  61.5 14.4 %all_to_all.24 = f32[8,32,128]{2,1,0:T(8,128)S(1)} all-to-all(f32[8,32,128]{2,1,0:T(8,128)S(1)} %broadcast_in_dim.7), channel_id=1, replica_groups=mesh['y'=8,'x'=4,'core'=2,'panel'=8] {'y'}, dimensions={0} | all-to-all | bytes 262144 | tf_op jit(solution)/shard_map/all_to_all | solution.py:388
  76.0 10.0 %all_to_all.25 = f32[8,32,128]{2,1,0:T(8,128)S(1)} all-to-all(f32[8,32,128]{2,1,0:T(8,128)S(1)} %broadcast_in_dim.8), channel_id=1, replica_groups=mesh['y'=8,'x'=4,'core'=2,'panel'=8] {'x','core'}, dimensions={0} | all-to-all | bytes 262144 | tf_op jit(solution)/shard_map/all_to_all | solution.py:388
  86.0 13.7 %finish.1 = f32[1024,128]{1,0:T(8,128)} custom-call(s32[1]{0:T(128)} %bitcast.pos, f32[256,128]{1,0:T(8,128)S(1)} %bitcast.11, f32[1024,128]{1,0:T(8,128)S(1)} %copy-done.2, bf16[1024,256]{1,0:T(8,128)(2,1)S(1)} %get-tuple-element.16.p01), custom_call_target="tpu_custom_call" | custom-call | tf_op jit(solution)/shard_map/finish/pallas_call | solution.py:376
  (5 shorter events, 0.1 us)
Async XLA Ops:
  1.8 17.9 %collective-permute-start = (bf16[528,128]{1,0:T(8,128)(2,1)}, bf16[528,128]{1,0:T(8,128)(2,1)}, u32[]{:S(2)}, u32[]{:S(2)}) collective-permute-start(bf16[528,128]{1,0:T(8,128)(2,1)} %get-tuple-element.11), channel_id=1, source_target_pairs={{0,8},{8,16},{16,24},{24,32},{32,40},{40,48},{48,56},{56,64},{64,7... | collective-permute-start | bytes 405512 | tf_op jit(solution)/shard_map/ppermute | solution.py:423
  6.3 13.4 %collective-permute-start.1 = (bf16[528,128]{1,0:T(8,128)(2,1)}, bf16[528,128]{1,0:T(8,128)(2,1)}, u32[]{:S(2)}, u32[]{:S(2)}) collective-permute-start(bf16[528,128]{1,0:T(8,128)(2,1)} %get-tuple-element.12), channel_id=1, source_target_pairs={{8,0},{16,8},{24,16},{32,24},{40,32},{48,40},{56,48},{64,56},{72,6... | collective-permute-start | bytes 405512 | tf_op jit(solution)/shard_map/ppermute | solution.py:424
  13.5 1.6 %copy-start = (bf16[8,256,256]{2,1,0:T(8,128)(2,1)S(1)}, bf16[8,256,256]{2,1,0:T(8,128)(2,1)}, u32[]{:S(2)}) copy-start(bf16[8,256,256]{2,1,0:T(8,128)(2,1)} %hop.1) | copy-start | bytes 3145732
  17.5 3.2 %copy-start.3 = (s32[4,2]{0,1:T(2,128)S(1)}, s32[4,2]{0,1:T(2,128)}, u32[]{:S(2)}) copy-start(s32[4,2]{0,1:T(2,128)} %param.9) | copy-start | bytes 100
  17.5 3.3 %copy-start.4 = (s32[4]{0:T(128)S(1)}, s32[4]{0:T(128)}, u32[]{:S(2)}) copy-start(s32[4]{0:T(128)} %param.10) | copy-start | bytes 52
  23.1 0.8 copy-start.1
  23.9 27.2 %copy-start.2 = (f32[1024,128]{1,0:T(8,128)S(1)}, f32[1024,128]{1,0:T(8,128)}, u32[]{:S(2)}) copy-start(f32[1024,128]{1,0:T(8,128)} %copy-done.1) | copy-start | bytes 1572868
  23.9 8.8 %collective-permute-start.2 = (bf16[1024,128]{1,0:T(8,128)(2,1)S(1)}, bf16[1024,128]{1,0:T(8,128)(2,1)S(1)}, u32[]{:S(2)}, u32[]{:S(2)}) collective-permute-start(bf16[1024,128]{1,0:T(8,128)(2,1)S(1)} %get-tuple-element.14), channel_id=1, source_target_pairs={{0,3},{1,6},{8,11},{9,14},{16,19},{17,22},{24,27},{25,30},{32,35},... | collective-permute-start | bytes 786440 | tf_op jit(solution)/shard_map/ppermute | solution.py:407
  32.7 12.6 %collective-permute-start.3 = (bf16[1024,128]{1,0:T(8,128)(2,1)S(1)}, bf16[1024,128]{1,0:T(8,128)(2,1)S(1)}, u32[]{:S(2)}, u32[]{:S(2)}) collective-permute-start(bf16[1024,128]{1,0:T(8,128)(2,1)S(1)} %broadcast_select_fusion.own), channel_id=1, source_target_pairs={{0,7},{3,4},{1,2},{6,5},{8,15},{11,12},{9,10},{14,13},{16,23},{19,... | collective-permute-start | bytes 786440 | tf_op jit(solution)/shard_map/ppermute | solution.py:409
  34.0 12.6 %collective-permute-start.4 = (bf16[1024,128]{1,0:T(8,128)(2,1)S(1)}, bf16[1024,128]{1,0:T(8,128)(2,1)S(1)}, u32[]{:S(2)}, u32[]{:S(2)}) collective-permute-start(bf16[1024,128]{1,0:T(8,128)(2,1)S(1)} %broadcast_select_fusion.own), channel_id=1, source_target_pairs={{0,1},{3,5},{1,0},{6,4},{8,9},{11,13},{9,8},{14,12},{16,17},{19,21... | collective-permute-start | bytes 786440 | tf_op jit(solution)/shard_map/ppermute | solution.py:409
  40.2 10.9 %collective-permute-start.5 = (bf16[1024,128]{1,0:T(8,128)(2,1)S(1)}, bf16[1024,128]{1,0:T(8,128)(2,1)S(1)}, u32[]{:S(2)}, u32[]{:S(2)}) collective-permute-start(bf16[1024,128]{1,0:T(8,128)(2,1)S(1)} %broadcast_select_fusion.own), channel_id=1, source_target_pairs={{0,6},{3,2},{1,3},{6,7},{8,14},{11,10},{9,11},{14,15},{16,22},{19,... | collective-permute-start | bytes 786440 | tf_op jit(solution)/shard_map/ppermute | solution.py:409

commit v12 on v10

--- a/solution.py
+++ b/solution.py
@@ -17,11 +17,11 @@
 META = 16
 MISSING = 8
 STEPS = (
-    [(0, 7), (3, 4), (1, 2), (6, 5)],
-    [(0, 1), (3, 5), (1, 0), (6, 4)],
-    [(0, 6), (3, 2), (1, 3), (6, 7)],
+    [(0, 7), (1, 2), (5, 6), (4, 3)],
+    [(0, 1), (1, 0), (5, 3), (4, 6)],
+    [(0, 2), (1, 7), (5, 4), (4, 5)],
 )
-HELD = ((0, 2, 3, 0, 1, 2, 3, 1), (2, 0, 1, 3, 2, 1, 0, 3))
+HELD = ((0, 2, 3, 2, 3, 0, 1, 1), (2, 0, 1, 1, 0, 3, 2, 3))
 VM = pltpu.VMEM
 SM = pltpu.SMEM
 
@@ -400,8 +400,8 @@
 
 
 def spread(w_hi, pos):
-    far = lax.ppermute(w_hi, "panel", [(0, 3), (1, 6)])
-    own = jnp.where((pos == 3) | (pos == 6), far, w_hi)
+    far = lax.ppermute(w_hi, "panel", [(0, 5), (1, 4)])
+    own = jnp.where((pos == 5) | (pos == 4), far, w_hi)
     return (own,) + tuple(lax.ppermute(own, "panel", pairs) for pairs in STEPS)
 
 

time: 97.6 us -> 97.2 us (level)
  starting transfers between devices: 26.8 us -> 22.1 us
  waiting for transfers between devices: 10 us -> 14 us
    ppermute x3, starting transfers between devices: 12.6 us -> 4.79 us  [spread(): lax.ppermute(own, 'panel', pairs)]
    ppermute x3, waiting for transfers between devices: 5.54 us -> 9.57 us  [spread(): lax.ppermute(own, 'panel', pairs)]
    ppermute x1, starting transfers between devices: 4.16 us -> 7.2 us  [spread(): far = lax.ppermute(w_hi, 'panel', [(0, 5), (1, 4)])]
  transfers between devices with their start and end apart: 6 -> 6, of which waited for: 3 -> 4; matrix products, arithmetic and copies ran while one was open for 3% -> 3% of each run, Pallas kernels for 0% -> 0%
where the time goes in v12:
time: 97.2 us; the launch traced here: 96.7 us
  blocking collectives  37.4 us (38%)
  starting transfers between devices  22.1 us (23%)
  Pallas kernels  18.6 us (19%)
  waiting for transfers between devices  14 us (14%)
  local copies, waits for them, and re-layouts  2.64 us (3%)
  between operations  1.54 us (2%)
    all_to_all x3, blocking collectives, swap(): return lax.all_to_all(x, axes, 0, 0, tiled=True)  37.4 us
    pallas_call x1, Pallas kernels, finish(): pl.pallas_call(finish_kernel, out_shape=jax.ShapeDtypeStruct(w.shape, F32...  13.7 us
    ppermute x3, waiting for transfers between devices, spread(): lax.ppermute(own, 'panel', pairs)  9.57 us
    ppermute x1, starting transfers between devices, spread(): far = lax.ppermute(w_hi, 'panel', [(0, 5), (1, 4)])  7.2 us
    ppermute x1, starting transfers between devices, body(): right = lax.ppermute(down, slab, [(i + 1, i) for i in range(count - 1)])  5.57 us
    ppermute x3, starting transfers between devices, spread(): lax.ppermute(own, 'panel', pairs)  4.79 us
    ppermute x1, starting transfers between devices, body(): left = lax.ppermute(up, slab, [(i, i + 1) for i in range(count - 1)])  4.5 us
    ppermute x1, waiting for transfers between devices, spread(): far = lax.ppermute(w_hi, 'panel', [(0, 5), (1, 4)])  4.46 us
  transfers between devices with their start and end apart: 6, of which 4 were waited for; matrix products, arithmetic and copies ran while one was open for 3% of the time, Pallas kernels for 0%

profile of v12, /device:TPU:1, one launch (start us, length us, event | category | flops | bytes accessed | tf_op | source)
XLA Modules:
  0.0 96.7 jit_solution(12048234350488372002)
XLA Ops:
  0.0 1.8 %pack.1 = (bf16[528,128]{1,0:T(8,128)(2,1)}, bf16[528,128]{1,0:T(8,128)(2,1)}) custom-call(f32[1024,128]{1,0:T(8,128)} %v.1, s32[2,4]{1,0:T(2,128)} %bitcast.16, s32[1,4]{1,0:T(1,128)} %bitcast.18), custom_call_target="tpu_custom_call" | custom-call | tf_op jit(solution)/shard_map/pack/pallas_call | solution.py:67
  1.8 4.5 %collective-permute-start = (bf16[528,128]{1,0:T(8,128)(2,1)}, bf16[528,128]{1,0:T(8,128)(2,1)S(1)}, u32[]{:S(2)}, u32[]{:S(2)}) collective-permute-start(bf16[528,128]{1,0:T(8,128)(2,1)} %get-tuple-element.11), channel_id=1, source_target_pairs={{0,8},{8,16},{16,24},{24,32},{32,40},{40,48},{48,56},{56,64},{64,7... | collective-permute-start | bytes 405512 | tf_op jit(solution)/shard_map/ppermute | solution.py:419
  6.3 5.6 %collective-permute-start.1 = (bf16[528,128]{1,0:T(8,128)(2,1)}, bf16[528,128]{1,0:T(8,128)(2,1)S(1)}, u32[]{:S(2)}, u32[]{:S(2)}) collective-permute-start(bf16[528,128]{1,0:T(8,128)(2,1)} %get-tuple-element.12), channel_id=1, source_target_pairs={{8,0},{16,8},{24,16},{32,24},{40,32},{48,40},{56,48},{64,56},{72,6... | collective-permute-start | bytes 405512 | tf_op jit(solution)/shard_map/ppermute | solution.py:420
  11.9 0.8 fusion.2
  12.7 0.1 copy.15
  12.8 0.1 copy.16
  12.9 0.0 copy-start
  13.0 1.6 %copy.14 = bf16[8,256,256]{1,2,0:T(8,128)(2,1)S(1)} copy(bf16[8,256,256]{2,1,0:T(8,128)(2,1)} %hop.1) | data formatting | bytes 2097152 | tf_op args[1]
  14.5 0.0 copy-done
  14.5 0.0 copy-start.3
  14.6 0.3 multiply_convert_fusion.sym
  14.9 0.0 copy-start.1
  14.9 0.0 copy-start.2
  16.2 0.0 copy-done.3
  16.3 0.0 collective-permute-done
  16.3 0.0 collective-permute-done.1
  16.3 0.0 copy-done.1
  16.3 0.0 copy-done.2
  16.3 2.4 %chebyshev.1 = (f32[1024,128]{1,0:T(8,128)S(1)}, bf16[1024,128]{1,0:T(8,128)(2,1)S(1)}) custom-call(s32[2,4]{1,0:T(2,128)S(1)} %bitcast.17, s32[1,4]{1,0:T(1,128)S(1)} %bitcast.19, f32[1]{0:T(128)S(6)} %copy.17.shift, f32[1]{0:T(128)} %copy.18.width, f32[1024,128]{1,0:T(8,128)S(1)} %broadcast_divide_fusion.base, ...), custom_call_target="tpu_custom_call" | custom-call | tf_op jit(solution)/shard_map/chebyshev/pallas_call | solution.py:164
  18.8 7.2 %collective-permute-start.2 = (bf16[1024,128]{1,0:T(8,128)(2,1)S(1)}, bf16[1024,128]{1,0:T(8,128)(2,1)S(1)}, u32[]{:S(2)}, u32[]{:S(2)}) collective-permute-start(bf16[1024,128]{1,0:T(8,128)(2,1)S(1)} %get-tuple-element.14), channel_id=1, source_target_pairs={{0,5},{1,4},{8,13},{9,12},{16,21},{17,20},{24,29},{25,28},{32,37},... | collective-permute-start | bytes 786440 | tf_op jit(solution)/shard_map/ppermute | solution.py:403
  26.0 4.5 %collective-permute-done.2 = bf16[1024,128]{1,0:T(8,128)(2,1)S(1)} collective-permute-done((bf16[1024,128]{1,0:T(8,128)(2,1)S(1)}, bf16[1024,128]{1,0:T(8,128)(2,1)S(1)}, u32[]{:S(2)}, u32[]{:S(2)}) %collective-permute-start.2) | collective-permute-done | bytes 262176 | tf_op jit(solution)/shard_map/ppermute | solution.py:403
  30.5 1.3 %collective-permute-start.3 = (bf16[1024,128]{1,0:T(8,128)(2,1)S(1)}, bf16[1024,128]{1,0:T(8,128)(2,1)S(1)}, u32[]{:S(2)}, u32[]{:S(2)}) collective-permute-start(bf16[1024,128]{1,0:T(8,128)(2,1)S(1)} %broadcast_select_fusion.own), channel_id=1, source_target_pairs={{0,7},{1,2},{5,6},{4,3},{8,15},{9,10},{13,14},{12,11},{16,23},{17,... | collective-permute-start | bytes 786440 | tf_op jit(solution)/shard_map/ppermute | solution.py:405
  31.8 2.2 %collective-permute-start.4 = (bf16[1024,128]{1,0:T(8,128)(2,1)S(1)}, bf16[1024,128]{1,0:T(8,128)(2,1)S(1)}, u32[]{:S(2)}, u32[]{:S(2)}) collective-permute-start(bf16[1024,128]{1,0:T(8,128)(2,1)S(1)} %broadcast_select_fusion.own), channel_id=1, source_target_pairs={{0,1},{1,0},{5,3},{4,6},{8,9},{9,8},{13,11},{12,14},{16,17},{17,16... | collective-permute-start | bytes 786440 | tf_op jit(solution)/shard_map/ppermute | solution.py:405
  34.0 1.3 %collective-permute-start.5 = (bf16[1024,128]{1,0:T(8,128)(2,1)S(1)}, bf16[1024,128]{1,0:T(8,128)(2,1)S(1)}, u32[]{:S(2)}, u32[]{:S(2)}) collective-permute-start(bf16[1024,128]{1,0:T(8,128)(2,1)S(1)} %broadcast_select_fusion.own), channel_id=1, source_target_pairs={{0,2},{1,7},{5,4},{4,5},{8,10},{9,15},{13,12},{12,13},{16,18},{17,... | collective-permute-start | bytes 786440 | tf_op jit(solution)/shard_map/ppermute | solution.py:405
  35.3 1.5 %collective-permute-done.3.first = bf16[1024,128]{1,0:T(8,128)(2,1)S(1)} collective-permute-done((bf16[1024,128]{1,0:T(8,128)(2,1)S(1)}, bf16[1024,128]{1,0:T(8,128)(2,1)S(1)}, u32[]{:S(2)}, u32[]{:S(2)}) %collective-permute-start.3) | collective-permute-done | bytes 262176 | tf_op jit(solution)/shard_map/ppermute | solution.py:405
  36.8 4.9 %collective-permute-done.4.second = bf16[1024,128]{1,0:T(8,128)(2,1)S(1)} collective-permute-done((bf16[1024,128]{1,0:T(8,128)(2,1)S(1)}, bf16[1024,128]{1,0:T(8,128)(2,1)S(1)}, u32[]{:S(2)}, u32[]{:S(2)}) %collective-permute-start.4) | collective-permute-done | bytes 262176 | tf_op jit(solution)/shard_map/ppermute | solution.py:405
  41.7 3.2 %collective-permute-done.5.third = bf16[1024,128]{1,0:T(8,128)(2,1)S(1)} collective-permute-done((bf16[1024,128]{1,0:T(8,128)(2,1)S(1)}, bf16[1024,128]{1,0:T(8,128)(2,1)S(1)}, u32[]{:S(2)}, u32[]{:S(2)}) %collective-permute-start.5) | collective-permute-done | bytes 262176 | tf_op jit(solution)/shard_map/ppermute | solution.py:405
  44.9 0.7 gram.1
  45.6 12.2 %all_to_all.23 = f32[8,32,128]{2,1,0:T(8,128)S(1)} all-to-all(f32[8,32,128]{2,1,0:T(8,128)S(1)} %bitcast.15), channel_id=1, replica_groups=mesh['y'=8,'x'=4,'core'=2,'panel'=8] {'x','core'}, dimensions={0} | all-to-all | bytes 262144 | tf_op jit(solution)/shard_map/all_to_all | solution.py:384
  57.8 15.1 %all_to_all.24 = f32[8,32,128]{2,1,0:T(8,128)S(1)} all-to-all(f32[8,32,128]{2,1,0:T(8,128)S(1)} %broadcast_in_dim.7), channel_id=1, replica_groups=mesh['y'=8,'x'=4,'core'=2,'panel'=8] {'y'}, dimensions={0} | all-to-all | bytes 262144 | tf_op jit(solution)/shard_map/all_to_all | solution.py:384
  73.0 10.0 %all_to_all.25 = f32[8,32,128]{2,1,0:T(8,128)S(1)} all-to-all(f32[8,32,128]{2,1,0:T(8,128)S(1)} %broadcast_in_dim.8), channel_id=1, replica_groups=mesh['y'=8,'x'=4,'core'=2,'panel'=8] {'x','core'}, dimensions={0} | all-to-all | bytes 262144 | tf_op jit(solution)/shard_map/all_to_all | solution.py:384
  83.0 13.7 %finish.1 = f32[1024,128]{1,0:T(8,128)} custom-call(s32[1]{0:T(128)} %bitcast.pos, f32[256,128]{1,0:T(8,128)S(1)} %bitcast.12, f32[1024,128]{1,0:T(8,128)S(1)} %get-tuple-element.13.w, bf16[1024,256]{1,0:T(8,128)(2,1)S(1)} %get-tuple-element.16.p01), custom_call_target="tpu_custom_call" | custom-call | tf_op jit(solution)/shard_map/finish/pallas_call | solution.py:372
  (10 shorter events, 0.2 us)
Async XLA Ops:
  1.8 14.5 %collective-permute-start = (bf16[528,128]{1,0:T(8,128)(2,1)}, bf16[528,128]{1,0:T(8,128)(2,1)S(1)}, u32[]{:S(2)}, u32[]{:S(2)}) collective-permute-start(bf16[528,128]{1,0:T(8,128)(2,1)} %get-tuple-element.11), channel_id=1, source_target_pairs={{0,8},{8,16},{16,24},{24,32},{32,40},{40,48},{48,56},{56,64},{64,7... | collective-permute-start | bytes 405512 | tf_op jit(solution)/shard_map/ppermute | solution.py:419
  6.3 10.0 %collective-permute-start.1 = (bf16[528,128]{1,0:T(8,128)(2,1)}, bf16[528,128]{1,0:T(8,128)(2,1)S(1)}, u32[]{:S(2)}, u32[]{:S(2)}) collective-permute-start(bf16[528,128]{1,0:T(8,128)(2,1)} %get-tuple-element.12), channel_id=1, source_target_pairs={{8,0},{16,8},{24,16},{32,24},{40,32},{48,40},{56,48},{64,56},{72,6... | collective-permute-start | bytes 405512 | tf_op jit(solution)/shard_map/ppermute | solution.py:420
  12.9 1.6 %copy-start = (bf16[8,256,256]{2,1,0:T(8,128)(2,1)S(1)}, bf16[8,256,256]{2,1,0:T(8,128)(2,1)}, u32[]{:S(2)}) copy-start(bf16[8,256,256]{2,1,0:T(8,128)(2,1)} %hop.1) | copy-start | bytes 3145732
  14.5 1.7 %copy-start.3 = (f32[1024,128]{1,0:T(8,128)S(1)}, f32[1024,128]{1,0:T(8,128)}, u32[]{:S(2)}) copy-start(f32[1024,128]{1,0:T(8,128)} %v.1) | copy-start | bytes 1572868
  14.9 1.4 %copy-start.1 = (s32[4,2]{0,1:T(2,128)S(1)}, s32[4,2]{0,1:T(2,128)}, u32[]{:S(2)}) copy-start(s32[4,2]{0,1:T(2,128)} %param.9) | copy-start | bytes 100
  14.9 1.4 %copy-start.2 = (s32[4]{0:T(128)S(1)}, s32[4]{0:T(128)}, u32[]{:S(2)}) copy-start(s32[4]{0:T(128)} %param.10) | copy-start | bytes 52
  18.8 11.7 %collective-permute-start.2 = (bf16[1024,128]{1,0:T(8,128)(2,1)S(1)}, bf16[1024,128]{1,0:T(8,128)(2,1)S(1)}, u32[]{:S(2)}, u32[]{:S(2)}) collective-permute-start(bf16[1024,128]{1,0:T(8,128)(2,1)S(1)} %get-tuple-element.14), channel_id=1, source_target_pairs={{0,5},{1,4},{8,13},{9,12},{16,21},{17,20},{24,29},{25,28},{32,37},... | collective-permute-start | bytes 786440 | tf_op jit(solution)/shard_map/ppermute | solution.py:403
  30.5 6.3 %collective-permute-start.3 = (bf16[1024,128]{1,0:T(8,128)(2,1)S(1)}, bf16[1024,128]{1,0:T(8,128)(2,1)S(1)}, u32[]{:S(2)}, u32[]{:S(2)}) collective-permute-start(bf16[1024,128]{1,0:T(8,128)(2,1)S(1)} %broadcast_select_fusion.own), channel_id=1, source_target_pairs={{0,7},{1,2},{5,6},{4,3},{8,15},{9,10},{13,14},{12,11},{16,23},{17,... | collective-permute-start | bytes 786440 | tf_op jit(solution)/shard_map/ppermute | solution.py:405
  31.8 9.9 %collective-permute-start.4 = (bf16[1024,128]{1,0:T(8,128)(2,1)S(1)}, bf16[1024,128]{1,0:T(8,128)(2,1)S(1)}, u32[]{:S(2)}, u32[]{:S(2)}) collective-permute-start(bf16[1024,128]{1,0:T(8,128)(2,1)S(1)} %broadcast_select_fusion.own), channel_id=1, source_target_pairs={{0,1},{1,0},{5,3},{4,6},{8,9},{9,8},{13,11},{12,14},{16,17},{17,16... | collective-permute-start | bytes 786440 | tf_op jit(solution)/shard_map/ppermute | solution.py:405
  34.0 10.9 %collective-permute-start.5 = (bf16[1024,128]{1,0:T(8,128)(2,1)S(1)}, bf16[1024,128]{1,0:T(8,128)(2,1)S(1)}, u32[]{:S(2)}, u32[]{:S(2)}) collective-permute-start(bf16[1024,128]{1,0:T(8,128)(2,1)S(1)} %broadcast_select_fusion.own), channel_id=1, source_target_pairs={{0,2},{1,7},{5,4},{4,5},{8,10},{9,15},{13,12},{12,13},{16,18},{17,... | collective-permute-start | bytes 786440 | tf_op jit(solution)/shard_map/ppermute | solution.py:405

commit v13 on v12

--- a/solution.py
+++ b/solution.py
@@ -18,10 +18,10 @@
 MISSING = 8
 STEPS = (
     [(0, 7), (1, 2), (5, 6), (4, 3)],
+    [(0, 2), (1, 7), (5, 4), (4, 5)],
     [(0, 1), (1, 0), (5, 3), (4, 6)],
-    [(0, 2), (1, 7), (5, 4), (4, 5)],
 )
-HELD = ((0, 2, 3, 2, 3, 0, 1, 1), (2, 0, 1, 1, 0, 3, 2, 3))
+HELD = ((0, 3, 2, 3, 2, 0, 1, 1), (3, 0, 1, 1, 0, 2, 3, 2))
 VM = pltpu.VMEM
 SM = pltpu.SMEM
 

time: 97.2 us -> 97.7 us (level)
  transfers between devices with their start and end apart: 6 -> 6, of which waited for: 4 -> 3; matrix products, arithmetic and copies ran while one was open for 3% -> 3% of each run, Pallas kernels for 0% -> 0%
where the time goes in v13:
time: 97.7 us; the launch traced here: 96.9 us
  blocking collectives  37.9 us (39%)
  starting transfers between devices  22.1 us (23%)
  Pallas kernels  18.6 us (19%)
  waiting for transfers between devices  13.6 us (14%)
  local copies, waits for them, and re-layouts  2.64 us (3%)
  between operations  1.54 us (2%)
    all_to_all x3, blocking collectives, swap(): return lax.all_to_all(x, axes, 0, 0, tiled=True)  37.9 us
    pallas_call x1, Pallas kernels, finish(): pl.pallas_call(finish_kernel, out_shape=jax.ShapeDtypeStruct(w.shape, F32...  13.7 us
    ppermute x3, waiting for transfers between devices, spread(): lax.ppermute(own, 'panel', pairs)  9.16 us
    ppermute x1, starting transfers between devices, spread(): far = lax.ppermute(w_hi, 'panel', [(0, 5), (1, 4)])  7.2 us
    ppermute x1, starting transfers between devices, body(): right = lax.ppermute(down, slab, [(i + 1, i) for i in range(count - 1)])  5.57 us
    ppermute x3, starting transfers between devices, spread(): lax.ppermute(own, 'panel', pairs)  4.79 us
    ppermute x1, starting transfers between devices, body(): left = lax.ppermute(up, slab, [(i, i + 1) for i in range(count - 1)])  4.5 us
    ppermute x1, waiting for transfers between devices, spread(): far = lax.ppermute(w_hi, 'panel', [(0, 5), (1, 4)])  4.46 us
  transfers between devices with their start and end apart: 6, of which 3 were waited for; matrix products, arithmetic and copies ran while one was open for 3% of the time, Pallas kernels for 0%

profile of v13, /device:TPU:1, one launch (start us, length us, event | category | flops | bytes accessed | tf_op | source)
XLA Modules:
  0.0 96.9 jit_solution(630064619738577848)
XLA Ops:
  0.0 1.8 %pack.1 = (bf16[528,128]{1,0:T(8,128)(2,1)}, bf16[528,128]{1,0:T(8,128)(2,1)}) custom-call(f32[1024,128]{1,0:T(8,128)} %v.1, s32[2,4]{1,0:T(2,128)} %bitcast.16, s32[1,4]{1,0:T(1,128)} %bitcast.18), custom_call_target="tpu_custom_call" | custom-call | tf_op jit(solution)/shard_map/pack/pallas_call | solution.py:67
  1.8 4.5 %collective-permute-start = (bf16[528,128]{1,0:T(8,128)(2,1)}, bf16[528,128]{1,0:T(8,128)(2,1)S(1)}, u32[]{:S(2)}, u32[]{:S(2)}) collective-permute-start(bf16[528,128]{1,0:T(8,128)(2,1)} %get-tuple-element.11), channel_id=1, source_target_pairs={{0,8},{8,16},{16,24},{24,32},{32,40},{40,48},{48,56},{56,64},{64,7... | collective-permute-start | bytes 405512 | tf_op jit(solution)/shard_map/ppermute | solution.py:419
  6.3 5.6 %collective-permute-start.1 = (bf16[528,128]{1,0:T(8,128)(2,1)}, bf16[528,128]{1,0:T(8,128)(2,1)S(1)}, u32[]{:S(2)}, u32[]{:S(2)}) collective-permute-start(bf16[528,128]{1,0:T(8,128)(2,1)} %get-tuple-element.12), channel_id=1, source_target_pairs={{8,0},{16,8},{24,16},{32,24},{40,32},{48,40},{56,48},{64,56},{72,6... | collective-permute-start | bytes 405512 | tf_op jit(solution)/shard_map/ppermute | solution.py:420
  11.9 0.8 fusion.2
  12.7 0.1 copy.15
  12.8 0.1 copy.16
  12.9 0.0 copy-start
  13.0 1.6 %copy.14 = bf16[8,256,256]{1,2,0:T(8,128)(2,1)S(1)} copy(bf16[8,256,256]{2,1,0:T(8,128)(2,1)} %hop.1) | data formatting | bytes 2097152 | tf_op args[1]
  14.5 0.0 copy-done
  14.5 0.0 copy-start.3
  14.6 0.3 multiply_convert_fusion.sym
  14.9 0.0 copy-start.1
  14.9 0.0 copy-start.2
  16.2 0.0 copy-done.3
  16.3 0.0 collective-permute-done
  16.3 0.0 collective-permute-done.1
  16.3 0.0 copy-done.1
  16.3 0.0 copy-done.2
  16.3 2.4 %chebyshev.1 = (f32[1024,128]{1,0:T(8,128)S(1)}, bf16[1024,128]{1,0:T(8,128)(2,1)S(1)}) custom-call(s32[2,4]{1,0:T(2,128)S(1)} %bitcast.17, s32[1,4]{1,0:T(1,128)S(1)} %bitcast.19, f32[1]{0:T(128)S(6)} %copy.17.shift, f32[1]{0:T(128)} %copy.18.width, f32[1024,128]{1,0:T(8,128)S(1)} %broadcast_divide_fusion.base, ...), custom_call_target="tpu_custom_call" | custom-call | tf_op jit(solution)/shard_map/chebyshev/pallas_call | solution.py:164
  18.8 7.2 %collective-permute-start.2 = (bf16[1024,128]{1,0:T(8,128)(2,1)S(1)}, bf16[1024,128]{1,0:T(8,128)(2,1)S(1)}, u32[]{:S(2)}, u32[]{:S(2)}) collective-permute-start(bf16[1024,128]{1,0:T(8,128)(2,1)S(1)} %get-tuple-element.14), channel_id=1, source_target_pairs={{0,5},{1,4},{8,13},{9,12},{16,21},{17,20},{24,29},{25,28},{32,37},... | collective-permute-start | bytes 786440 | tf_op jit(solution)/shard_map/ppermute | solution.py:403
  26.0 4.5 %collective-permute-done.2 = bf16[1024,128]{1,0:T(8,128)(2,1)S(1)} collective-permute-done((bf16[1024,128]{1,0:T(8,128)(2,1)S(1)}, bf16[1024,128]{1,0:T(8,128)(2,1)S(1)}, u32[]{:S(2)}, u32[]{:S(2)}) %collective-permute-start.2) | collective-permute-done | bytes 262176 | tf_op jit(solution)/shard_map/ppermute | solution.py:403
  30.5 1.3 %collective-permute-start.3 = (bf16[1024,128]{1,0:T(8,128)(2,1)S(1)}, bf16[1024,128]{1,0:T(8,128)(2,1)S(1)}, u32[]{:S(2)}, u32[]{:S(2)}) collective-permute-start(bf16[1024,128]{1,0:T(8,128)(2,1)S(1)} %broadcast_select_fusion.own), channel_id=1, source_target_pairs={{0,7},{1,2},{5,6},{4,3},{8,15},{9,10},{13,14},{12,11},{16,23},{17,... | collective-permute-start | bytes 786440 | tf_op jit(solution)/shard_map/ppermute | solution.py:405
  31.8 1.3 %collective-permute-start.4 = (bf16[1024,128]{1,0:T(8,128)(2,1)S(1)}, bf16[1024,128]{1,0:T(8,128)(2,1)S(1)}, u32[]{:S(2)}, u32[]{:S(2)}) collective-permute-start(bf16[1024,128]{1,0:T(8,128)(2,1)S(1)} %broadcast_select_fusion.own), channel_id=1, source_target_pairs={{0,2},{1,7},{5,4},{4,5},{8,10},{9,15},{13,12},{12,13},{16,18},{17,... | collective-permute-start | bytes 786440 | tf_op jit(solution)/shard_map/ppermute | solution.py:405
  33.1 2.2 %collective-permute-start.5 = (bf16[1024,128]{1,0:T(8,128)(2,1)S(1)}, bf16[1024,128]{1,0:T(8,128)(2,1)S(1)}, u32[]{:S(2)}, u32[]{:S(2)}) collective-permute-start(bf16[1024,128]{1,0:T(8,128)(2,1)S(1)} %broadcast_select_fusion.own), channel_id=1, source_target_pairs={{0,1},{1,0},{5,3},{4,6},{8,9},{9,8},{13,11},{12,14},{16,17},{17,16... | collective-permute-start | bytes 786440 | tf_op jit(solution)/shard_map/ppermute | solution.py:405
  35.3 7.1 %collective-permute-done.3.first = bf16[1024,128]{1,0:T(8,128)(2,1)S(1)} collective-permute-done((bf16[1024,128]{1,0:T(8,128)(2,1)S(1)}, bf16[1024,128]{1,0:T(8,128)(2,1)S(1)}, u32[]{:S(2)}, u32[]{:S(2)}) %collective-permute-start.3) | collective-permute-done | bytes 262176 | tf_op jit(solution)/shard_map/ppermute | solution.py:405
  42.4 0.0 collective-permute-done.4.second
  42.4 2.1 %collective-permute-done.5.third = bf16[1024,128]{1,0:T(8,128)(2,1)S(1)} collective-permute-done((bf16[1024,128]{1,0:T(8,128)(2,1)S(1)}, bf16[1024,128]{1,0:T(8,128)(2,1)S(1)}, u32[]{:S(2)}, u32[]{:S(2)}) %collective-permute-start.5) | collective-permute-done | bytes 262176 | tf_op jit(solution)/shard_map/ppermute | solution.py:405
  44.4 0.7 gram.1
  45.2 12.2 %all_to_all.23 = f32[8,32,128]{2,1,0:T(8,128)S(1)} all-to-all(f32[8,32,128]{2,1,0:T(8,128)S(1)} %bitcast.15), channel_id=1, replica_groups=mesh['y'=8,'x'=4,'core'=2,'panel'=8] {'x','core'}, dimensions={0} | all-to-all | bytes 262144 | tf_op jit(solution)/shard_map/all_to_all | solution.py:384
  57.4 15.7 %all_to_all.24 = f32[8,32,128]{2,1,0:T(8,128)S(1)} all-to-all(f32[8,32,128]{2,1,0:T(8,128)S(1)} %broadcast_in_dim.7), channel_id=1, replica_groups=mesh['y'=8,'x'=4,'core'=2,'panel'=8] {'y'}, dimensions={0} | all-to-all | bytes 262144 | tf_op jit(solution)/shard_map/all_to_all | solution.py:384
  73.1 10.0 %all_to_all.25 = f32[8,32,128]{2,1,0:T(8,128)S(1)} all-to-all(f32[8,32,128]{2,1,0:T(8,128)S(1)} %broadcast_in_dim.8), channel_id=1, replica_groups=mesh['y'=8,'x'=4,'core'=2,'panel'=8] {'x','core'}, dimensions={0} | all-to-all | bytes 262144 | tf_op jit(solution)/shard_map/all_to_all | solution.py:384
  83.2 13.7 %finish.1 = f32[1024,128]{1,0:T(8,128)} custom-call(s32[1]{0:T(128)} %bitcast.pos, f32[256,128]{1,0:T(8,128)S(1)} %bitcast.12, f32[1024,128]{1,0:T(8,128)S(1)} %get-tuple-element.13.w, bf16[1024,256]{1,0:T(8,128)(2,1)S(1)} %get-tuple-element.16.p01), custom_call_target="tpu_custom_call" | custom-call | tf_op jit(solution)/shard_map/finish/pallas_call | solution.py:372
  (10 shorter events, 0.2 us)
Async XLA Ops:
  1.8 14.5 %collective-permute-start = (bf16[528,128]{1,0:T(8,128)(2,1)}, bf16[528,128]{1,0:T(8,128)(2,1)S(1)}, u32[]{:S(2)}, u32[]{:S(2)}) collective-permute-start(bf16[528,128]{1,0:T(8,128)(2,1)} %get-tuple-element.11), channel_id=1, source_target_pairs={{0,8},{8,16},{16,24},{24,32},{32,40},{40,48},{48,56},{56,64},{64,7... | collective-permute-start | bytes 405512 | tf_op jit(solution)/shard_map/ppermute | solution.py:419
  6.3 10.0 %collective-permute-start.1 = (bf16[528,128]{1,0:T(8,128)(2,1)}, bf16[528,128]{1,0:T(8,128)(2,1)S(1)}, u32[]{:S(2)}, u32[]{:S(2)}) collective-permute-start(bf16[528,128]{1,0:T(8,128)(2,1)} %get-tuple-element.12), channel_id=1, source_target_pairs={{8,0},{16,8},{24,16},{32,24},{40,32},{48,40},{56,48},{64,56},{72,6... | collective-permute-start | bytes 405512 | tf_op jit(solution)/shard_map/ppermute | solution.py:420
  12.9 1.6 %copy-start = (bf16[8,256,256]{2,1,0:T(8,128)(2,1)S(1)}, bf16[8,256,256]{2,1,0:T(8,128)(2,1)}, u32[]{:S(2)}) copy-start(bf16[8,256,256]{2,1,0:T(8,128)(2,1)} %hop.1) | copy-start | bytes 3145732
  14.5 1.7 %copy-start.3 = (f32[1024,128]{1,0:T(8,128)S(1)}, f32[1024,128]{1,0:T(8,128)}, u32[]{:S(2)}) copy-start(f32[1024,128]{1,0:T(8,128)} %v.1) | copy-start | bytes 1572868
  14.9 1.4 %copy-start.1 = (s32[4,2]{0,1:T(2,128)S(1)}, s32[4,2]{0,1:T(2,128)}, u32[]{:S(2)}) copy-start(s32[4,2]{0,1:T(2,128)} %param.9) | copy-start | bytes 100
  14.9 1.4 %copy-start.2 = (s32[4]{0:T(128)S(1)}, s32[4]{0:T(128)}, u32[]{:S(2)}) copy-start(s32[4]{0:T(128)} %param.10) | copy-start | bytes 52
  18.8 11.7 %collective-permute-start.2 = (bf16[1024,128]{1,0:T(8,128)(2,1)S(1)}, bf16[1024,128]{1,0:T(8,128)(2,1)S(1)}, u32[]{:S(2)}, u32[]{:S(2)}) collective-permute-start(bf16[1024,128]{1,0:T(8,128)(2,1)S(1)} %get-tuple-element.14), channel_id=1, source_target_pairs={{0,5},{1,4},{8,13},{9,12},{16,21},{17,20},{24,29},{25,28},{32,37},... | collective-permute-start | bytes 786440 | tf_op jit(solution)/shard_map/ppermute | solution.py:403
  30.5 11.9 %collective-permute-start.3 = (bf16[1024,128]{1,0:T(8,128)(2,1)S(1)}, bf16[1024,128]{1,0:T(8,128)(2,1)S(1)}, u32[]{:S(2)}, u32[]{:S(2)}) collective-permute-start(bf16[1024,128]{1,0:T(8,128)(2,1)S(1)} %broadcast_select_fusion.own), channel_id=1, source_target_pairs={{0,7},{1,2},{5,6},{4,3},{8,15},{9,10},{13,14},{12,11},{16,23},{17,... | collective-permute-start | bytes 786440 | tf_op jit(solution)/shard_map/ppermute | solution.py:405
  31.8 10.6 %collective-permute-start.4 = (bf16[1024,128]{1,0:T(8,128)(2,1)S(1)}, bf16[1024,128]{1,0:T(8,128)(2,1)S(1)}, u32[]{:S(2)}, u32[]{:S(2)}) collective-permute-start(bf16[1024,128]{1,0:T(8,128)(2,1)S(1)} %broadcast_select_fusion.own), channel_id=1, source_target_pairs={{0,2},{1,7},{5,4},{4,5},{8,10},{9,15},{13,12},{12,13},{16,18},{17,... | collective-permute-start | bytes 786440 | tf_op jit(solution)/shard_map/ppermute | solution.py:405
  33.1 11.3 %collective-permute-start.5 = (bf16[1024,128]{1,0:T(8,128)(2,1)S(1)}, bf16[1024,128]{1,0:T(8,128)(2,1)S(1)}, u32[]{:S(2)}, u32[]{:S(2)}) collective-permute-start(bf16[1024,128]{1,0:T(8,128)(2,1)S(1)} %broadcast_select_fusion.own), channel_id=1, source_target_pairs={{0,1},{1,0},{5,3},{4,6},{8,9},{9,8},{13,11},{12,14},{16,17},{17,16... | collective-permute-start | bytes 786440 | tf_op jit(solution)/shard_map/ppermute | solution.py:405
